TPU v7x, 32 devices: a whole 2x2x4 slice. The times are simulated.
32 devices in a mesh: tile: 8 (over z, y), col: 4 (over x, core).
Axes of the slice: x: 2, y: 2, z: 4, core: 2. Of those that a mesh axis runs over, the one named last changes fastest.
Arguments:
- positions: float32 [3, 4096], P(None, 'tile'), may hold values from 0 to 640, as said below
- trial_block: float32 [3, 16, 4096], P(None, None, 'tile')
- pair_tiles: int32 [2, 8, 4, 8], P(None, 'tile'), may hold values from 0 to 31, as said below
- pair_count: int32 [8, 4], P('tile'), may hold values from 0 to 8, as said below
Outputs:
- next_block: float32 [3, 16, 4096], P(None, None, 'tile')
- rayleigh: float32 [16, 16], replicated
- correlation_norm: float32 [16, 16], replicated
- residual_norms: float32 [16], replicated
Inputs may be any that keep to these rules, and one draw needn't show every extreme that they name: `positions`: tiles follow one another along the first component, in order of their numbers. `pair_tiles`: entry 1 lies between the row tile and two tiles past it, never below it, within the tiles of the same index along tile or of the next one. Each unordered pair of tiles is listed at most once among live slots; every pair of beads closer than 15 is covered by a live slot. Slots at or past the count hold valid numbers too. `pair_count`: for every index along tile but the last, one of its 4 devices along col has all 8 slots live.
All inputs are finite; a program needn't handle non-finite values.
Results may differ from a plain program's by a relative error of at most 0.0003.
Values sent between devices are 32-bit elements; how exact they have to be, the bound alone decides.
No kernel may reach another device: no remote copies, remote signals or barrier semaphores. Data moves between devices by JAX's collectives and lax.ppermute only.
A program may use at most 64 MiB of HBM per device.

v0:
```python
import functools

import jax
import jax.numpy as jnp
from jax import lax
from jax.experimental import pallas as pl
from jax.experimental.pallas import tpu as pltpu
from jax.sharding import PartitionSpec as P

TILE_B = 128
REACH = 2
CHUNK = 32

spring_scale = 1.0 / 64.0
cutoff_sq = 225.0
step_size = 0.2
highest = lax.Precision.HIGHEST
f32 = jnp.float32
bf16 = jnp.bfloat16
COMPONENT_PAIRS = ((0, 0), (0, 1), (0, 2), (1, 1), (1, 2), (2, 2))


def parity():
    return lax.rem(lax.axis_index("col"), 2)


def lanes(start, size):
    return pl.ds(pl.multiple_of(start, TILE_B), size)


def pack_kernel(vec_ref, pos_ref, tiles_ref, count_ref, out_ref):
    rows, width = vec_ref.shape
    out_ref[0:rows, :] = vec_ref[...]
    first_tile = lax.axis_index("tile") * (width // TILE_B)
    tile_of = lax.broadcasted_iota(jnp.int32, (8, width), 1) // TILE_B
    reach_of = lax.broadcasted_iota(jnp.int32, (8, width), 0) - 4
    live = jnp.zeros((8, width), f32)
    for c in range(tiles_ref.shape[2]):
        for s in range(tiles_ref.shape[3]):
            row = tiles_ref[0, 0, c, s]
            reach = tiles_ref[1, 0, c, s] - first_tile - row
            row = jnp.where(s < count_ref[0, c], row, -1)
            live += jnp.where((tile_of == row) & (reach_of == reach), 1.0, 0.0)
    out_ref[rows : rows + 8, :] = live * (spring_scale * step_size)
    out_ref[rows : rows + 3, :] = pos_ref[...]


def split(x):
    high = x.astype(bf16)
    return high, (x - high.astype(f32)).astype(bf16)


def store_vectors(lhs, x, base):
    rows, width = x.shape
    high, low = split(x)
    lhs[0:rows, lanes(base, width)] = high
    lhs[rows + 16 : 2 * rows + 16, lanes(base, width)] = low


def store_places(pos, pos_t, block, base):
    width = block.shape[1]
    pos[:, lanes(base, width)] = block
    pos_t[lanes(base, width), :] = jnp.transpose(block)


def fill_springs(pos, pos_t, spring_high, spring_low, row_tiles):
    for j in range(row_tiles[0] - REACH, row_tiles[-1] + REACH + 1):
        near = [w for w in row_tiles if abs(w - j) <= REACH]

        def one_chunk(q, carry):
            start = pl.multiple_of(q * CHUNK, CHUNK)
            col = pos_t[pl.ds(j * TILE_B + start, CHUNK), :]
            down = [jnp.broadcast_to(col[:, c : c + 1], (CHUNK, TILE_B)) for c in range(3)]
            for w in near:
                first, reach = min(j, w), abs(w - j)
                live = pos[4 + reach : 5 + reach, first * TILE_B : (first + 1) * TILE_B]
                offset = [down[c] - pos[c : c + 1, w * TILE_B : (w + 1) * TILE_B] for c in range(3)]
                dist_sq = offset[0] * offset[0] + offset[1] * offset[1] + offset[2] * offset[2]
                falloff = jnp.maximum(1.0 - dist_sq * (1.0 / cutoff_sq), 0.0)
                weight = falloff * falloff * live / jnp.maximum(dist_sq, 1.0)
                pulled = [weight * offset[c] for c in range(3)]
                place = pl.ds((j - w + REACH) * TILE_B + start, CHUNK)
                for n, (c, d) in enumerate(COMPONENT_PAIRS):
                    high, low = split(pulled[c] * offset[d])
                    r = row_tiles.index(w)
                    spring_high[r, place, n * TILE_B : (n + 1) * TILE_B] = high
                    spring_low[r, place, n * TILE_B : (n + 1) * TILE_B] = low
            return carry

        lax.fori_loop(0, TILE_B // CHUNK, one_chunk, 0)


def apply_springs(lhs, spring_high, spring_low, r, w, vec, cols):
    rows = 3 * cols
    near = slice((w - REACH) * TILE_B, (w + REACH + 1) * TILE_B)
    with_high = jnp.dot(lhs[:, near], spring_high[r], preferred_element_type=f32)
    with_low = jnp.dot(lhs[0 : rows + 16, near], spring_low[r], preferred_element_type=f32)
    total = with_high[0 : rows + 16] + with_low
    diag = total[rows : rows + 1]
    total = total[0:rows] + with_high[rows + 16 :]
    out = [None] * 3
    for n, (c, d) in enumerate(COMPONENT_PAIRS):
        part = slice(n * TILE_B, (n + 1) * TILE_B)
        for a, b in dict.fromkeys(((c, d), (d, c))):
            term = diag[:, part] * vec[b] - total[b * cols : (b + 1) * cols, part]
            out[a] = term if out[a] is None else out[a] + term
    return out


def first_kernel(own_ref, got_ref, out_ref, lhs, pos, pos_t, spring_high, spring_low):
    rows, width = out_ref.shape
    cols = rows // 3
    tiles = width // TILE_B
    odd = parity()
    lhs[rows : rows + 16, :] = jnp.ones((16, lhs.shape[1]), bf16)
    for ref, slot in ((own_ref, 1 - odd), (got_ref, odd)):
        store_vectors(lhs, ref[0:rows, :], slot * width)
        store_places(pos, pos_t, ref[rows : rows + 8, :], slot * width)
    row_tiles = list(range(REACH, REACH + tiles))
    fill_springs(pos, pos_t, spring_high, spring_low, row_tiles)
    for r, w in enumerate(row_tiles):
        part = slice(w * TILE_B, (w + 1) * TILE_B)
        vec = [
            lhs[d * cols : (d + 1) * cols, part].astype(f32)
            + lhs[rows + 16 + d * cols : rows + 16 + (d + 1) * cols, part].astype(f32)
            for d in range(3)
        ]
        out = apply_springs(lhs, spring_high, spring_low, r, w, vec, cols)
        for c in range(3):
            out_ref[c * cols : (c + 1) * cols, r * TILE_B : (r + 1) * TILE_B] = out[c]


def second_kernel(
    own_ref, got_ref, prod_ref, prod_got_ref, out_ref, gram_ref, lhs, pos, pos_t, spring_high, spring_low
):
    rows, width = prod_ref.shape
    cols = rows // 3
    half = width // 2
    odd = parity()
    lhs[rows : rows + 16, :] = jnp.ones((16, lhs.shape[1]), bf16)
    store_places(pos, pos_t, own_ref[rows : rows + 8, :], (1 - odd) * half)
    store_places(pos, pos_t, got_ref[rows : rows + 8, lanes((1 - odd) * half, half)], odd * width)
    store_vectors(lhs, prod_ref[...], odd * half)
    store_vectors(lhs, prod_got_ref[:, lanes(odd * half, half)], (1 - odd) * width)
    row_tiles = [REACH, REACH + 1]
    fill_springs(pos, pos_t, spring_high, spring_low, row_tiles)
    for r, w in enumerate(row_tiles):
        here = lanes((1 - odd) * half + r * TILE_B, TILE_B)
        vec = [prod_ref[d * cols : (d + 1) * cols, here] for d in range(3)]
        out = apply_springs(lhs, spring_high, spring_low, r, w, vec, cols)
        for c in range(3):
            out_ref[c * cols : (c + 1) * cols, r * TILE_B : (r + 1) * TILE_B] = out[c]
    gram = jnp.zeros((rows, rows), f32)
    for d in range(3):
        band = slice(d * cols, (d + 1) * cols)
        joint = jnp.concatenate(
            [own_ref[band, lanes(odd * half, half)], prod_ref[band, lanes((1 - odd) * half, half)], out_ref[band, :]],
            axis=0,
        )
        gram += lax.dot_general(joint, joint, (((1,), (1,)), ((), ())), precision=highest, preferred_element_type=f32)
    block = [[gram[a * cols : (a + 1) * cols, b * cols : (b + 1) * cols] for b in range(3)] for a in range(3)]
    gram_ref[...] = jnp.zeros(gram_ref.shape, f32)
    for n, part in enumerate((block[0][0], block[0][1], block[1][1], block[1][2], block[2][2])):
        gram_ref[:, n * cols : (n + 1) * cols] = part


def solve(matrix, rhs):
    n = matrix.shape[0]
    joint = jnp.concatenate([matrix, rhs], axis=1)
    row_of = lax.broadcasted_iota(jnp.int32, joint.shape, 0)
    for k in range(n):
        row = joint[k : k + 1, :] / joint[k : k + 1, k : k + 1]
        joint = jnp.where(row_of == k, row, joint - joint[:, k : k + 1] * row)
    return joint[:, n:]


def mul(a, b):
    return jnp.dot(a, b, precision=highest, preferred_element_type=f32)


def mul_t(a, b):
    return lax.dot_general(a, b, (((0,), (0,)), ((), ())), precision=highest, preferred_element_type=f32)


def last_kernel(
    bead_scale, own_ref, prod_ref, prod_got_ref, quad_ref, quad_got_ref, gram_ref, out_ref, ray_ref, corr_ref, norm_ref
):
    rows, width = prod_ref.shape
    cols = rows // 3
    half = width // 2
    odd = parity()
    xx, xp, pp, pq, qq = [gram_ref[:, n * cols : (n + 1) * cols] for n in range(5)]
    row_of = lax.broadcasted_iota(jnp.int32, (cols, cols), 0)
    col_of = lax.broadcasted_iota(jnp.int32, (cols, cols), 1)
    eye = jnp.where(row_of == col_of, 1.0, 0.0).astype(f32)
    shift = solve(xx, xp)
    turn = eye + shift
    first = mul_t(turn, xp)
    corr = mul_t(turn, mul(xx, turn) - xp) - mul_t(xp, turn) + pp
    gram = mul(first, turn) - mul_t(turn, pp) - mul(pp, turn) + pq
    squares = jnp.sum(eye * (mul_t(turn, mul(pp, turn) - 2.0 * pq) + qq), axis=0, keepdims=True)
    second = solve(corr, gram)
    squares = squares - jnp.sum(gram * second, axis=0, keepdims=True)
    ray_ref[...] = gram * (bead_scale / step_size)
    corr_ref[...] = corr * bead_scale
    norm_ref[...] = squares * (bead_scale / step_size**2)
    both = shift + second
    with_vec = both + mul(shift, second)
    for side in range(2):
        here = slice(side * half, (side + 1) * half)
        away = slice((1 - side) * half, (2 - side) * half)
        mine = odd == side
        for d in range(3):
            band = slice(d * cols, (d + 1) * cols)
            vec = own_ref[band, here]
            prod = jnp.where(mine, prod_ref[band, away], prod_got_ref[band, away])
            quad = jnp.where(mine, quad_ref[band, :], quad_got_ref[band, :])
            out_ref[band, here] = vec + mul_t(with_vec, vec) - 2.0 * prod - mul_t(both, prod) + quad


def per_device(positions, trial_block, pair_tiles, pair_count):
    comps, cols, width = trial_block.shape
    rows = comps * cols
    n_tile, n_col = lax.axis_size("tile"), lax.axis_size("col")
    tiles = width // TILE_B
    half = width // 2
    assert tiles == 2 * REACH and n_col % 2 == 0
    bead_scale = 1.0 / (3.0 * n_tile * width)
    vmem = pl.BlockSpec(memory_space=pltpu.VMEM)
    smem = pl.BlockSpec(memory_space=pltpu.SMEM)
    params = pltpu.CompilerParams(vmem_limit_bytes=40 * 2**20)

    own = pl.pallas_call(
        pack_kernel,
        out_shape=jax.ShapeDtypeStruct((rows + 8, width), f32),
        in_specs=[vmem, vmem, smem, smem],
        out_specs=vmem,
        name="pack",
    )(trial_block.reshape(rows, width), positions, pair_tiles, pair_count)

    halo = []
    for t in range(n_tile):
        for c in range(n_col):
            source = t - 1 if c % 2 == 0 else t + 1
            if 0 <= source < n_tile:
                halo.append((source * n_col + c, t * n_col + c))
    got = lax.ppermute(own, ("tile", "col"), halo)

    def swapped(x):
        return lax.ppermute(x, "col", [(c, c ^ 1) for c in range(n_col)])

    def scratch(window, count):
        deep = (2 * REACH + 1) * TILE_B
        across = len(COMPONENT_PAIRS) * TILE_B
        return [
            pltpu.VMEM((2 * rows + 16, window), bf16),
            pltpu.VMEM((8, window), f32),
            pltpu.VMEM((window, 8), f32),
            pltpu.VMEM((count, deep, across), bf16),
            pltpu.VMEM((count, deep, across), bf16),
        ]

    prod = pl.pallas_call(
        first_kernel,
        out_shape=jax.ShapeDtypeStruct((rows, width), f32),
        in_specs=[vmem] * 2,
        out_specs=vmem,
        scratch_shapes=scratch(2 * width, tiles),
        compiler_params=params,
        name="first",
    )(own, got)
    prod_got = swapped(prod)
    quad, gram = pl.pallas_call(
        second_kernel,
        out_shape=(jax.ShapeDtypeStruct((rows, half), f32), jax.ShapeDtypeStruct((cols, 128), f32)),
        in_specs=[vmem] * 4,
        out_specs=(vmem, vmem),
        scratch_shapes=scratch(width + half, REACH),
        compiler_params=params,
        name="second",
    )(own, got, prod, prod_got)
    gram = gram + swapped(gram)
    quad_got = swapped(quad)
    step = 1
    while step < n_tile:
        gram = gram + lax.ppermute(gram, "tile", [(t, t ^ step) for t in range(n_tile)])
        step *= 2
    block, ray, corr, norms = pl.pallas_call(
        functools.partial(last_kernel, bead_scale),
        out_shape=(
            jax.ShapeDtypeStruct((rows, width), f32),
            jax.ShapeDtypeStruct((cols, cols), f32),
            jax.ShapeDtypeStruct((cols, cols), f32),
            jax.ShapeDtypeStruct((1, cols), f32),
        ),
        in_specs=[vmem] * 6,
        out_specs=(vmem,) * 4,
        compiler_params=params,
        name="last",
    )(own, prod, prod_got, quad, quad_got, gram)
    return block.reshape(comps, cols, width), ray, corr, norms.reshape(cols)


def solution(mesh):
    return jax.shard_map(
        per_device,
        mesh=mesh,
        in_specs=(
            P(None, "tile"),
            P(None, None, "tile"),
            P(None, "tile", None, None),
            P("tile", None),
        ),
        out_specs=(P(None, None, "tile"), P(), P(), P()),
        check_vma=False,
    )
```

profile of v0, /device:TPU:0, one launch (start us, length us, event | category | flops | bytes accessed | tf_op | source)
XLA Modules:
  0.0 42.3 jit_solution(4149909425378688993)
XLA Ops:
  0.6 1.6 %pack.1.own_ref = f32[56,512]{1,0:T(8,128)} custom-call(f32[48,512]{1,0:T(8,128)} %bitcast.3, f32[3,512]{1,0:T(4,128)} %pos_ref.1, s32[2,1,4,8]{3,2,1,0:T(4,128)} %tiles_ref.1, s32[1,4]{1,0:T(1,128)} %count_ref.1), custom_call_target="tpu_custom_call" | custom-call | tf_op jit(solution)/shard_map/pack/pallas_call | solution.py:233
  2.3 4.9 %collective-permute-start = (f32[56,512]{1,0:T(8,128)}, f32[56,512]{1,0:T(8,128)S(1)}, u32[]{:S(2)}, u32[]{:S(2)}) collective-permute-start(f32[56,512]{1,0:T(8,128)} %pack.1.own_ref), channel_id=1, source_target_pairs={{5,1},{7,3},{0,4},{9,5},{2,6},{11,7},{4,8},{13,9},{6,10},{15,11},{... | collective-permute-start | bytes 344072 | tf_op jit(solution)/shard_map/ppermute | solution.py:247
  7.2 3.6 %collective-permute-done.got_ref = f32[56,512]{1,0:T(8,128)S(1)} collective-permute-done((f32[56,512]{1,0:T(8,128)}, f32[56,512]{1,0:T(8,128)S(1)}, u32[]{:S(2)}, u32[]{:S(2)}) %collective-permute-start) | collective-permute-done | bytes 114720 | tf_op jit(solution)/shard_map/ppermute | solution.py:247
  10.7 0.0 copy-start
  10.7 0.9 %copy-done = f32[56,512]{1,0:T(8,128)S(1)} copy-done((f32[56,512]{1,0:T(8,128)S(1)}, f32[56,512]{1,0:T(8,128)}, u32[]{:S(2)}) %copy-start) | copy-done | bytes 114712
  11.6 6.6 %first.1.prod_ref = f32[48,512]{1,0:T(8,128)S(1)} custom-call(f32[56,512]{1,0:T(8,128)S(1)} %copy-done, f32[56,512]{1,0:T(8,128)S(1)} %collective-permute-done.got_ref), custom_call_target="tpu_custom_call" | custom-call | tf_op jit(solution)/shard_map/first/pallas_call | solution.py:263
  18.2 0.1 collective-permute-start.1
  18.3 1.3 %collective-permute-done.1.prod_got_ref = f32[48,512]{1,0:T(8,128)S(1)} collective-permute-done((f32[48,512]{1,0:T(8,128)S(1)}, f32[48,512]{1,0:T(8,128)S(1)}, u32[]{:S(2)}, u32[]{:S(2)}) %collective-permute-start.1) | collective-permute-done | bytes 98336 | tf_op jit(solution)/shard_map/ppermute | solution.py:250
  19.6 0.0 copy-start.1
  19.6 4.6 %second.1 = (f32[48,256]{1,0:T(8,128)S(1)}, f32[16,128]{1,0:T(8,128)S(1)}) custom-call(f32[56,512]{1,0:T(8,128)S(1)} %copy-done, f32[56,512]{1,0:T(8,128)S(1)} %collective-permute-done.got_ref, f32[48,512]{1,0:T(8,128)S(1)} %first.1.prod_ref, f32[48,512]{1,0:T(8,128)S(1)} %collective-permute-done.1.prod_got_ref), custom_call_target="tpu_custom_call" | custom-call | tf_op jit(solution)/shard_map/second/pallas_call | solution.py:273
  24.2 0.2 collective-permute-start.2
  24.3 0.4 collective-permute-start.3
  24.7 0.8 %collective-permute-done.3 = f32[16,128]{1,0:T(8,128)S(1)} collective-permute-done((f32[16,128]{1,0:T(8,128)S(1)}, f32[16,128]{1,0:T(8,128)S(1)}, u32[]{:S(2)}, u32[]{:S(2)}) %collective-permute-start.3) | collective-permute-done | bytes 8224 | tf_op jit(solution)/shard_map/ppermute | solution.py:250
  25.5 2.4 %collective-permute-start.4 = (f32[16,128]{1,0:T(8,128)S(1)}, f32[16,128]{1,0:T(8,128)S(1)}, u32[]{:S(2)}, u32[]{:S(2)}) collective-permute-start(f32[16,128]{1,0:T(8,128)S(1)} %add.12), channel_id=1, source_target_pairs={{0,4},{4,0},{8,12},{12,8},{16,20},{20,16},{24,28},{28,24},{1,5},{5... | collective-permute-start | bytes 24584 | tf_op jit(solution)/shard_map/ppermute | solution.py:286
  27.9 1.6 %collective-permute-done.4 = f32[16,128]{1,0:T(8,128)S(1)} collective-permute-done((f32[16,128]{1,0:T(8,128)S(1)}, f32[16,128]{1,0:T(8,128)S(1)}, u32[]{:S(2)}, u32[]{:S(2)}) %collective-permute-start.4) | collective-permute-done | bytes 8224 | tf_op jit(solution)/shard_map/ppermute | solution.py:286
  29.5 2.0 %collective-permute-start.5 = (f32[16,128]{1,0:T(8,128)S(1)}, f32[16,128]{1,0:T(8,128)S(1)}, u32[]{:S(2)}, u32[]{:S(2)}) collective-permute-start(f32[16,128]{1,0:T(8,128)S(1)} %add.13), channel_id=1, source_target_pairs={{0,8},{4,12},{8,0},{12,4},{16,24},{20,28},{24,16},{28,20},{1,9},{5... | collective-permute-start | bytes 24584 | tf_op jit(solution)/shard_map/ppermute | solution.py:286
  31.5 1.7 %collective-permute-done.5 = f32[16,128]{1,0:T(8,128)S(1)} collective-permute-done((f32[16,128]{1,0:T(8,128)S(1)}, f32[16,128]{1,0:T(8,128)S(1)}, u32[]{:S(2)}, u32[]{:S(2)}) %collective-permute-start.5) | collective-permute-done | bytes 8224 | tf_op jit(solution)/shard_map/ppermute | solution.py:286
  33.2 3.0 %collective-permute-start.6 = (f32[16,128]{1,0:T(8,128)S(1)}, f32[16,128]{1,0:T(8,128)S(1)}, u32[]{:S(2)}, u32[]{:S(2)}) collective-permute-start(f32[16,128]{1,0:T(8,128)S(1)} %add.14), channel_id=1, source_target_pairs={{0,16},{4,20},{8,24},{12,28},{16,0},{20,4},{24,8},{28,12},{1,17},{... | collective-permute-start | bytes 24584 | tf_op jit(solution)/shard_map/ppermute | solution.py:286
  36.2 1.6 %collective-permute-done.6 = f32[16,128]{1,0:T(8,128)S(1)} collective-permute-done((f32[16,128]{1,0:T(8,128)S(1)}, f32[16,128]{1,0:T(8,128)S(1)}, u32[]{:S(2)}, u32[]{:S(2)}) %collective-permute-start.6) | collective-permute-done | bytes 8224 | tf_op jit(solution)/shard_map/ppermute | solution.py:286
  37.8 0.0 collective-permute-done.2.quad_got_ref
  37.8 0.0 copy-done.1
  37.8 4.5 %last.1 = (f32[48,512]{1,0:T(8,128)}, f32[16,16]{1,0:T(8,128)}, f32[16,16]{1,0:T(8,128)}, f32[1,16]{1,0:T(1,128)}) custom-call(f32[56,512]{1,0:T(8,128)S(1)} %copy-done.1, f32[48,512]{1,0:T(8,128)S(1)} %first.1.prod_ref, f32[48,512]{1,0:T(8,128)S(1)} %collective-permute-done.1.prod_got_ref, f32[48,256]{1,0:T(8,128)S(1)} %get-tuple-element.10.quad_ref, ...), custom_call_target="tpu_custom_call" | custom-call | tf_op jit(solution)/shard_map/last/pallas_call | solution.py:288
  (4 shorter events, 0.0 us)
Async XLA Ops:
  2.3 8.5 %collective-permute-start = (f32[56,512]{1,0:T(8,128)}, f32[56,512]{1,0:T(8,128)S(1)}, u32[]{:S(2)}, u32[]{:S(2)}) collective-permute-start(f32[56,512]{1,0:T(8,128)} %pack.1.own_ref), channel_id=1, source_target_pairs={{5,1},{7,3},{0,4},{9,5},{2,6},{11,7},{4,8},{13,9},{6,10},{15,11},{... | collective-permute-start | bytes 344072 | tf_op jit(solution)/shard_map/ppermute | solution.py:247
  10.7 0.9 %copy-start = (f32[56,512]{1,0:T(8,128)S(1)}, f32[56,512]{1,0:T(8,128)}, u32[]{:S(2)}) copy-start(f32[56,512]{1,0:T(8,128)} %pack.1.own_ref) | copy-start | bytes 344068
  18.2 1.4 %collective-permute-start.1 = (f32[48,512]{1,0:T(8,128)S(1)}, f32[48,512]{1,0:T(8,128)S(1)}, u32[]{:S(2)}, u32[]{:S(2)}) collective-permute-start(f32[48,512]{1,0:T(8,128)S(1)} %first.1.prod_ref), channel_id=1, source_target_pairs={{0,1},{1,0},{2,3},{3,2},{4,5},{5,4},{6,7},{7,6},{8,9},{9,8},{10,11... | collective-permute-start | bytes 294920 | tf_op jit(solution)/shard_map/ppermute | solution.py:250
  19.6 18.3 %copy-start.1 = (f32[56,512]{1,0:T(8,128)S(1)}, f32[56,512]{1,0:T(8,128)}, u32[]{:S(2)}) copy-start(f32[56,512]{1,0:T(8,128)} %pack.1.own_ref) | copy-start | bytes 344068
  24.2 13.7 %collective-permute-start.2 = (f32[48,256]{1,0:T(8,128)S(1)}, f32[48,256]{1,0:T(8,128)S(1)}, u32[]{:S(2)}, u32[]{:S(2)}) collective-permute-start(f32[48,256]{1,0:T(8,128)S(1)} %get-tuple-element.10.quad_ref), channel_id=1, source_target_pairs={{0,1},{1,0},{2,3},{3,2},{4,5},{5,4},{6,7},{7,6},{8,9},{9,8},{10,11... | collective-permute-start | bytes 147464 | tf_op jit(solution)/shard_map/ppermute | solution.py:250
  24.3 1.2 %collective-permute-start.3 = (f32[16,128]{1,0:T(8,128)S(1)}, f32[16,128]{1,0:T(8,128)S(1)}, u32[]{:S(2)}, u32[]{:S(2)}) collective-permute-start(f32[16,128]{1,0:T(8,128)S(1)} %get-tuple-element.11), channel_id=1, source_target_pairs={{0,1},{1,0},{2,3},{3,2},{4,5},{5,4},{6,7},{7,6},{8,9},{9,8},{10,11... | collective-permute-start | bytes 24584 | tf_op jit(solution)/shard_map/ppermute | solution.py:250
  25.5 4.0 %collective-permute-start.4 = (f32[16,128]{1,0:T(8,128)S(1)}, f32[16,128]{1,0:T(8,128)S(1)}, u32[]{:S(2)}, u32[]{:S(2)}) collective-permute-start(f32[16,128]{1,0:T(8,128)S(1)} %add.12), channel_id=1, source_target_pairs={{0,4},{4,0},{8,12},{12,8},{16,20},{20,16},{24,28},{28,24},{1,5},{5... | collective-permute-start | bytes 24584 | tf_op jit(solution)/shard_map/ppermute | solution.py:286
  29.5 3.7 %collective-permute-start.5 = (f32[16,128]{1,0:T(8,128)S(1)}, f32[16,128]{1,0:T(8,128)S(1)}, u32[]{:S(2)}, u32[]{:S(2)}) collective-permute-start(f32[16,128]{1,0:T(8,128)S(1)} %add.13), channel_id=1, source_target_pairs={{0,8},{4,12},{8,0},{12,4},{16,24},{20,28},{24,16},{28,20},{1,9},{5... | collective-permute-start | bytes 24584 | tf_op jit(solution)/shard_map/ppermute | solution.py:286
  33.2 4.6 %collective-permute-start.6 = (f32[16,128]{1,0:T(8,128)S(1)}, f32[16,128]{1,0:T(8,128)S(1)}, u32[]{:S(2)}, u32[]{:S(2)}) collective-permute-start(f32[16,128]{1,0:T(8,128)S(1)} %add.14), channel_id=1, source_target_pairs={{0,16},{4,20},{8,24},{12,28},{16,0},{20,4},{24,8},{28,12},{1,17},{... | collective-permute-start | bytes 24584 | tf_op jit(solution)/shard_map/ppermute | solution.py:286
where the time goes:
time: 42.5 us; the launch traced here: 42.3 us
  Pallas kernels  17.3 us (41%)
  starting transfers between devices  12.8 us (30%)
  waiting for transfers between devices  10.6 us (25%)
  local copies, waits for them, and re-layouts  0.9 us (2%)
  between operations  0.67 us (2%)
    ppermute x3, starting transfers between devices, per_device(): lax.ppermute(gram, 'tile', [(t, t ^ step) for t in range(n_tile)])  7.36 us
    pallas_call x1, Pallas kernels, per_device(): pl.pallas_call(first_kernel, out_shape=jax.ShapeDtypeStruct((rows, width)...  6.55 us
    ppermute x3, waiting for transfers between devices, per_device(): lax.ppermute(gram, 'tile', [(t, t ^ step) for t in range(n_tile)])  4.92 us
    ppermute x1, starting transfers between devices, per_device(): got = lax.ppermute(own, ('tile', 'col'), halo)  4.86 us
    pallas_call x1, Pallas kernels, per_device(): pl.pallas_call(second_kernel, out_shape=(jax.ShapeDtypeStruct((rows, half...  4.58 us
    pallas_call x1, Pallas kernels, per_device(): pl.pallas_call(functools.partial(last_kernel, bead_scale), out_shape=(jax...  4.52 us
    ppermute x1, waiting for transfers between devices, per_device(): got = lax.ppermute(own, ('tile', 'col'), halo)  3.59 us
    ppermute x3, waiting for transfers between devices, swapped(): return lax.ppermute(x, 'col', [(c, c ^ 1) for c in range(n_col)])  2.12 us
  transfers between devices with their start and end apart: 7, of which 6 were waited for; matrix products, arithmetic and copies ran while one was open for 0% of the time, Pallas kernels for 0%

commit v1 on v0

v1 whole, which is shorter than its diff:
```python
import functools

import jax
import jax.numpy as jnp
from jax import lax
from jax.experimental import pallas as pl
from jax.experimental.pallas import tpu as pltpu
from jax.sharding import PartitionSpec as P

TILE_B = 128
REACH = 2
CHUNK = 32

spring_scale = 1.0 / 64.0
cutoff_sq = 225.0
step_size = 0.2
highest = lax.Precision.HIGHEST
f32 = jnp.float32
bf16 = jnp.bfloat16


def parity():
    return lax.rem(lax.axis_index("col"), 2)


def lanes(start, size):
    return pl.ds(pl.multiple_of(start, TILE_B), size)


def pack_kernel(vec_ref, pos_ref, tiles_ref, count_ref, out_ref, tiles, count, pos, sems):
    rows, width = vec_ref.shape
    copies = [
        pltpu.make_async_copy(tiles_ref, tiles, sems.at[0]),
        pltpu.make_async_copy(count_ref, count, sems.at[1]),
        pltpu.make_async_copy(pos_ref, pos, sems.at[2]),
        pltpu.make_async_copy(vec_ref, out_ref.at[0:rows], sems.at[3]),
    ]
    for copy in copies:
        copy.start()
    first_tile = lax.axis_index("tile") * (width // TILE_B)
    tile_of = lax.broadcasted_iota(jnp.int32, (8, width), 1) // TILE_B
    reach_of = lax.broadcasted_iota(jnp.int32, (8, width), 0) - 4
    live = jnp.zeros((8, width), f32)
    copies[0].wait()
    copies[1].wait()
    for c in range(tiles.shape[2]):
        for s in range(tiles.shape[3]):
            row = tiles[0, 0, c, s]
            reach = tiles[1, 0, c, s] - first_tile - row
            row = jnp.where(s < count[0, c], row, -1)
            live += jnp.where((tile_of == row) & (reach_of == reach), cutoff_sq, 0.0)
    out_ref[rows : rows + 8, :] = live
    copies[2].wait()
    out_ref[rows : rows + 3, :] = pos[...]
    copies[3].wait()


def split(x):
    high = x.astype(bf16)
    return high, (x - high.astype(f32)).astype(bf16)


def store_vectors(vec, high, low, x, base):
    place = lanes(base, x.shape[1])
    vec[:, place] = x
    high[:, place], low[:, place] = split(x)


def store_places(pos, pos_t, block, base):
    place = lanes(base, block.shape[1])
    pos[:, place] = block
    if pos_t is not None:
        pos_t[place, :] = jnp.transpose(block)


def tile_slice(w):
    return slice(w * TILE_B, (w + 1) * TILE_B)


def fill_pulls(pos, pos_t, pull_high, pull_low, r, w):
    across = pos[:, tile_slice(w)]
    for j in range(w - REACH, w + REACH + 1):
        first, reach = min(j, w), abs(w - j)
        bound = pos[4 + reach : 5 + reach, tile_slice(first)]
        for q in range(0, TILE_B, CHUNK):
            down = pos_t[j * TILE_B + q : j * TILE_B + q + CHUNK, :]
            offset = [down[:, c : c + 1] - across[c : c + 1, :] for c in range(3)]
            dist_sq = offset[0] * offset[0] + offset[1] * offset[1] + offset[2] * offset[2]
            falloff = jnp.maximum(bound - dist_sq, 0.0)
            weight = falloff * falloff / jnp.maximum(dist_sq, 1.0)
            place = slice((j - w + REACH) * TILE_B + q, (j - w + REACH) * TILE_B + q + CHUNK)
            for c in range(3):
                high, low = split(weight * offset[c])
                pull_high[r, place, tile_slice(c)] = high
                pull_low[r, place, tile_slice(c)] = low


def apply_pulls(vec, high, low, pos, pull_high, pull_low, w):
    rows = vec.shape[0]
    cols = rows // 3
    near = slice((w - REACH) * TILE_B, (w + REACH + 1) * TILE_B)
    here = tile_slice(w)
    middle = jnp.mean(pos[:, here], axis=1, keepdims=True)
    place = pos[:, near] - middle
    row_of = lax.broadcasted_iota(jnp.int32, place.shape, 0)
    extra = jnp.where(row_of < 3, place, jnp.where(row_of == 3, 1.0, 0.0))
    along = sum(place[d : d + 1] * vec[d * cols : (d + 1) * cols, near] for d in range(3))
    more_high, more_low = split(jnp.concatenate([along, extra, jnp.zeros_like(extra)], axis=0))
    left_high = jnp.concatenate([high[:, near], more_high], axis=0)
    left_low = jnp.concatenate([low[:, near], more_low], axis=0)
    left = jnp.concatenate([left_high, left_low], axis=0)
    n = left_high.shape[0]
    with_high = jnp.dot(left, pull_high, preferred_element_type=f32)
    with_low = jnp.dot(left_high, pull_low, preferred_element_type=f32)
    total = with_high[0:n] + (with_high[n:] + with_low)
    mine = [place[d : d + 1, REACH * TILE_B : (REACH + 1) * TILE_B] for d in range(3)]
    out = []
    for c in range(3):
        part = total[:, tile_slice(c)]
        e = rows + cols
        term = -part[rows:e]
        for d in range(3):
            diag = part[e + d : e + d + 1] - mine[d] * part[e + 3 : e + 4]
            term += diag * vec[d * cols : (d + 1) * cols, here] + mine[d] * part[d * cols : (d + 1) * cols]
        out.append(term * (spring_scale * step_size / cutoff_sq**2))
    return jnp.concatenate(out, axis=0)


def first_kernel(own_ref, got_ref, out_ref, pull_high, pull_low, vec, high, low, pos, pos_t):
    rows, width = out_ref.shape
    odd = parity()
    store_vectors(vec, high, low, own_ref[0:rows, :], (1 - odd) * width)
    store_vectors(vec, high, low, got_ref[0:rows, :], odd * width)
    store_places(pos, pos_t, own_ref[rows : rows + 8, :], (1 - odd) * width)
    store_places(pos, pos_t, got_ref[rows : rows + 8, :], odd * width)
    for r in range(width // TILE_B):
        w = REACH + r
        fill_pulls(pos, pos_t, pull_high, pull_low, r, w)
        out_ref[:, tile_slice(r)] = apply_pulls(vec, high, low, pos, pull_high[r], pull_low[r], w)


def second_kernel(
    own_ref, got_ref, prod_ref, prod_got_ref, pull_high, pull_low, out_ref, gram_ref, vec, high, low, pos
):
    rows, width = prod_ref.shape
    cols = rows // 3
    half = width // 2
    odd = parity()
    store_places(pos, None, own_ref[rows : rows + 8, :], (1 - odd) * half)
    store_places(pos, None, got_ref[rows : rows + 8, lanes((1 - odd) * half, half)], odd * width)
    store_vectors(vec, high, low, prod_ref[...], odd * half)
    store_vectors(vec, high, low, prod_got_ref[:, lanes(odd * half, half)], (1 - odd) * width)
    for r in range(REACH):
        from_first = r + (1 - odd) * REACH
        out_ref[:, tile_slice(r)] = apply_pulls(
            vec, high, low, pos, pull_high[from_first], pull_low[from_first], REACH + r
        )
    gram = jnp.zeros((rows, rows), f32)
    for d in range(3):
        band = slice(d * cols, (d + 1) * cols)
        joint = jnp.concatenate(
            [own_ref[band, lanes(odd * half, half)], vec[band, half:width], out_ref[band, :]], axis=0
        )
        gram += lax.dot_general(joint, joint, (((1,), (1,)), ((), ())), precision=highest, preferred_element_type=f32)
    block = [[gram[a * cols : (a + 1) * cols, b * cols : (b + 1) * cols] for b in range(3)] for a in range(3)]
    gram_ref[...] = jnp.zeros(gram_ref.shape, f32)
    for n, part in enumerate((block[0][0], block[0][1], block[1][1], block[1][2], block[2][2])):
        gram_ref[:, n * cols : (n + 1) * cols] = part


def solve(matrix, rhs):
    n = matrix.shape[0]
    joint = jnp.concatenate([matrix, rhs], axis=1)
    row_of = lax.broadcasted_iota(jnp.int32, joint.shape, 0)
    for k in range(n):
        row = joint[k : k + 1, :] / joint[k : k + 1, k : k + 1]
        joint = jnp.where(row_of == k, row, joint - joint[:, k : k + 1] * row)
    return joint[:, n:]


def mul(a, b):
    return jnp.dot(a, b, precision=highest, preferred_element_type=f32)


def mul_t(a, b):
    return lax.dot_general(a, b, (((0,), (0,)), ((), ())), precision=highest, preferred_element_type=f32)


def last_kernel(
    bead_scale, own_ref, prod_ref, prod_got_ref, quad_ref, quad_got_ref, gram_ref, out_ref, ray_ref, corr_ref, norm_ref
):
    rows, width = prod_ref.shape
    cols = rows // 3
    half = width // 2
    odd = parity()
    xx, xp, pp, pq, qq = [gram_ref[:, n * cols : (n + 1) * cols] for n in range(5)]
    row_of = lax.broadcasted_iota(jnp.int32, (cols, cols), 0)
    col_of = lax.broadcasted_iota(jnp.int32, (cols, cols), 1)
    eye = jnp.where(row_of == col_of, 1.0, 0.0).astype(f32)
    shift = solve(xx, xp)
    turn = eye + shift
    first = mul_t(turn, xp)
    corr = mul_t(turn, mul(xx, turn) - xp) - mul_t(xp, turn) + pp
    gram = mul(first, turn) - mul_t(turn, pp) - mul(pp, turn) + pq
    squares = jnp.sum(eye * (mul_t(turn, mul(pp, turn) - 2.0 * pq) + qq), axis=0, keepdims=True)
    second = solve(corr, gram)
    squares = squares - jnp.sum(gram * second, axis=0, keepdims=True)
    ray_ref[...] = gram * (bead_scale / step_size)
    corr_ref[...] = corr * bead_scale
    norm_ref[...] = squares * (bead_scale / step_size**2)
    both = shift + second
    with_vec = both + mul(shift, second)
    for side in range(2):
        here = slice(side * half, (side + 1) * half)
        away = slice((1 - side) * half, (2 - side) * half)
        mine = odd == side
        for d in range(3):
            band = slice(d * cols, (d + 1) * cols)
            vec = own_ref[band, here]
            prod = jnp.where(mine, prod_ref[band, away], prod_got_ref[band, away])
            quad = jnp.where(mine, quad_ref[band, :], quad_got_ref[band, :])
            out_ref[band, here] = vec + mul_t(with_vec, vec) - 2.0 * prod - mul_t(both, prod) + quad


def per_device(positions, trial_block, pair_tiles, pair_count):
    comps, cols, width = trial_block.shape
    rows = comps * cols
    n_tile, n_col = lax.axis_size("tile"), lax.axis_size("col")
    tiles = width // TILE_B
    half = width // 2
    assert tiles == 2 * REACH and n_col % 2 == 0
    bead_scale = 1.0 / (3.0 * n_tile * width)
    vmem = pl.BlockSpec(memory_space=pltpu.VMEM)
    smem = pl.BlockSpec(memory_space=pltpu.SMEM)
    params = pltpu.CompilerParams(vmem_limit_bytes=24 * 2**20)

    hbm = pl.BlockSpec(memory_space=pltpu.HBM)
    own = pl.pallas_call(
        pack_kernel,
        out_shape=jax.ShapeDtypeStruct((rows + 8, width), f32),
        in_specs=[hbm] * 4,
        out_specs=vmem,
        scratch_shapes=[
            pltpu.SMEM(pair_tiles.shape, jnp.int32),
            pltpu.SMEM(pair_count.shape, jnp.int32),
            pltpu.VMEM(positions.shape, f32),
            pltpu.SemaphoreType.DMA((4,)),
        ],
        compiler_params=pltpu.CompilerParams(vmem_limit_bytes=4 * 2**20),
        name="pack",
    )(*[
        pltpu.with_memory_space_constraint(x, pltpu.HBM)
        for x in (trial_block.reshape(rows, width), positions, pair_tiles, pair_count)
    ])

    halo = []
    for t in range(n_tile):
        for c in range(n_col):
            source = t - 1 if c % 2 == 0 else t + 1
            if 0 <= source < n_tile:
                halo.append((source * n_col + c, t * n_col + c))
    got = lax.ppermute(own, ("tile", "col"), halo)

    def swapped(x):
        return lax.ppermute(x, "col", [(c, c ^ 1) for c in range(n_col)])

    def scratch(window):
        return [
            pltpu.VMEM((rows, window), f32),
            pltpu.VMEM((rows, window), bf16),
            pltpu.VMEM((rows, window), bf16),
            pltpu.VMEM((8, window), f32),
        ]

    pulls = jax.ShapeDtypeStruct((tiles, (2 * REACH + 1) * TILE_B, 3 * TILE_B), bf16)
    prod, pull_high, pull_low = pl.pallas_call(
        first_kernel,
        out_shape=(jax.ShapeDtypeStruct((rows, width), f32), pulls, pulls),
        in_specs=[vmem] * 2,
        out_specs=(vmem,) * 3,
        scratch_shapes=scratch(2 * width) + [pltpu.VMEM((2 * width, 8), f32)],
        compiler_params=params,
        name="first",
    )(own, got)
    prod_got = swapped(prod)
    quad, gram = pl.pallas_call(
        second_kernel,
        out_shape=(jax.ShapeDtypeStruct((rows, half), f32), jax.ShapeDtypeStruct((cols, 128), f32)),
        in_specs=[vmem] * 6,
        out_specs=(vmem, vmem),
        scratch_shapes=scratch(width + half),
        compiler_params=params,
        name="second",
    )(own, got, prod, prod_got, pull_high, pull_low)
    gram = gram + swapped(gram)
    quad_got = swapped(quad)
    step = 1
    while step < n_tile:
        gram = gram + lax.ppermute(gram, "tile", [(t, t ^ step) for t in range(n_tile)])
        step *= 2
    block, ray, corr, norms = pl.pallas_call(
        functools.partial(last_kernel, bead_scale),
        out_shape=(
            jax.ShapeDtypeStruct((rows, width), f32),
            jax.ShapeDtypeStruct((cols, cols), f32),
            jax.ShapeDtypeStruct((cols, cols), f32),
            jax.ShapeDtypeStruct((1, cols), f32),
        ),
        in_specs=[vmem] * 6,
        out_specs=(vmem,) * 4,
        compiler_params=params,
        name="last",
    )(own, prod, prod_got, quad, quad_got, gram)
    return block.reshape(comps, cols, width), ray, corr, norms.reshape(cols)


def solution(mesh):
    return jax.shard_map(
        per_device,
        mesh=mesh,
        in_specs=(
            P(None, "tile"),
            P(None, None, "tile"),
            P(None, "tile", None, None),
            P("tile", None),
        ),
        out_specs=(P(None, None, "tile"), P(), P(), P()),
        check_vma=False,
    )
```

time: 42.5 us -> 33.5 us (0.79)
  Pallas kernels: 17.3 us -> 9.38 us
  local copies, waits for them, and re-layouts: 0.9 us -> 0 us
    pallas_call x1, Pallas kernels: 6.55 us -> 2.93 us  [per_device(): pl.pallas_call(first_kernel, out_shape=(jax.ShapeDtypeStruct((rows, width...]
    pallas_call x1, Pallas kernels: 4.58 us -> 0.99 us  [per_device(): pl.pallas_call(second_kernel, out_shape=(jax.ShapeDtypeStruct((rows, half...]
    unnamed x4 -> x0, local copies, waits for them, and re-layouts: 0.9 us -> none
    pallas_call x1, Pallas kernels: 1.65 us -> 0.95 us  [per_device(): pl.pallas_call(pack_kernel, out_shape=jax.ShapeDtypeStruct((rows + 8, wid...]
where the time goes in v1:
time: 33.5 us; the launch traced here: 33.3 us
  starting transfers between devices  12.9 us (39%)
  waiting for transfers between devices  10.3 us (31%)
  Pallas kernels  9.38 us (28%)
  between operations  0.67 us (2%)
    ppermute x3, starting transfers between devices, per_device(): lax.ppermute(gram, 'tile', [(t, t ^ step) for t in range(n_tile)])  7.46 us
    ppermute x3, waiting for transfers between devices, per_device(): lax.ppermute(gram, 'tile', [(t, t ^ step) for t in range(n_tile)])  4.92 us
    ppermute x1, starting transfers between devices, per_device(): got = lax.ppermute(own, ('tile', 'col'), halo)  4.88 us
    pallas_call x1, Pallas kernels, per_device(): pl.pallas_call(functools.partial(last_kernel, bead_scale), out_shape=(jax...  4.51 us
    ppermute x1, waiting for transfers between devices, per_device(): got = lax.ppermute(own, ('tile', 'col'), halo)  3.28 us
    pallas_call x1, Pallas kernels, per_device(): pl.pallas_call(first_kernel, out_shape=(jax.ShapeDtypeStruct((rows, width...  2.93 us
    ppermute x3, waiting for transfers between devices, swapped(): return lax.ppermute(x, 'col', [(c, c ^ 1) for c in range(n_col)])  2.12 us
    pallas_call x1, Pallas kernels, per_device(): pl.pallas_call(second_kernel, out_shape=(jax.ShapeDtypeStruct((rows, half...  0.99 us
  transfers between devices with their start and end apart: 7, of which 6 were waited for; matrix products, arithmetic and copies ran while one was open for 0% of the time, Pallas kernels for 0%

profile of v1, /device:TPU:0, one launch (start us, length us, event | category | flops | bytes accessed | tf_op | source)
XLA Modules:
  0.0 33.3 jit_solution(17388103971967630888)
XLA Ops:
  0.6 0.9 %pack.1.own_ref = f32[56,512]{1,0:T(8,128)S(1)} custom-call(f32[48,512]{1,0:T(8,128)} %bitcast.3, f32[3,512]{1,0:T(4,128)} %pos_ref.1, s32[2,1,4,8]{3,2,1,0:T(4,128)} %tiles_ref.1, s32[1,4]{1,0:T(1,128)} %count_ref.1), custom_call_target="tpu_custom_call" | custom-call | tf_op jit(solution)/shard_map/pack/pallas_call | solution.py:238
  1.6 4.9 %collective-permute-start = (f32[56,512]{1,0:T(8,128)S(1)}, f32[56,512]{1,0:T(8,128)S(1)}, u32[]{:S(2)}, u32[]{:S(2)}) collective-permute-start(f32[56,512]{1,0:T(8,128)S(1)} %pack.1.own_ref), channel_id=1, source_target_pairs={{5,1},{7,3},{0,4},{9,5},{2,6},{11,7},{4,8},{13,9},{6,10},{15,11},{... | collective-permute-start | bytes 344072 | tf_op jit(solution)/shard_map/ppermute | solution.py:262
  6.5 3.3 %collective-permute-done.got_ref = f32[56,512]{1,0:T(8,128)S(1)} collective-permute-done((f32[56,512]{1,0:T(8,128)S(1)}, f32[56,512]{1,0:T(8,128)S(1)}, u32[]{:S(2)}, u32[]{:S(2)}) %collective-permute-start) | collective-permute-done | bytes 114720 | tf_op jit(solution)/shard_map/ppermute | solution.py:262
  9.8 2.9 %first.1 = (f32[48,512]{1,0:T(8,128)S(1)}, bf16[4,640,384]{2,1,0:T(8,128)(2,1)S(1)}, bf16[4,640,384]{2,1,0:T(8,128)(2,1)S(1)}) custom-call(f32[56,512]{1,0:T(8,128)S(1)} %pack.1.own_ref, f32[56,512]{1,0:T(8,128)S(1)} %collective-permute-done.got_ref), custom_call_target="tpu_custom_call" | custom-call | tf_op jit(solution)/shard_map/first/pallas_call | solution.py:276
  12.7 0.1 collective-permute-start.1
  12.8 1.3 %collective-permute-done.1.prod_got_ref = f32[48,512]{1,0:T(8,128)S(1)} collective-permute-done((f32[48,512]{1,0:T(8,128)S(1)}, f32[48,512]{1,0:T(8,128)S(1)}, u32[]{:S(2)}, u32[]{:S(2)}) %collective-permute-start.1) | collective-permute-done | bytes 98336 | tf_op jit(solution)/shard_map/ppermute | solution.py:265
  14.1 1.0 %second.1 = (f32[48,256]{1,0:T(8,128)S(1)}, f32[16,128]{1,0:T(8,128)S(1)}) custom-call(f32[56,512]{1,0:T(8,128)S(1)} %pack.1.own_ref, f32[56,512]{1,0:T(8,128)S(1)} %collective-permute-done.got_ref, f32[48,512]{1,0:T(8,128)S(1)} %get-tuple-element.13.prod_ref, f32[48,512]{1,0:T(8,128)S(1)} %collective-permute-done.1.prod_got_ref, ...), custom_call_target="tpu_custom_call" | custom-call | tf_op jit(solution)/shard_map/second/pallas_call | solution.py:286
  15.1 0.2 collective-permute-start.2
  15.2 0.4 %collective-permute-start.3 = (f32[16,128]{1,0:T(8,128)S(1)}, f32[16,128]{1,0:T(8,128)S(1)}, u32[]{:S(2)}, u32[]{:S(2)}) collective-permute-start(f32[16,128]{1,0:T(8,128)S(1)} %get-tuple-element.17), channel_id=1, source_target_pairs={{0,1},{1,0},{2,3},{3,2},{4,5},{5,4},{6,7},{7,6},{8,9},{9,8},{10,11... | collective-permute-start | bytes 24584 | tf_op jit(solution)/shard_map/ppermute | solution.py:265
  15.6 0.8 %collective-permute-done.3 = f32[16,128]{1,0:T(8,128)S(1)} collective-permute-done((f32[16,128]{1,0:T(8,128)S(1)}, f32[16,128]{1,0:T(8,128)S(1)}, u32[]{:S(2)}, u32[]{:S(2)}) %collective-permute-start.3) | collective-permute-done | bytes 8224 | tf_op jit(solution)/shard_map/ppermute | solution.py:265
  16.4 2.5 %collective-permute-start.4 = (f32[16,128]{1,0:T(8,128)S(1)}, f32[16,128]{1,0:T(8,128)S(1)}, u32[]{:S(2)}, u32[]{:S(2)}) collective-permute-start(f32[16,128]{1,0:T(8,128)S(1)} %add.12), channel_id=1, source_target_pairs={{0,4},{4,0},{8,12},{12,8},{16,20},{20,16},{24,28},{28,24},{1,5},{5... | collective-permute-start | bytes 24584 | tf_op jit(solution)/shard_map/ppermute | solution.py:299
  18.9 1.6 %collective-permute-done.4 = f32[16,128]{1,0:T(8,128)S(1)} collective-permute-done((f32[16,128]{1,0:T(8,128)S(1)}, f32[16,128]{1,0:T(8,128)S(1)}, u32[]{:S(2)}, u32[]{:S(2)}) %collective-permute-start.4) | collective-permute-done | bytes 8224 | tf_op jit(solution)/shard_map/ppermute | solution.py:299
  20.5 2.0 %collective-permute-start.5 = (f32[16,128]{1,0:T(8,128)S(1)}, f32[16,128]{1,0:T(8,128)S(1)}, u32[]{:S(2)}, u32[]{:S(2)}) collective-permute-start(f32[16,128]{1,0:T(8,128)S(1)} %add.13), channel_id=1, source_target_pairs={{0,8},{4,12},{8,0},{12,4},{16,24},{20,28},{24,16},{28,20},{1,9},{5... | collective-permute-start | bytes 24584 | tf_op jit(solution)/shard_map/ppermute | solution.py:299
  22.5 1.7 %collective-permute-done.5 = f32[16,128]{1,0:T(8,128)S(1)} collective-permute-done((f32[16,128]{1,0:T(8,128)S(1)}, f32[16,128]{1,0:T(8,128)S(1)}, u32[]{:S(2)}, u32[]{:S(2)}) %collective-permute-start.5) | collective-permute-done | bytes 8224 | tf_op jit(solution)/shard_map/ppermute | solution.py:299
  24.2 3.0 %collective-permute-start.6 = (f32[16,128]{1,0:T(8,128)S(1)}, f32[16,128]{1,0:T(8,128)S(1)}, u32[]{:S(2)}, u32[]{:S(2)}) collective-permute-start(f32[16,128]{1,0:T(8,128)S(1)} %add.14), channel_id=1, source_target_pairs={{0,16},{4,20},{8,24},{12,28},{16,0},{20,4},{24,8},{28,12},{1,17},{... | collective-permute-start | bytes 24584 | tf_op jit(solution)/shard_map/ppermute | solution.py:299
  27.2 1.6 %collective-permute-done.6 = f32[16,128]{1,0:T(8,128)S(1)} collective-permute-done((f32[16,128]{1,0:T(8,128)S(1)}, f32[16,128]{1,0:T(8,128)S(1)}, u32[]{:S(2)}, u32[]{:S(2)}) %collective-permute-start.6) | collective-permute-done | bytes 8224 | tf_op jit(solution)/shard_map/ppermute | solution.py:299
  28.8 0.0 collective-permute-done.2.quad_got_ref
  28.8 4.5 %last.1 = (f32[48,512]{1,0:T(8,128)}, f32[16,16]{1,0:T(8,128)}, f32[16,16]{1,0:T(8,128)}, f32[1,16]{1,0:T(1,128)}) custom-call(f32[56,512]{1,0:T(8,128)S(1)} %pack.1.own_ref, f32[48,512]{1,0:T(8,128)S(1)} %get-tuple-element.13.prod_ref, f32[48,512]{1,0:T(8,128)S(1)} %collective-permute-done.1.prod_got_ref, f32[48,256]{1,0:T(8,128)S(1)} %get-tuple-element.16.quad_ref, ...), custom_call_target="tpu_custom_call" | custom-call | tf_op jit(solution)/shard_map/last/pallas_call | solution.py:301
  (4 shorter events, 0.0 us)
Async XLA Ops:
  1.6 8.2 %collective-permute-start = (f32[56,512]{1,0:T(8,128)S(1)}, f32[56,512]{1,0:T(8,128)S(1)}, u32[]{:S(2)}, u32[]{:S(2)}) collective-permute-start(f32[56,512]{1,0:T(8,128)S(1)} %pack.1.own_ref), channel_id=1, source_target_pairs={{5,1},{7,3},{0,4},{9,5},{2,6},{11,7},{4,8},{13,9},{6,10},{15,11},{... | collective-permute-start | bytes 344072 | tf_op jit(solution)/shard_map/ppermute | solution.py:262
  12.7 1.4 %collective-permute-start.1 = (f32[48,512]{1,0:T(8,128)S(1)}, f32[48,512]{1,0:T(8,128)S(1)}, u32[]{:S(2)}, u32[]{:S(2)}) collective-permute-start(f32[48,512]{1,0:T(8,128)S(1)} %get-tuple-element.13.prod_ref), channel_id=1, source_target_pairs={{0,1},{1,0},{2,3},{3,2},{4,5},{5,4},{6,7},{7,6},{8,9},{9,8},{10,11... | collective-permute-start | bytes 294920 | tf_op jit(solution)/shard_map/ppermute | solution.py:265
  15.1 13.8 %collective-permute-start.2 = (f32[48,256]{1,0:T(8,128)S(1)}, f32[48,256]{1,0:T(8,128)S(1)}, u32[]{:S(2)}, u32[]{:S(2)}) collective-permute-start(f32[48,256]{1,0:T(8,128)S(1)} %get-tuple-element.16.quad_ref), channel_id=1, source_target_pairs={{0,1},{1,0},{2,3},{3,2},{4,5},{5,4},{6,7},{7,6},{8,9},{9,8},{10,11... | collective-permute-start | bytes 147464 | tf_op jit(solution)/shard_map/ppermute | solution.py:265
  15.2 1.2 %collective-permute-start.3 = (f32[16,128]{1,0:T(8,128)S(1)}, f32[16,128]{1,0:T(8,128)S(1)}, u32[]{:S(2)}, u32[]{:S(2)}) collective-permute-start(f32[16,128]{1,0:T(8,128)S(1)} %get-tuple-element.17), channel_id=1, source_target_pairs={{0,1},{1,0},{2,3},{3,2},{4,5},{5,4},{6,7},{7,6},{8,9},{9,8},{10,11... | collective-permute-start | bytes 24584 | tf_op jit(solution)/shard_map/ppermute | solution.py:265
  16.4 4.1 %collective-permute-start.4 = (f32[16,128]{1,0:T(8,128)S(1)}, f32[16,128]{1,0:T(8,128)S(1)}, u32[]{:S(2)}, u32[]{:S(2)}) collective-permute-start(f32[16,128]{1,0:T(8,128)S(1)} %add.12), channel_id=1, source_target_pairs={{0,4},{4,0},{8,12},{12,8},{16,20},{20,16},{24,28},{28,24},{1,5},{5... | collective-permute-start | bytes 24584 | tf_op jit(solution)/shard_map/ppermute | solution.py:299
  20.5 3.7 %collective-permute-start.5 = (f32[16,128]{1,0:T(8,128)S(1)}, f32[16,128]{1,0:T(8,128)S(1)}, u32[]{:S(2)}, u32[]{:S(2)}) collective-permute-start(f32[16,128]{1,0:T(8,128)S(1)} %add.13), channel_id=1, source_target_pairs={{0,8},{4,12},{8,0},{12,4},{16,24},{20,28},{24,16},{28,20},{1,9},{5... | collective-permute-start | bytes 24584 | tf_op jit(solution)/shard_map/ppermute | solution.py:299
  24.2 4.6 %collective-permute-start.6 = (f32[16,128]{1,0:T(8,128)S(1)}, f32[16,128]{1,0:T(8,128)S(1)}, u32[]{:S(2)}, u32[]{:S(2)}) collective-permute-start(f32[16,128]{1,0:T(8,128)S(1)} %add.14), channel_id=1, source_target_pairs={{0,16},{4,20},{8,24},{12,28},{16,0},{20,4},{24,8},{28,12},{1,17},{... | collective-permute-start | bytes 24584 | tf_op jit(solution)/shard_map/ppermute | solution.py:299

commit v2 on v1

--- a/solution.py
+++ b/solution.py
@@ -64,6 +64,13 @@
     place = lanes(base, x.shape[1])
     vec[:, place] = x
     high[:, place], low[:, place] = split(x)
+
+
+def received_places(block):
+    t = lax.axis_index("tile")
+    missing = jnp.where(parity() == 0, t == 0, t == lax.axis_size("tile") - 1)
+    row_of = lax.broadcasted_iota(jnp.int32, block.shape, 0)
+    return jnp.where((row_of > 3) & missing, 0.0, block)
 
 
 def store_places(pos, pos_t, block, base):
@@ -132,7 +139,7 @@
     store_vectors(vec, high, low, own_ref[0:rows, :], (1 - odd) * width)
     store_vectors(vec, high, low, got_ref[0:rows, :], odd * width)
     store_places(pos, pos_t, own_ref[rows : rows + 8, :], (1 - odd) * width)
-    store_places(pos, pos_t, got_ref[rows : rows + 8, :], odd * width)
+    store_places(pos, pos_t, received_places(got_ref[rows : rows + 8, :]), odd * width)
     for r in range(width // TILE_B):
         w = REACH + r
         fill_pulls(pos, pos_t, pull_high, pull_low, r, w)
@@ -172,9 +179,15 @@
     n = matrix.shape[0]
     joint = jnp.concatenate([matrix, rhs], axis=1)
     row_of = lax.broadcasted_iota(jnp.int32, joint.shape, 0)
-    for k in range(n):
-        row = joint[k : k + 1, :] / joint[k : k + 1, k : k + 1]
-        joint = jnp.where(row_of == k, row, joint - joint[:, k : k + 1] * row)
+    for k in range(0, n, 2):
+        col = [jnp.broadcast_to(joint[:, k + i : k + i + 1], joint.shape) for i in range(2)]
+        row = [joint[k + i : k + i + 1, :] for i in range(2)]
+        inverse = 1.0 / col[0][k : k + 1]
+        ratio = col[0][k + 1 : k + 2] * inverse
+        lower = (row[1] - ratio * row[0]) / (col[1][k + 1 : k + 2] - ratio * col[1][k : k + 1])
+        upper = (row[0] - col[1][k : k + 1] * lower) * inverse
+        joint = joint - col[0] * upper - col[1] * lower
+        joint = jnp.where(row_of == k, upper, jnp.where(row_of == k + 1, lower, joint))
     return joint[:, n:]
 
 
@@ -187,7 +200,22 @@
 
 
 def last_kernel(
-    bead_scale, own_ref, prod_ref, prod_got_ref, quad_ref, quad_got_ref, gram_ref, out_ref, ray_ref, corr_ref, norm_ref
+    bead_scale,
+    own_ref,
+    prod_ref,
+    prod_got_ref,
+    quad_ref,
+    quad_got_ref,
+    gram_ref,
+    out_ref,
+    ray_ref,
+    corr_ref,
+    norm_ref,
+    out,
+    ray,
+    small,
+    norm,
+    sems,
 ):
     rows, width = prod_ref.shape
     cols = rows // 3
@@ -198,28 +226,47 @@
     col_of = lax.broadcasted_iota(jnp.int32, (cols, cols), 1)
     eye = jnp.where(row_of == col_of, 1.0, 0.0).astype(f32)
     shift = solve(xx, xp)
+    rest = pp - mul_t(xp, shift)
+    corr = xx + rest
+    gram = xp - 2.0 * rest + pq - mul_t(shift, pp) - mul(rest, shift)
+    second = solve(corr, gram)
+    both = shift + second
     turn = eye + shift
-    first = mul_t(turn, xp)
-    corr = mul_t(turn, mul(xx, turn) - xp) - mul_t(xp, turn) + pp
-    gram = mul(first, turn) - mul_t(turn, pp) - mul(pp, turn) + pq
-    squares = jnp.sum(eye * (mul_t(turn, mul(pp, turn) - 2.0 * pq) + qq), axis=0, keepdims=True)
-    second = solve(corr, gram)
-    squares = squares - jnp.sum(gram * second, axis=0, keepdims=True)
-    ray_ref[...] = gram * (bead_scale / step_size)
-    corr_ref[...] = corr * bead_scale
-    norm_ref[...] = squares * (bead_scale / step_size**2)
-    both = shift + second
-    with_vec = both + mul(shift, second)
-    for side in range(2):
-        here = slice(side * half, (side + 1) * half)
-        away = slice((1 - side) * half, (2 - side) * half)
-        mine = odd == side
-        for d in range(3):
-            band = slice(d * cols, (d + 1) * cols)
-            vec = own_ref[band, here]
-            prod = jnp.where(mine, prod_ref[band, away], prod_got_ref[band, away])
-            quad = jnp.where(mine, quad_ref[band, :], quad_got_ref[band, :])
-            out_ref[band, here] = vec + mul_t(with_vec, vec) - 2.0 * prod - mul_t(both, prod) + quad
+    squares = turn * (mul(pp, turn) - 2.0 * pq) + eye * qq - gram * second
+    ray[...] = gram * (bead_scale / step_size)
+    small[...] = corr * bead_scale
+    norm[...] = jnp.sum(squares, axis=0, keepdims=True) * (bead_scale / step_size**2)
+    copies = [
+        pltpu.make_async_copy(ray, ray_ref, sems.at[0]),
+        pltpu.make_async_copy(small, corr_ref, sems.at[1]),
+        pltpu.make_async_copy(norm, norm_ref, sems.at[2]),
+    ]
+    factor = jnp.concatenate([both + mul(shift, second), -both], axis=0)
+    factor_high, factor_low = split(factor)
+    factor = jnp.concatenate([factor_high, factor_low], axis=1)
+    for d in range(3):
+        band = slice(d * cols, (d + 1) * cols)
+        prod, quad = [], []
+        for side in range(2):
+            away = slice((1 - side) * half, (2 - side) * half)
+            mine = odd == side
+            prod.append(jnp.where(mine, prod_ref[band, away], prod_got_ref[band, away]))
+            quad.append(jnp.where(mine, quad_ref[band, :], quad_got_ref[band, :]))
+        vec = own_ref[band, :]
+        prod = jnp.concatenate(prod, axis=1)
+        quad = jnp.concatenate(quad, axis=1)
+        high, low = split(jnp.concatenate([vec, prod], axis=0))
+        turned = lax.dot_general(factor, high, (((0,), (0,)), ((), ())), preferred_element_type=f32)
+        small_turned = lax.dot_general(factor_high, low, (((0,), (0,)), ((), ())), preferred_element_type=f32)
+        out[band, :] = vec - 2.0 * prod + quad + (turned[0:cols] + (turned[cols:] + small_turned))
+        copies.append(pltpu.make_async_copy(out.at[band], out_ref.at[band], sems.at[3 + d]))
+        if d == 0:
+            for copy in copies:
+                copy.start()
+        else:
+            copies[-1].start()
+    for copy in copies:
+        copy.wait()
 
 
 def per_device(positions, trial_block, pair_tiles, pair_count):
@@ -259,6 +306,8 @@
             source = t - 1 if c % 2 == 0 else t + 1
             if 0 <= source < n_tile:
                 halo.append((source * n_col + c, t * n_col + c))
+            else:
+                halo.append((t * n_col + (c ^ 1), t * n_col + c))
     got = lax.ppermute(own, ("tile", "col"), halo)
 
     def swapped(x):
@@ -294,20 +343,28 @@
     )(own, got, prod, prod_got, pull_high, pull_low)
     gram = gram + swapped(gram)
     quad_got = swapped(quad)
+
+    def crossed(x, step):
+        route = [
+            (t * n_col + c, (t ^ step) * n_col + (c ^ 1)) for t in range(n_tile) for c in range(n_col)
+        ]
+        return lax.ppermute(x, ("tile", "col"), route)
+
     step = 1
     while step < n_tile:
-        gram = gram + lax.ppermute(gram, "tile", [(t, t ^ step) for t in range(n_tile)])
-        step *= 2
+        if 2 * step < n_tile:
+            near, far, both = [crossed(gram, s) for s in (step, 2 * step, 3 * step)]
+            gram = (gram + near) + (far + both)
+        else:
+            gram = gram + crossed(gram, step)
+        step *= 4
+    shapes = [(rows, width), (cols, cols), (cols, cols), (1, cols)]
     block, ray, corr, norms = pl.pallas_call(
         functools.partial(last_kernel, bead_scale),
-        out_shape=(
-            jax.ShapeDtypeStruct((rows, width), f32),
-            jax.ShapeDtypeStruct((cols, cols), f32),
-            jax.ShapeDtypeStruct((cols, cols), f32),
-            jax.ShapeDtypeStruct((1, cols), f32),
-        ),
+        out_shape=tuple(jax.ShapeDtypeStruct(shape, f32) for shape in shapes),
         in_specs=[vmem] * 6,
-        out_specs=(vmem,) * 4,
+        out_specs=(hbm,) * 4,
+        scratch_shapes=[pltpu.VMEM(shape, f32) for shape in shapes] + [pltpu.SemaphoreType.DMA((6,))],
         compiler_params=params,
         name="last",
     )(own, prod, prod_got, quad, quad_got, gram)

time: 33.5 us -> 28.7 us (0.86)
  starting transfers between devices: 12.9 us -> 9.56 us
  Pallas kernels: 9.38 us -> 8.28 us
    ppermute x1, starting transfers between devices: 4.88 us -> 3.02 us  [per_device(): got = lax.ppermute(own, ('tile', 'col'), halo)]
    ppermute x3 -> x4, starting transfers between devices: 7.46 us -> 6.14 us  [crossed(): return lax.ppermute(x, ('tile', 'col'), route)]
    pallas_call x1, Pallas kernels: 4.51 us -> 3.45 us  [per_device(): pl.pallas_call(functools.partial(last_kernel, bead_scale), out_shape=tupl...]
    ppermute x3 -> x4, waiting for transfers between devices: 4.92 us -> 4.4 us  [crossed(): return lax.ppermute(x, ('tile', 'col'), route)]
  transfers between devices with their start and end apart: 7 -> 8, of which waited for: 6 -> 7; matrix products, arithmetic and copies ran while one was open for 0% -> 0% of each run, Pallas kernels for 0% -> 0%
where the time goes in v2:
time: 28.7 us; the launch traced here: 28.5 us
  waiting for transfers between devices  10 us (35%)
  starting transfers between devices  9.56 us (33%)
  Pallas kernels  8.28 us (29%)
  between operations  0.66 us (2%)
    ppermute x4, starting transfers between devices, crossed(): return lax.ppermute(x, ('tile', 'col'), route)  6.14 us
    ppermute x4, waiting for transfers between devices, crossed(): return lax.ppermute(x, ('tile', 'col'), route)  4.4 us
    pallas_call x1, Pallas kernels, per_device(): pl.pallas_call(functools.partial(last_kernel, bead_scale), out_shape=tupl...  3.45 us
    ppermute x1, waiting for transfers between devices, per_device(): got = lax.ppermute(own, ('tile', 'col'), halo)  3.3 us
    ppermute x1, starting transfers between devices, per_device(): got = lax.ppermute(own, ('tile', 'col'), halo)  3.02 us
    pallas_call x1, Pallas kernels, per_device(): pl.pallas_call(first_kernel, out_shape=(jax.ShapeDtypeStruct((rows, width...  2.89 us
    ppermute x3, waiting for transfers between devices, swapped(): return lax.ppermute(x, 'col', [(c, c ^ 1) for c in range(n_col)])  2.33 us
    pallas_call x1, Pallas kernels, per_device(): pl.pallas_call(second_kernel, out_shape=(jax.ShapeDtypeStruct((rows, half...  1 us
  transfers between devices with their start and end apart: 8, of which 7 were waited for; matrix products, arithmetic and copies ran while one was open for 0% of the time, Pallas kernels for 0%

profile of v2, /device:TPU:0, one launch (start us, length us, event | category | flops | bytes accessed | tf_op | source)
XLA Modules:
  0.0 28.5 jit_solution(17087280124506550625)
XLA Ops:
  0.6 0.9 %pack.1.own_ref = f32[56,512]{1,0:T(8,128)S(1)} custom-call(f32[48,512]{1,0:T(8,128)} %bitcast.3, f32[3,512]{1,0:T(4,128)} %pos_ref.1, s32[2,1,4,8]{3,2,1,0:T(4,128)} %tiles_ref.1, s32[1,4]{1,0:T(1,128)} %count_ref.1), custom_call_target="tpu_custom_call" | custom-call | tf_op jit(solution)/shard_map/pack/pallas_call | solution.py:285
  1.6 3.0 %collective-permute-start = (f32[56,512]{1,0:T(8,128)S(1)}, f32[56,512]{1,0:T(8,128)S(1)}, u32[]{:S(2)}, u32[]{:S(2)}) collective-permute-start(f32[56,512]{1,0:T(8,128)S(1)} %pack.1.own_ref), channel_id=1, source_target_pairs={{1,0},{5,1},{3,2},{7,3},{0,4},{9,5},{2,6},{11,7},{4,8},{13,9},{6,1... | collective-permute-start | bytes 344072 | tf_op jit(solution)/shard_map/ppermute | solution.py:311
  4.6 3.3 %collective-permute-done.got_ref = f32[56,512]{1,0:T(8,128)S(1)} collective-permute-done((f32[56,512]{1,0:T(8,128)S(1)}, f32[56,512]{1,0:T(8,128)S(1)}, u32[]{:S(2)}, u32[]{:S(2)}) %collective-permute-start) | collective-permute-done | bytes 114720 | tf_op jit(solution)/shard_map/ppermute | solution.py:311
  7.9 2.9 %first.1 = (f32[48,512]{1,0:T(8,128)S(1)}, bf16[4,640,384]{2,1,0:T(8,128)(2,1)S(1)}, bf16[4,640,384]{2,1,0:T(8,128)(2,1)S(1)}) custom-call(f32[56,512]{1,0:T(8,128)S(1)} %pack.1.own_ref, f32[56,512]{1,0:T(8,128)S(1)} %collective-permute-done.got_ref), custom_call_target="tpu_custom_call" | custom-call | tf_op jit(solution)/shard_map/first/pallas_call | solution.py:325
  10.8 0.1 collective-permute-start.1
  10.9 1.3 %collective-permute-done.1.prod_got_ref = f32[48,512]{1,0:T(8,128)S(1)} collective-permute-done((f32[48,512]{1,0:T(8,128)S(1)}, f32[48,512]{1,0:T(8,128)S(1)}, u32[]{:S(2)}, u32[]{:S(2)}) %collective-permute-start.1) | collective-permute-done | bytes 98336 | tf_op jit(solution)/shard_map/ppermute | solution.py:314
  12.2 1.0 %second.1 = (f32[48,256]{1,0:T(8,128)S(1)}, f32[16,128]{1,0:T(8,128)S(1)}) custom-call(f32[56,512]{1,0:T(8,128)S(1)} %pack.1.own_ref, f32[56,512]{1,0:T(8,128)S(1)} %collective-permute-done.got_ref, f32[48,512]{1,0:T(8,128)S(1)} %get-tuple-element.13.prod_ref, f32[48,512]{1,0:T(8,128)S(1)} %collective-permute-done.1.prod_got_ref, ...), custom_call_target="tpu_custom_call" | custom-call | tf_op jit(solution)/shard_map/second/pallas_call | solution.py:335
  13.2 0.2 collective-permute-start.3
  13.3 1.0 %collective-permute-done.3 = f32[16,128]{1,0:T(8,128)S(1)} collective-permute-done((f32[16,128]{1,0:T(8,128)S(1)}, f32[16,128]{1,0:T(8,128)S(1)}, u32[]{:S(2)}, u32[]{:S(2)}) %collective-permute-start.3) | collective-permute-done | bytes 8224 | tf_op jit(solution)/shard_map/ppermute | solution.py:314
  14.4 3.3 %collective-permute-start.6 = (f32[16,128]{1,0:T(8,128)S(1)}, f32[16,128]{1,0:T(8,128)S(1)}, u32[]{:S(2)}, u32[]{:S(2)}) collective-permute-start(f32[16,128]{1,0:T(8,128)S(1)} %add.15), channel_id=1, source_target_pairs={{0,13},{1,12},{2,15},{3,14},{4,9},{5,8},{6,11},{7,10},{8,5},{9,4},... | collective-permute-start | bytes 24584 | tf_op jit(solution)/shard_map/ppermute | solution.py:351
  17.6 0.4 %collective-permute-start.5 = (f32[16,128]{1,0:T(8,128)S(1)}, f32[16,128]{1,0:T(8,128)S(1)}, u32[]{:S(2)}, u32[]{:S(2)}) collective-permute-start(f32[16,128]{1,0:T(8,128)S(1)} %add.15), channel_id=1, source_target_pairs={{0,9},{1,8},{2,11},{3,10},{4,13},{5,12},{6,15},{7,14},{8,1},{9,0},... | collective-permute-start | bytes 24584 | tf_op jit(solution)/shard_map/ppermute | solution.py:351
  18.0 0.1 collective-permute-start.4
  18.1 0.2 collective-permute-start.2
  18.3 0.7 %collective-permute-done.6 = f32[16,128]{1,0:T(8,128)S(1)} collective-permute-done((f32[16,128]{1,0:T(8,128)S(1)}, f32[16,128]{1,0:T(8,128)S(1)}, u32[]{:S(2)}, u32[]{:S(2)}) %collective-permute-start.6) | collective-permute-done | bytes 8224 | tf_op jit(solution)/shard_map/ppermute | solution.py:351
  19.0 1.7 %collective-permute-done.5 = f32[16,128]{1,0:T(8,128)S(1)} collective-permute-done((f32[16,128]{1,0:T(8,128)S(1)}, f32[16,128]{1,0:T(8,128)S(1)}, u32[]{:S(2)}, u32[]{:S(2)}) %collective-permute-start.5) | collective-permute-done | bytes 8224 | tf_op jit(solution)/shard_map/ppermute | solution.py:351
  20.7 0.4 %collective-permute-done.4 = f32[16,128]{1,0:T(8,128)S(1)} collective-permute-done((f32[16,128]{1,0:T(8,128)S(1)}, f32[16,128]{1,0:T(8,128)S(1)}, u32[]{:S(2)}, u32[]{:S(2)}) %collective-permute-start.4) | collective-permute-done | bytes 8224 | tf_op jit(solution)/shard_map/ppermute | solution.py:351
  21.1 2.4 %collective-permute-start.7 = (f32[16,128]{1,0:T(8,128)S(1)}, f32[16,128]{1,0:T(8,128)S(1)}, u32[]{:S(2)}, u32[]{:S(2)}) collective-permute-start(f32[16,128]{1,0:T(8,128)S(1)} %add_add_fusion), channel_id=1, source_target_pairs={{0,17},{1,16},{2,19},{3,18},{4,21},{5,20},{6,23},{7,22},{8,25},{9,... | collective-permute-start | bytes 24584 | tf_op jit(solution)/shard_map/ppermute | solution.py:351
  23.5 1.6 %collective-permute-done.7 = f32[16,128]{1,0:T(8,128)S(1)} collective-permute-done((f32[16,128]{1,0:T(8,128)S(1)}, f32[16,128]{1,0:T(8,128)S(1)}, u32[]{:S(2)}, u32[]{:S(2)}) %collective-permute-start.7) | collective-permute-done | bytes 8224 | tf_op jit(solution)/shard_map/ppermute | solution.py:351
  25.1 0.0 collective-permute-done.2.quad_got_ref
  25.1 3.5 %last.1 = (f32[48,512]{1,0:T(8,128)}, f32[16,16]{1,0:T(8,128)}, f32[16,16]{1,0:T(8,128)}, f32[1,16]{1,0:T(1,128)}) custom-call(f32[56,512]{1,0:T(8,128)S(1)} %pack.1.own_ref, f32[48,512]{1,0:T(8,128)S(1)} %get-tuple-element.13.prod_ref, f32[48,512]{1,0:T(8,128)S(1)} %collective-permute-done.1.prod_got_ref, f32[48,256]{1,0:T(8,128)S(1)} %get-tuple-element.16.quad_ref, ...), custom_call_target="tpu_custom_call" | custom-call | tf_op jit(solution)/shard_map/last/pallas_call | solution.py:362
  (3 shorter events, 0.0 us)
Async XLA Ops:
  1.6 6.3 %collective-permute-start = (f32[56,512]{1,0:T(8,128)S(1)}, f32[56,512]{1,0:T(8,128)S(1)}, u32[]{:S(2)}, u32[]{:S(2)}) collective-permute-start(f32[56,512]{1,0:T(8,128)S(1)} %pack.1.own_ref), channel_id=1, source_target_pairs={{1,0},{5,1},{3,2},{7,3},{0,4},{9,5},{2,6},{11,7},{4,8},{13,9},{6,1... | collective-permute-start | bytes 344072 | tf_op jit(solution)/shard_map/ppermute | solution.py:311
  10.8 1.4 %collective-permute-start.1 = (f32[48,512]{1,0:T(8,128)S(1)}, f32[48,512]{1,0:T(8,128)S(1)}, u32[]{:S(2)}, u32[]{:S(2)}) collective-permute-start(f32[48,512]{1,0:T(8,128)S(1)} %get-tuple-element.13.prod_ref), channel_id=1, source_target_pairs={{0,1},{1,0},{2,3},{3,2},{4,5},{5,4},{6,7},{7,6},{8,9},{9,8},{10,11... | collective-permute-start | bytes 294920 | tf_op jit(solution)/shard_map/ppermute | solution.py:314
  13.2 1.2 %collective-permute-start.3 = (f32[16,128]{1,0:T(8,128)S(1)}, f32[16,128]{1,0:T(8,128)S(1)}, u32[]{:S(2)}, u32[]{:S(2)}) collective-permute-start(f32[16,128]{1,0:T(8,128)S(1)} %get-tuple-element.17), channel_id=1, source_target_pairs={{0,1},{1,0},{2,3},{3,2},{4,5},{5,4},{6,7},{7,6},{8,9},{9,8},{10,11... | collective-permute-start | bytes 24584 | tf_op jit(solution)/shard_map/ppermute | solution.py:314
  14.4 4.6 %collective-permute-start.6 = (f32[16,128]{1,0:T(8,128)S(1)}, f32[16,128]{1,0:T(8,128)S(1)}, u32[]{:S(2)}, u32[]{:S(2)}) collective-permute-start(f32[16,128]{1,0:T(8,128)S(1)} %add.15), channel_id=1, source_target_pairs={{0,13},{1,12},{2,15},{3,14},{4,9},{5,8},{6,11},{7,10},{8,5},{9,4},... | collective-permute-start | bytes 24584 | tf_op jit(solution)/shard_map/ppermute | solution.py:351
  17.6 3.1 %collective-permute-start.5 = (f32[16,128]{1,0:T(8,128)S(1)}, f32[16,128]{1,0:T(8,128)S(1)}, u32[]{:S(2)}, u32[]{:S(2)}) collective-permute-start(f32[16,128]{1,0:T(8,128)S(1)} %add.15), channel_id=1, source_target_pairs={{0,9},{1,8},{2,11},{3,10},{4,13},{5,12},{6,15},{7,14},{8,1},{9,0},... | collective-permute-start | bytes 24584 | tf_op jit(solution)/shard_map/ppermute | solution.py:351
  18.0 3.1 %collective-permute-start.4 = (f32[16,128]{1,0:T(8,128)S(1)}, f32[16,128]{1,0:T(8,128)S(1)}, u32[]{:S(2)}, u32[]{:S(2)}) collective-permute-start(f32[16,128]{1,0:T(8,128)S(1)} %add.15), channel_id=1, source_target_pairs={{0,5},{1,4},{2,7},{3,6},{4,1},{5,0},{6,3},{7,2},{8,13},{9,12},{10,... | collective-permute-start | bytes 24584 | tf_op jit(solution)/shard_map/ppermute | solution.py:351
  18.1 6.9 %collective-permute-start.2 = (f32[48,256]{1,0:T(8,128)S(1)}, f32[48,256]{1,0:T(8,128)S(1)}, u32[]{:S(2)}, u32[]{:S(2)}) collective-permute-start(f32[48,256]{1,0:T(8,128)S(1)} %get-tuple-element.16.quad_ref), channel_id=1, source_target_pairs={{0,1},{1,0},{2,3},{3,2},{4,5},{5,4},{6,7},{7,6},{8,9},{9,8},{10,11... | collective-permute-start | bytes 147464 | tf_op jit(solution)/shard_map/ppermute | solution.py:314
  21.1 4.0 %collective-permute-start.7 = (f32[16,128]{1,0:T(8,128)S(1)}, f32[16,128]{1,0:T(8,128)S(1)}, u32[]{:S(2)}, u32[]{:S(2)}) collective-permute-start(f32[16,128]{1,0:T(8,128)S(1)} %add_add_fusion), channel_id=1, source_target_pairs={{0,17},{1,16},{2,19},{3,18},{4,21},{5,20},{6,23},{7,22},{8,25},{9,... | collective-permute-start | bytes 24584 | tf_op jit(solution)/shard_map/ppermute | solution.py:351

commit v3 on v2

--- a/solution.py
+++ b/solution.py
@@ -73,36 +73,37 @@
     return jnp.where((row_of > 3) & missing, 0.0, block)
 
 
-def store_places(pos, pos_t, block, base):
-    place = lanes(base, block.shape[1])
-    pos[:, place] = block
-    if pos_t is not None:
-        pos_t[place, :] = jnp.transpose(block)
+def spread_places(pos, wide):
+    high, middle = split(pos[...])
+    low = (pos[...] - high.astype(f32) - middle.astype(f32)).astype(bf16)
+    parts = jnp.concatenate([x.astype(f32) for x in (high, middle, low)], axis=0).astype(bf16)
+    part_of = lax.broadcasted_iota(jnp.int32, (parts.shape[0], 3 * TILE_B), 0) % 8
+    lane_of = lax.broadcasted_iota(jnp.int32, (parts.shape[0], 3 * TILE_B), 1) // TILE_B
+    pick = jnp.where(part_of == lane_of, 1.0, 0.0).astype(bf16)
+    wide[...] = lax.dot_general(parts, pick, (((0,), (0,)), ((), ())), preferred_element_type=f32)
 
 
 def tile_slice(w):
     return slice(w * TILE_B, (w + 1) * TILE_B)
 
 
-def fill_pulls(pos, pos_t, pull_high, pull_low, r, w):
+def fill_pulls(pos, wide, pull, r, w):
     across = pos[:, tile_slice(w)]
     for j in range(w - REACH, w + REACH + 1):
         first, reach = min(j, w), abs(w - j)
         bound = pos[4 + reach : 5 + reach, tile_slice(first)]
         for q in range(0, TILE_B, CHUNK):
-            down = pos_t[j * TILE_B + q : j * TILE_B + q + CHUNK, :]
-            offset = [down[:, c : c + 1] - across[c : c + 1, :] for c in range(3)]
+            down = slice(j * TILE_B + q, j * TILE_B + q + CHUNK)
+            offset = [wide[down, tile_slice(c)] - across[c : c + 1, :] for c in range(3)]
             dist_sq = offset[0] * offset[0] + offset[1] * offset[1] + offset[2] * offset[2]
             falloff = jnp.maximum(bound - dist_sq, 0.0)
             weight = falloff * falloff / jnp.maximum(dist_sq, 1.0)
             place = slice((j - w + REACH) * TILE_B + q, (j - w + REACH) * TILE_B + q + CHUNK)
             for c in range(3):
-                high, low = split(weight * offset[c])
-                pull_high[r, place, tile_slice(c)] = high
-                pull_low[r, place, tile_slice(c)] = low
-
-
-def apply_pulls(vec, high, low, pos, pull_high, pull_low, w):
+                pull[r, place, tile_slice(c)] = (weight * offset[c]).astype(bf16)
+
+
+def apply_pulls(vec, high, low, pos, pull, w):
     rows = vec.shape[0]
     cols = rows // 3
     near = slice((w - REACH) * TILE_B, (w + REACH + 1) * TILE_B)
@@ -117,9 +118,8 @@
     left_low = jnp.concatenate([low[:, near], more_low], axis=0)
     left = jnp.concatenate([left_high, left_low], axis=0)
     n = left_high.shape[0]
-    with_high = jnp.dot(left, pull_high, preferred_element_type=f32)
-    with_low = jnp.dot(left_high, pull_low, preferred_element_type=f32)
-    total = with_high[0:n] + (with_high[n:] + with_low)
+    total = jnp.dot(left, pull, preferred_element_type=f32)
+    total = total[0:n] + total[n:]
     mine = [place[d : d + 1, REACH * TILE_B : (REACH + 1) * TILE_B] for d in range(3)]
     out = []
     for c in range(3):
@@ -133,35 +133,34 @@
     return jnp.concatenate(out, axis=0)
 
 
-def first_kernel(own_ref, got_ref, out_ref, pull_high, pull_low, vec, high, low, pos, pos_t):
+def first_kernel(own_ref, got_ref, out_ref, pull, vec, high, low, pos, wide):
     rows, width = out_ref.shape
     odd = parity()
     store_vectors(vec, high, low, own_ref[0:rows, :], (1 - odd) * width)
     store_vectors(vec, high, low, got_ref[0:rows, :], odd * width)
-    store_places(pos, pos_t, own_ref[rows : rows + 8, :], (1 - odd) * width)
-    store_places(pos, pos_t, received_places(got_ref[rows : rows + 8, :]), odd * width)
+    pos[:, lanes((1 - odd) * width, width)] = own_ref[rows : rows + 8, :]
+    pos[:, lanes(odd * width, width)] = received_places(got_ref[rows : rows + 8, :])
+    spread_places(pos, wide)
     for r in range(width // TILE_B):
         w = REACH + r
-        fill_pulls(pos, pos_t, pull_high, pull_low, r, w)
-        out_ref[:, tile_slice(r)] = apply_pulls(vec, high, low, pos, pull_high[r], pull_low[r], w)
+        fill_pulls(pos, wide, pull, r, w)
+        out_ref[:, tile_slice(r)] = apply_pulls(vec, high, low, pos, pull[r], w)
 
 
 def second_kernel(
-    own_ref, got_ref, prod_ref, prod_got_ref, pull_high, pull_low, out_ref, gram_ref, vec, high, low, pos
+    own_ref, got_ref, prod_ref, prod_got_ref, pull, out_ref, gram_ref, vec, high, low, pos
 ):
     rows, width = prod_ref.shape
     cols = rows // 3
     half = width // 2
     odd = parity()
-    store_places(pos, None, own_ref[rows : rows + 8, :], (1 - odd) * half)
-    store_places(pos, None, got_ref[rows : rows + 8, lanes((1 - odd) * half, half)], odd * width)
+    pos[:, lanes((1 - odd) * half, width)] = own_ref[rows : rows + 8, :]
+    pos[:, lanes(odd * width, half)] = got_ref[rows : rows + 8, lanes((1 - odd) * half, half)]
     store_vectors(vec, high, low, prod_ref[...], odd * half)
     store_vectors(vec, high, low, prod_got_ref[:, lanes(odd * half, half)], (1 - odd) * width)
     for r in range(REACH):
         from_first = r + (1 - odd) * REACH
-        out_ref[:, tile_slice(r)] = apply_pulls(
-            vec, high, low, pos, pull_high[from_first], pull_low[from_first], REACH + r
-        )
+        out_ref[:, tile_slice(r)] = apply_pulls(vec, high, low, pos, pull[from_first], REACH + r)
     gram = jnp.zeros((rows, rows), f32)
     for d in range(3):
         band = slice(d * cols, (d + 1) * cols)
@@ -169,34 +168,34 @@
             [own_ref[band, lanes(odd * half, half)], vec[band, half:width], out_ref[band, :]], axis=0
         )
         gram += lax.dot_general(joint, joint, (((1,), (1,)), ((), ())), precision=highest, preferred_element_type=f32)
-    block = [[gram[a * cols : (a + 1) * cols, b * cols : (b + 1) * cols] for b in range(3)] for a in range(3)]
     gram_ref[...] = jnp.zeros(gram_ref.shape, f32)
-    for n, part in enumerate((block[0][0], block[0][1], block[1][1], block[1][2], block[2][2])):
-        gram_ref[:, n * cols : (n + 1) * cols] = part
-
-
-def solve(matrix, rhs):
-    n = matrix.shape[0]
-    joint = jnp.concatenate([matrix, rhs], axis=1)
+    gram_ref[:, 0:rows] = gram[0:cols]
+    gram_ref[:, rows : 2 * rows] = gram[cols : 2 * cols]
+    gram_ref[:, 2 * rows : 2 * rows + cols] = gram[2 * cols :, 2 * cols :]
+
+
+def eliminate(joint, n):
     row_of = lax.broadcasted_iota(jnp.int32, joint.shape, 0)
-    for k in range(0, n, 2):
-        col = [jnp.broadcast_to(joint[:, k + i : k + i + 1], joint.shape) for i in range(2)]
-        row = [joint[k + i : k + i + 1, :] for i in range(2)]
-        inverse = 1.0 / col[0][k : k + 1]
-        ratio = col[0][k + 1 : k + 2] * inverse
-        lower = (row[1] - ratio * row[0]) / (col[1][k + 1 : k + 2] - ratio * col[1][k : k + 1])
-        upper = (row[0] - col[1][k : k + 1] * lower) * inverse
-        joint = joint - col[0] * upper - col[1] * lower
-        joint = jnp.where(row_of == k, upper, jnp.where(row_of == k + 1, lower, joint))
-    return joint[:, n:]
+    col = [jnp.broadcast_to(joint[:, j : j + 1], joint.shape) for j in range(n)]
+    for k in range(n):
+        inverse = 1.0 / col[k][k : k + 1]
+        here = row_of == k
+        factor = jnp.where(here, -1.0, col[k])
+        joint = jnp.where(here, 0.0, joint) - factor * (joint[k : k + 1] * inverse)
+        for j in range(k + 1, n):
+            col[j] = jnp.where(here, 0.0, col[j]) - factor * (col[j][k : k + 1] * inverse)
+    return joint
 
 
 def mul(a, b):
     return jnp.dot(a, b, precision=highest, preferred_element_type=f32)
 
 
-def mul_t(a, b):
-    return lax.dot_general(a, b, (((0,), (0,)), ((), ())), precision=highest, preferred_element_type=f32)
+def turned(high, both, vec):
+    vec_high, vec_low = split(vec)
+    n = high.shape[1]
+    first = lax.dot_general(both, vec_high, (((0,), (0,)), ((), ())), preferred_element_type=f32)
+    return first[0:n] + (first[n:] + lax.dot_general(high, vec_low, (((0,), (0,)), ((), ())), preferred_element_type=f32))
 
 
 def last_kernel(
@@ -221,16 +220,21 @@
     cols = rows // 3
     half = width // 2
     odd = parity()
-    xx, xp, pp, pq, qq = [gram_ref[:, n * cols : (n + 1) * cols] for n in range(5)]
     row_of = lax.broadcasted_iota(jnp.int32, (cols, cols), 0)
     col_of = lax.broadcasted_iota(jnp.int32, (cols, cols), 1)
     eye = jnp.where(row_of == col_of, 1.0, 0.0).astype(f32)
-    shift = solve(xx, xp)
-    rest = pp - mul_t(xp, shift)
+    xx, xp = gram_ref[:, 0:cols], gram_ref[:, cols : 2 * cols]
+    pp, pq = gram_ref[:, rows + cols : rows + 2 * cols], gram_ref[:, rows + 2 * cols : 2 * rows]
+    qq = gram_ref[:, 2 * rows : 2 * rows + cols]
+    joint = eliminate(jnp.concatenate([gram_ref[:, 0:rows], gram_ref[:, rows : 2 * rows]], axis=0), cols)
+    shift = joint[0:cols, cols : 2 * cols]
+    rest = joint[cols:, cols : 2 * cols]
+    cross = joint[cols:, 2 * cols :]
     corr = xx + rest
-    gram = xp - 2.0 * rest + pq - mul_t(shift, pp) - mul(rest, shift)
-    second = solve(corr, gram)
-    both = shift + second
+    side = xp - 2.0 * rest + cross
+    both = eliminate(jnp.concatenate([corr, side + xp], axis=1), cols)[:, cols:]
+    second = both - shift
+    gram = side - mul(rest, shift)
     turn = eye + shift
     squares = turn * (mul(pp, turn) - 2.0 * pq) + eye * qq - gram * second
     ray[...] = gram * (bead_scale / step_size)
@@ -241,24 +245,24 @@
         pltpu.make_async_copy(small, corr_ref, sems.at[1]),
         pltpu.make_async_copy(norm, norm_ref, sems.at[2]),
     ]
-    factor = jnp.concatenate([both + mul(shift, second), -both], axis=0)
-    factor_high, factor_low = split(factor)
-    factor = jnp.concatenate([factor_high, factor_low], axis=1)
+    shift_high, shift_low = split(shift)
+    shift_both = jnp.concatenate([shift_high, shift_low], axis=1)
+    factor_high, factor_low = split(jnp.concatenate([both, second], axis=0))
+    factor_both = jnp.concatenate([factor_high, factor_low], axis=1)
     for d in range(3):
         band = slice(d * cols, (d + 1) * cols)
         prod, quad = [], []
-        for side in range(2):
-            away = slice((1 - side) * half, (2 - side) * half)
-            mine = odd == side
+        for part in range(2):
+            away = slice((1 - part) * half, (2 - part) * half)
+            mine = odd == part
             prod.append(jnp.where(mine, prod_ref[band, away], prod_got_ref[band, away]))
             quad.append(jnp.where(mine, quad_ref[band, :], quad_got_ref[band, :]))
         vec = own_ref[band, :]
         prod = jnp.concatenate(prod, axis=1)
         quad = jnp.concatenate(quad, axis=1)
-        high, low = split(jnp.concatenate([vec, prod], axis=0))
-        turned = lax.dot_general(factor, high, (((0,), (0,)), ((), ())), preferred_element_type=f32)
-        small_turned = lax.dot_general(factor_high, low, (((0,), (0,)), ((), ())), preferred_element_type=f32)
-        out[band, :] = vec - 2.0 * prod + quad + (turned[0:cols] + (turned[cols:] + small_turned))
+        moved = turned(shift_high, shift_both, vec)
+        base = vec - 2.0 * prod + quad
+        out[band, :] = base + turned(factor_high, factor_both, jnp.concatenate([vec - prod, moved], axis=0))
         copies.append(pltpu.make_async_copy(out.at[band], out_ref.at[band], sems.at[3 + d]))
         if d == 0:
             for copy in copies:
@@ -322,12 +326,12 @@
         ]
 
     pulls = jax.ShapeDtypeStruct((tiles, (2 * REACH + 1) * TILE_B, 3 * TILE_B), bf16)
-    prod, pull_high, pull_low = pl.pallas_call(
+    prod, pull = pl.pallas_call(
         first_kernel,
-        out_shape=(jax.ShapeDtypeStruct((rows, width), f32), pulls, pulls),
+        out_shape=(jax.ShapeDtypeStruct((rows, width), f32), pulls),
         in_specs=[vmem] * 2,
-        out_specs=(vmem,) * 3,
-        scratch_shapes=scratch(2 * width) + [pltpu.VMEM((2 * width, 8), f32)],
+        out_specs=(vmem,) * 2,
+        scratch_shapes=scratch(2 * width) + [pltpu.VMEM((2 * width, 3 * TILE_B), f32)],
         compiler_params=params,
         name="first",
     )(own, got)
@@ -335,12 +339,12 @@
     quad, gram = pl.pallas_call(
         second_kernel,
         out_shape=(jax.ShapeDtypeStruct((rows, half), f32), jax.ShapeDtypeStruct((cols, 128), f32)),
-        in_specs=[vmem] * 6,
+        in_specs=[vmem] * 5,
         out_specs=(vmem, vmem),
         scratch_shapes=scratch(width + half),
         compiler_params=params,
         name="second",
-    )(own, got, prod, prod_got, pull_high, pull_low)
+    )(own, got, prod, prod_got, pull)
     gram = gram + swapped(gram)
     quad_got = swapped(quad)
 

time: 28.7 us -> 25.8 us (0.90)
  Pallas kernels: 8.28 us -> 5.4 us
    pallas_call x1, Pallas kernels: 3.45 us -> 1.91 us  [per_device(): pl.pallas_call(functools.partial(last_kernel, bead_scale), out_shape=tupl...]
    pallas_call x1, Pallas kernels: 2.89 us -> 1.67 us  [per_device(): pl.pallas_call(first_kernel, out_shape=(jax.ShapeDtypeStruct((rows, width...]
where the time goes in v3:
time: 25.8 us; the launch traced here: 25.7 us
  waiting for transfers between devices  10 us (39%)
  starting transfers between devices  9.57 us (37%)
  Pallas kernels  5.4 us (21%)
  between operations  0.66 us (3%)
    ppermute x4, starting transfers between devices, crossed(): return lax.ppermute(x, ('tile', 'col'), route)  6.14 us
    ppermute x4, waiting for transfers between devices, crossed(): return lax.ppermute(x, ('tile', 'col'), route)  4.41 us
    ppermute x1, waiting for transfers between devices, per_device(): got = lax.ppermute(own, ('tile', 'col'), halo)  3.3 us
    ppermute x1, starting transfers between devices, per_device(): got = lax.ppermute(own, ('tile', 'col'), halo)  3.02 us
    ppermute x3, waiting for transfers between devices, swapped(): return lax.ppermute(x, 'col', [(c, c ^ 1) for c in range(n_col)])  2.31 us
    pallas_call x1, Pallas kernels, per_device(): pl.pallas_call(functools.partial(last_kernel, bead_scale), out_shape=tupl...  1.91 us
    pallas_call x1, Pallas kernels, per_device(): pl.pallas_call(first_kernel, out_shape=(jax.ShapeDtypeStruct((rows, width...  1.67 us
    pallas_call x1, Pallas kernels, per_device(): pl.pallas_call(pack_kernel, out_shape=jax.ShapeDtypeStruct((rows + 8, wid...  0.95 us
  transfers between devices with their start and end apart: 8, of which 7 were waited for; matrix products, arithmetic and copies ran while one was open for 0% of the time, Pallas kernels for 0%

profile of v3, /device:TPU:0, one launch (start us, length us, event | category | flops | bytes accessed | tf_op | source)
XLA Modules:
  0.0 25.7 jit_solution(6617321083571427768)
XLA Ops:
  0.6 0.9 %pack.1.own_ref = f32[56,512]{1,0:T(8,128)S(1)} custom-call(f32[48,512]{1,0:T(8,128)} %bitcast.3, f32[3,512]{1,0:T(4,128)} %pos_ref.1, s32[2,1,4,8]{3,2,1,0:T(4,128)} %tiles_ref.1, s32[1,4]{1,0:T(1,128)} %count_ref.1), custom_call_target="tpu_custom_call" | custom-call | tf_op jit(solution)/shard_map/pack/pallas_call | solution.py:289
  1.6 3.0 %collective-permute-start = (f32[56,512]{1,0:T(8,128)S(1)}, f32[56,512]{1,0:T(8,128)S(1)}, u32[]{:S(2)}, u32[]{:S(2)}) collective-permute-start(f32[56,512]{1,0:T(8,128)S(1)} %pack.1.own_ref), channel_id=1, source_target_pairs={{1,0},{5,1},{3,2},{7,3},{0,4},{9,5},{2,6},{11,7},{4,8},{13,9},{6,1... | collective-permute-start | bytes 344072 | tf_op jit(solution)/shard_map/ppermute | solution.py:315
  4.6 3.3 %collective-permute-done.got_ref = f32[56,512]{1,0:T(8,128)S(1)} collective-permute-done((f32[56,512]{1,0:T(8,128)S(1)}, f32[56,512]{1,0:T(8,128)S(1)}, u32[]{:S(2)}, u32[]{:S(2)}) %collective-permute-start) | collective-permute-done | bytes 114720 | tf_op jit(solution)/shard_map/ppermute | solution.py:315
  7.9 1.7 %first.1 = (f32[48,512]{1,0:T(8,128)S(1)}, bf16[4,640,384]{2,1,0:T(8,128)(2,1)S(1)}) custom-call(f32[56,512]{1,0:T(8,128)S(1)} %pack.1.own_ref, f32[56,512]{1,0:T(8,128)S(1)} %collective-permute-done.got_ref), custom_call_target="tpu_custom_call" | custom-call | tf_op jit(solution)/shard_map/first/pallas_call | solution.py:329
  9.6 0.1 collective-permute-start.1
  9.7 1.3 %collective-permute-done.1.prod_got_ref = f32[48,512]{1,0:T(8,128)S(1)} collective-permute-done((f32[48,512]{1,0:T(8,128)S(1)}, f32[48,512]{1,0:T(8,128)S(1)}, u32[]{:S(2)}, u32[]{:S(2)}) %collective-permute-start.1) | collective-permute-done | bytes 98336 | tf_op jit(solution)/shard_map/ppermute | solution.py:318
  11.0 0.9 %second.1 = (f32[48,256]{1,0:T(8,128)S(1)}, f32[16,128]{1,0:T(8,128)S(1)}) custom-call(f32[56,512]{1,0:T(8,128)S(1)} %pack.1.own_ref, f32[56,512]{1,0:T(8,128)S(1)} %collective-permute-done.got_ref, f32[48,512]{1,0:T(8,128)S(1)} %get-tuple-element.12.prod_ref, f32[48,512]{1,0:T(8,128)S(1)} %collective-permute-done.1.prod_got_ref, ...), custom_call_target="tpu_custom_call" | custom-call | tf_op jit(solution)/shard_map/second/pallas_call | solution.py:339
  11.8 0.2 collective-permute-start.3
  12.0 1.0 %collective-permute-done.3 = f32[16,128]{1,0:T(8,128)S(1)} collective-permute-done((f32[16,128]{1,0:T(8,128)S(1)}, f32[16,128]{1,0:T(8,128)S(1)}, u32[]{:S(2)}, u32[]{:S(2)}) %collective-permute-start.3) | collective-permute-done | bytes 8224 | tf_op jit(solution)/shard_map/ppermute | solution.py:318
  13.0 3.3 %collective-permute-start.6 = (f32[16,128]{1,0:T(8,128)S(1)}, f32[16,128]{1,0:T(8,128)S(1)}, u32[]{:S(2)}, u32[]{:S(2)}) collective-permute-start(f32[16,128]{1,0:T(8,128)S(1)} %add.15), channel_id=1, source_target_pairs={{0,13},{1,12},{2,15},{3,14},{4,9},{5,8},{6,11},{7,10},{8,5},{9,4},... | collective-permute-start | bytes 24584 | tf_op jit(solution)/shard_map/ppermute | solution.py:355
  16.3 0.4 %collective-permute-start.5 = (f32[16,128]{1,0:T(8,128)S(1)}, f32[16,128]{1,0:T(8,128)S(1)}, u32[]{:S(2)}, u32[]{:S(2)}) collective-permute-start(f32[16,128]{1,0:T(8,128)S(1)} %add.15), channel_id=1, source_target_pairs={{0,9},{1,8},{2,11},{3,10},{4,13},{5,12},{6,15},{7,14},{8,1},{9,0},... | collective-permute-start | bytes 24584 | tf_op jit(solution)/shard_map/ppermute | solution.py:355
  16.7 0.1 collective-permute-start.4
  16.8 0.2 collective-permute-start.2
  17.0 0.7 %collective-permute-done.6 = f32[16,128]{1,0:T(8,128)S(1)} collective-permute-done((f32[16,128]{1,0:T(8,128)S(1)}, f32[16,128]{1,0:T(8,128)S(1)}, u32[]{:S(2)}, u32[]{:S(2)}) %collective-permute-start.6) | collective-permute-done | bytes 8224 | tf_op jit(solution)/shard_map/ppermute | solution.py:355
  17.7 1.7 %collective-permute-done.5 = f32[16,128]{1,0:T(8,128)S(1)} collective-permute-done((f32[16,128]{1,0:T(8,128)S(1)}, f32[16,128]{1,0:T(8,128)S(1)}, u32[]{:S(2)}, u32[]{:S(2)}) %collective-permute-start.5) | collective-permute-done | bytes 8224 | tf_op jit(solution)/shard_map/ppermute | solution.py:355
  19.4 0.4 %collective-permute-done.4 = f32[16,128]{1,0:T(8,128)S(1)} collective-permute-done((f32[16,128]{1,0:T(8,128)S(1)}, f32[16,128]{1,0:T(8,128)S(1)}, u32[]{:S(2)}, u32[]{:S(2)}) %collective-permute-start.4) | collective-permute-done | bytes 8224 | tf_op jit(solution)/shard_map/ppermute | solution.py:355
  19.8 2.4 %collective-permute-start.7 = (f32[16,128]{1,0:T(8,128)S(1)}, f32[16,128]{1,0:T(8,128)S(1)}, u32[]{:S(2)}, u32[]{:S(2)}) collective-permute-start(f32[16,128]{1,0:T(8,128)S(1)} %add_add_fusion), channel_id=1, source_target_pairs={{0,17},{1,16},{2,19},{3,18},{4,21},{5,20},{6,23},{7,22},{8,25},{9,... | collective-permute-start | bytes 24584 | tf_op jit(solution)/shard_map/ppermute | solution.py:355
  22.1 1.6 %collective-permute-done.7 = f32[16,128]{1,0:T(8,128)S(1)} collective-permute-done((f32[16,128]{1,0:T(8,128)S(1)}, f32[16,128]{1,0:T(8,128)S(1)}, u32[]{:S(2)}, u32[]{:S(2)}) %collective-permute-start.7) | collective-permute-done | bytes 8224 | tf_op jit(solution)/shard_map/ppermute | solution.py:355
  23.7 0.0 collective-permute-done.2.quad_got_ref
  23.7 1.9 %last.1 = (f32[48,512]{1,0:T(8,128)}, f32[16,16]{1,0:T(8,128)}, f32[16,16]{1,0:T(8,128)}, f32[1,16]{1,0:T(1,128)}) custom-call(f32[56,512]{1,0:T(8,128)S(1)} %pack.1.own_ref, f32[48,512]{1,0:T(8,128)S(1)} %get-tuple-element.12.prod_ref, f32[48,512]{1,0:T(8,128)S(1)} %collective-permute-done.1.prod_got_ref, f32[48,256]{1,0:T(8,128)S(1)} %get-tuple-element.14.quad_ref, ...), custom_call_target="tpu_custom_call" | custom-call | tf_op jit(solution)/shard_map/last/pallas_call | solution.py:366
  (3 shorter events, 0.0 us)
Async XLA Ops:
  1.6 6.3 %collective-permute-start = (f32[56,512]{1,0:T(8,128)S(1)}, f32[56,512]{1,0:T(8,128)S(1)}, u32[]{:S(2)}, u32[]{:S(2)}) collective-permute-start(f32[56,512]{1,0:T(8,128)S(1)} %pack.1.own_ref), channel_id=1, source_target_pairs={{1,0},{5,1},{3,2},{7,3},{0,4},{9,5},{2,6},{11,7},{4,8},{13,9},{6,1... | collective-permute-start | bytes 344072 | tf_op jit(solution)/shard_map/ppermute | solution.py:315
  9.6 1.4 %collective-permute-start.1 = (f32[48,512]{1,0:T(8,128)S(1)}, f32[48,512]{1,0:T(8,128)S(1)}, u32[]{:S(2)}, u32[]{:S(2)}) collective-permute-start(f32[48,512]{1,0:T(8,128)S(1)} %get-tuple-element.12.prod_ref), channel_id=1, source_target_pairs={{0,1},{1,0},{2,3},{3,2},{4,5},{5,4},{6,7},{7,6},{8,9},{9,8},{10,11... | collective-permute-start | bytes 294920 | tf_op jit(solution)/shard_map/ppermute | solution.py:318
  11.8 1.2 %collective-permute-start.3 = (f32[16,128]{1,0:T(8,128)S(1)}, f32[16,128]{1,0:T(8,128)S(1)}, u32[]{:S(2)}, u32[]{:S(2)}) collective-permute-start(f32[16,128]{1,0:T(8,128)S(1)} %get-tuple-element.15), channel_id=1, source_target_pairs={{0,1},{1,0},{2,3},{3,2},{4,5},{5,4},{6,7},{7,6},{8,9},{9,8},{10,11... | collective-permute-start | bytes 24584 | tf_op jit(solution)/shard_map/ppermute | solution.py:318
  13.0 4.6 %collective-permute-start.6 = (f32[16,128]{1,0:T(8,128)S(1)}, f32[16,128]{1,0:T(8,128)S(1)}, u32[]{:S(2)}, u32[]{:S(2)}) collective-permute-start(f32[16,128]{1,0:T(8,128)S(1)} %add.15), channel_id=1, source_target_pairs={{0,13},{1,12},{2,15},{3,14},{4,9},{5,8},{6,11},{7,10},{8,5},{9,4},... | collective-permute-start | bytes 24584 | tf_op jit(solution)/shard_map/ppermute | solution.py:355
  16.3 3.1 %collective-permute-start.5 = (f32[16,128]{1,0:T(8,128)S(1)}, f32[16,128]{1,0:T(8,128)S(1)}, u32[]{:S(2)}, u32[]{:S(2)}) collective-permute-start(f32[16,128]{1,0:T(8,128)S(1)} %add.15), channel_id=1, source_target_pairs={{0,9},{1,8},{2,11},{3,10},{4,13},{5,12},{6,15},{7,14},{8,1},{9,0},... | collective-permute-start | bytes 24584 | tf_op jit(solution)/shard_map/ppermute | solution.py:355
  16.7 3.1 %collective-permute-start.4 = (f32[16,128]{1,0:T(8,128)S(1)}, f32[16,128]{1,0:T(8,128)S(1)}, u32[]{:S(2)}, u32[]{:S(2)}) collective-permute-start(f32[16,128]{1,0:T(8,128)S(1)} %add.15), channel_id=1, source_target_pairs={{0,5},{1,4},{2,7},{3,6},{4,1},{5,0},{6,3},{7,2},{8,13},{9,12},{10,... | collective-permute-start | bytes 24584 | tf_op jit(solution)/shard_map/ppermute | solution.py:355
  16.8 6.9 %collective-permute-start.2 = (f32[48,256]{1,0:T(8,128)S(1)}, f32[48,256]{1,0:T(8,128)S(1)}, u32[]{:S(2)}, u32[]{:S(2)}) collective-permute-start(f32[48,256]{1,0:T(8,128)S(1)} %get-tuple-element.14.quad_ref), channel_id=1, source_target_pairs={{0,1},{1,0},{2,3},{3,2},{4,5},{5,4},{6,7},{7,6},{8,9},{9,8},{10,11... | collective-permute-start | bytes 147464 | tf_op jit(solution)/shard_map/ppermute | solution.py:318
  19.8 4.0 %collective-permute-start.7 = (f32[16,128]{1,0:T(8,128)S(1)}, f32[16,128]{1,0:T(8,128)S(1)}, u32[]{:S(2)}, u32[]{:S(2)}) collective-permute-start(f32[16,128]{1,0:T(8,128)S(1)} %add_add_fusion), channel_id=1, source_target_pairs={{0,17},{1,16},{2,19},{3,18},{4,21},{5,20},{6,23},{7,22},{8,25},{9,... | collective-permute-start | bytes 24584 | tf_op jit(solution)/shard_map/ppermute | solution.py:355

commit v4 on v3

--- a/solution.py
+++ b/solution.py
@@ -20,11 +20,7 @@
 
 
 def parity():
-    return lax.rem(lax.axis_index("col"), 2)
-
-
-def lanes(start, size):
-    return pl.ds(pl.multiple_of(start, TILE_B), size)
+    return lax.rem(lax.axis_index("col") + lax.axis_index("tile") + 1, 2)
 
 
 def pack_kernel(vec_ref, pos_ref, tiles_ref, count_ref, out_ref, tiles, count, pos, sems):
@@ -60,8 +56,7 @@
     return high, (x - high.astype(f32)).astype(bf16)
 
 
-def store_vectors(vec, high, low, x, base):
-    place = lanes(base, x.shape[1])
+def store_vectors(vec, high, low, x, place):
     vec[:, place] = x
     high[:, place], low[:, place] = split(x)
 
@@ -73,34 +68,41 @@
     return jnp.where((row_of > 3) & missing, 0.0, block)
 
 
-def spread_places(pos, wide):
-    high, middle = split(pos[...])
-    low = (pos[...] - high.astype(f32) - middle.astype(f32)).astype(bf16)
+def spread_places(places):
+    high, middle = split(places)
+    low = (places - high.astype(f32) - middle.astype(f32)).astype(bf16)
     parts = jnp.concatenate([x.astype(f32) for x in (high, middle, low)], axis=0).astype(bf16)
     part_of = lax.broadcasted_iota(jnp.int32, (parts.shape[0], 3 * TILE_B), 0) % 8
     lane_of = lax.broadcasted_iota(jnp.int32, (parts.shape[0], 3 * TILE_B), 1) // TILE_B
     pick = jnp.where(part_of == lane_of, 1.0, 0.0).astype(bf16)
-    wide[...] = lax.dot_general(parts, pick, (((0,), (0,)), ((), ())), preferred_element_type=f32)
+    return lax.dot_general(parts, pick, (((0,), (0,)), ((), ())), preferred_element_type=f32)
 
 
 def tile_slice(w):
     return slice(w * TILE_B, (w + 1) * TILE_B)
 
 
-def fill_pulls(pos, wide, pull, r, w):
-    across = pos[:, tile_slice(w)]
-    for j in range(w - REACH, w + REACH + 1):
-        first, reach = min(j, w), abs(w - j)
-        bound = pos[4 + reach : 5 + reach, tile_slice(first)]
-        for q in range(0, TILE_B, CHUNK):
-            down = slice(j * TILE_B + q, j * TILE_B + q + CHUNK)
-            offset = [wide[down, tile_slice(c)] - across[c : c + 1, :] for c in range(3)]
-            dist_sq = offset[0] * offset[0] + offset[1] * offset[1] + offset[2] * offset[2]
-            falloff = jnp.maximum(bound - dist_sq, 0.0)
-            weight = falloff * falloff / jnp.maximum(dist_sq, 1.0)
-            place = slice((j - w + REACH) * TILE_B + q, (j - w + REACH) * TILE_B + q + CHUNK)
-            for c in range(3):
-                pull[r, place, tile_slice(c)] = (weight * offset[c]).astype(bf16)
+def fill_pull(across, bound, wide, wide_base, pull, row, m):
+    for q in range(0, TILE_B, CHUNK):
+        down = slice(wide_base + q, wide_base + q + CHUNK)
+        offset = [wide[down, tile_slice(c)] - across[c : c + 1, :] for c in range(3)]
+        dist_sq = offset[0] * offset[0] + offset[1] * offset[1] + offset[2] * offset[2]
+        falloff = jnp.maximum(bound - dist_sq, 0.0)
+        weight = falloff * falloff / jnp.maximum(dist_sq, 1.0)
+        place = slice(m * TILE_B + q, m * TILE_B + q + CHUNK)
+        for c in range(3):
+            pull[row, place, tile_slice(c)] = (weight * offset[c]).astype(bf16)
+
+
+def bound_of(pos, w, j):
+    reach = abs(w - j)
+    return pos[4 + reach : 5 + reach, tile_slice(min(w, j))]
+
+
+def by_parity(body):
+    odd = parity()
+    pl.when(odd == 0)(functools.partial(body, 0))
+    pl.when(odd == 1)(functools.partial(body, 1))
 
 
 def apply_pulls(vec, high, low, pos, pull, w):
@@ -133,39 +135,75 @@
     return jnp.concatenate(out, axis=0)
 
 
-def first_kernel(own_ref, got_ref, out_ref, pull, vec, high, low, pos, wide):
-    rows, width = out_ref.shape
-    odd = parity()
-    store_vectors(vec, high, low, own_ref[0:rows, :], (1 - odd) * width)
-    store_vectors(vec, high, low, got_ref[0:rows, :], odd * width)
-    pos[:, lanes((1 - odd) * width, width)] = own_ref[rows : rows + 8, :]
-    pos[:, lanes(odd * width, width)] = received_places(got_ref[rows : rows + 8, :])
-    spread_places(pos, wide)
-    for r in range(width // TILE_B):
-        w = REACH + r
-        fill_pulls(pos, wide, pull, r, w)
-        out_ref[:, tile_slice(r)] = apply_pulls(vec, high, low, pos, pull[r], w)
-
-
-def second_kernel(
-    own_ref, got_ref, prod_ref, prod_got_ref, pull, out_ref, gram_ref, vec, high, low, pos
-):
-    rows, width = prod_ref.shape
+def own_kernel(own_ref, pull, wide):
+    rows = own_ref.shape[0] - 8
+    tiles = own_ref.shape[1] // TILE_B
+    pos = own_ref.at[rows : rows + 8]
+    wide[...] = spread_places(pos[...])
+    for u in range(tiles):
+        for j in range(max(0, u - REACH), min(tiles, u + REACH + 1)):
+            fill_pull(pos[:, tile_slice(u)], bound_of(pos, u, j), wide, j * TILE_B, pull, u + REACH, j - u + REACH)
+
+
+def first_kernel(own_ref, got_ref, wide_own, pull_in, out_ref, pull, vec, high, low, pos, wide_got):
+    rows = vec.shape[0]
+    width = own_ref.shape[1]
+    tiles = width // TILE_B
+    places = received_places(got_ref[rows : rows + 8, :])
+    out_ref[rows : rows + 8, :] = places
+    wide_got[...] = spread_places(places)
+
+    def body(odd):
+        ours = slice((1 - odd) * width, (2 - odd) * width)
+        others = slice(odd * width, (1 + odd) * width)
+        store_vectors(vec, high, low, own_ref[0:rows, :], ours)
+        store_vectors(vec, high, low, got_ref[0:rows, :], others)
+        pos[:, ours] = own_ref[rows : rows + 8, :]
+        pos[:, others] = places
+        for r in range(tiles):
+            w = r + REACH
+            row = r + odd * tiles
+            for j in range(w - REACH, w + REACH + 1):
+                wide, base = (wide_got, odd) if j // tiles == odd else (wide_own, 1 - odd)
+                if wide is wide_got or w // tiles == odd:
+                    bound = bound_of(pos, w, j)
+                    fill_pull(pos[:, tile_slice(w)], bound, wide, (j - base * tiles) * TILE_B, pull, row, j - w + REACH)
+            out_ref[0:rows, tile_slice(r)] = apply_pulls(vec, high, low, pos, pull[row], w)
+
+    by_parity(body)
+
+
+def second_kernel(own_ref, prod_ref, prod_got_ref, pull_in, out_ref, mid_ref, gram_ref, pull, vec, high, low, pos, wide):
+    rows = vec.shape[0]
     cols = rows // 3
-    half = width // 2
-    odd = parity()
-    pos[:, lanes((1 - odd) * half, width)] = own_ref[rows : rows + 8, :]
-    pos[:, lanes(odd * width, half)] = got_ref[rows : rows + 8, lanes((1 - odd) * half, half)]
-    store_vectors(vec, high, low, prod_ref[...], odd * half)
-    store_vectors(vec, high, low, prod_got_ref[:, lanes(odd * half, half)], (1 - odd) * width)
-    for r in range(REACH):
-        from_first = r + (1 - odd) * REACH
-        out_ref[:, tile_slice(r)] = apply_pulls(vec, high, low, pos, pull[from_first], REACH + r)
+    width = own_ref.shape[1]
+    tiles = width // TILE_B
+    edge = REACH * TILE_B
+
+    def body(odd):
+        sides = prod_ref, prod_got_ref
+        pos[:, 0:edge] = sides[odd][rows : rows + 8, width - edge :]
+        pos[:, edge : edge + width] = own_ref[rows : rows + 8, :]
+        pos[:, edge + width :] = sides[1 - odd][rows : rows + 8, 0:edge]
+        store_vectors(vec, high, low, prod_ref[0:rows, :], slice(odd * width, (1 + odd) * width))
+        store_vectors(vec, high, low, prod_got_ref[0:rows, :], slice((1 - odd) * width, (2 - odd) * width))
+        start = (1 - odd) * (tiles + REACH)
+        wide[...] = spread_places(pos[:, start * TILE_B : start * TILE_B + edge])
+        half = tiles // 2
+        for w in range(REACH + (1 - odd) * half, REACH + (2 - odd) * half):
+            for j in range(max(start, w - REACH), min(start + REACH, w + REACH + 1)):
+                bound = bound_of(pos, w, j)
+                fill_pull(pos[:, tile_slice(w)], bound, wide, (j - start) * TILE_B, pull, w, j - w + REACH)
+
+    by_parity(body)
+    for u in range(tiles):
+        out_ref[:, tile_slice(u)] = apply_pulls(vec, high, low, pos, pull[u + REACH], u + REACH)
+    mid_ref[...] = vec[:, edge : edge + width]
     gram = jnp.zeros((rows, rows), f32)
     for d in range(3):
         band = slice(d * cols, (d + 1) * cols)
         joint = jnp.concatenate(
-            [own_ref[band, lanes(odd * half, half)], vec[band, half:width], out_ref[band, :]], axis=0
+            [own_ref[band, :], mid_ref[band, :], out_ref[band, :]], axis=0
         )
         gram += lax.dot_general(joint, joint, (((1,), (1,)), ((), ())), precision=highest, preferred_element_type=f32)
     gram_ref[...] = jnp.zeros(gram_ref.shape, f32)
@@ -202,9 +240,7 @@
     bead_scale,
     own_ref,
     prod_ref,
-    prod_got_ref,
     quad_ref,
-    quad_got_ref,
     gram_ref,
     out_ref,
     ray_ref,
@@ -218,8 +254,6 @@
 ):
     rows, width = prod_ref.shape
     cols = rows // 3
-    half = width // 2
-    odd = parity()
     row_of = lax.broadcasted_iota(jnp.int32, (cols, cols), 0)
     col_of = lax.broadcasted_iota(jnp.int32, (cols, cols), 1)
     eye = jnp.where(row_of == col_of, 1.0, 0.0).astype(f32)
@@ -251,17 +285,9 @@
     factor_both = jnp.concatenate([factor_high, factor_low], axis=1)
     for d in range(3):
         band = slice(d * cols, (d + 1) * cols)
-        prod, quad = [], []
-        for part in range(2):
-            away = slice((1 - part) * half, (2 - part) * half)
-            mine = odd == part
-            prod.append(jnp.where(mine, prod_ref[band, away], prod_got_ref[band, away]))
-            quad.append(jnp.where(mine, quad_ref[band, :], quad_got_ref[band, :]))
-        vec = own_ref[band, :]
-        prod = jnp.concatenate(prod, axis=1)
-        quad = jnp.concatenate(quad, axis=1)
+        vec, prod = own_ref[band, :], prod_ref[band, :]
         moved = turned(shift_high, shift_both, vec)
-        base = vec - 2.0 * prod + quad
+        base = vec - 2.0 * prod + quad_ref[band, :]
         out[band, :] = base + turned(factor_high, factor_both, jnp.concatenate([vec - prod, moved], axis=0))
         copies.append(pltpu.make_async_copy(out.at[band], out_ref.at[band], sems.at[3 + d]))
         if d == 0:
@@ -278,7 +304,6 @@
     rows = comps * cols
     n_tile, n_col = lax.axis_size("tile"), lax.axis_size("col")
     tiles = width // TILE_B
-    half = width // 2
     assert tiles == 2 * REACH and n_col % 2 == 0
     bead_scale = 1.0 / (3.0 * n_tile * width)
     vmem = pl.BlockSpec(memory_space=pltpu.VMEM)
@@ -307,15 +332,11 @@
     halo = []
     for t in range(n_tile):
         for c in range(n_col):
-            source = t - 1 if c % 2 == 0 else t + 1
-            if 0 <= source < n_tile:
-                halo.append((source * n_col + c, t * n_col + c))
-            else:
-                halo.append((t * n_col + (c ^ 1), t * n_col + c))
+            source = t - 1 if (c + t + 1) % 2 == 0 else t + 1
+            if not 0 <= source < n_tile:
+                source = t
+            halo.append((source * n_col + (c ^ 1), t * n_col + c))
     got = lax.ppermute(own, ("tile", "col"), halo)
-
-    def swapped(x):
-        return lax.ppermute(x, "col", [(c, c ^ 1) for c in range(n_col)])
 
     def scratch(window):
         return [
@@ -325,28 +346,38 @@
             pltpu.VMEM((8, window), f32),
         ]
 
-    pulls = jax.ShapeDtypeStruct((tiles, (2 * REACH + 1) * TILE_B, 3 * TILE_B), bf16)
+    pulls = jax.ShapeDtypeStruct((2 * tiles, (2 * REACH + 1) * TILE_B, 3 * TILE_B), bf16)
+    pull, wide = pl.pallas_call(
+        own_kernel,
+        out_shape=(pulls, jax.ShapeDtypeStruct((width, 3 * TILE_B), f32)),
+        in_specs=[vmem],
+        out_specs=(vmem,) * 2,
+        compiler_params=params,
+        cost_estimate=pl.CostEstimate(flops=10**8, bytes_accessed=10**6, transcendentals=0),
+        name="own_pulls",
+    )(own)
     prod, pull = pl.pallas_call(
         first_kernel,
-        out_shape=(jax.ShapeDtypeStruct((rows, width), f32), pulls),
-        in_specs=[vmem] * 2,
+        out_shape=(jax.ShapeDtypeStruct((rows + 8, width), f32), pulls),
+        in_specs=[vmem] * 4,
         out_specs=(vmem,) * 2,
-        scratch_shapes=scratch(2 * width) + [pltpu.VMEM((2 * width, 3 * TILE_B), f32)],
+        input_output_aliases={3: 1},
+        scratch_shapes=scratch(2 * width) + [pltpu.VMEM((width, 3 * TILE_B), f32)],
         compiler_params=params,
         name="first",
-    )(own, got)
-    prod_got = swapped(prod)
-    quad, gram = pl.pallas_call(
+    )(own, got, wide, pull)
+    prod_got = lax.ppermute(prod, "col", [(c, c ^ 1) for c in range(n_col)])
+    block_shape = jax.ShapeDtypeStruct((rows, width), f32)
+    quad, prod, gram, pull = pl.pallas_call(
         second_kernel,
-        out_shape=(jax.ShapeDtypeStruct((rows, half), f32), jax.ShapeDtypeStruct((cols, 128), f32)),
-        in_specs=[vmem] * 5,
-        out_specs=(vmem, vmem),
-        scratch_shapes=scratch(width + half),
+        out_shape=(block_shape, block_shape, jax.ShapeDtypeStruct((cols, 128), f32), pulls),
+        in_specs=[vmem] * 4,
+        out_specs=(vmem,) * 4,
+        input_output_aliases={3: 3},
+        scratch_shapes=scratch(2 * width) + [pltpu.VMEM((REACH * TILE_B, 3 * TILE_B), f32)],
         compiler_params=params,
         name="second",
-    )(own, got, prod, prod_got, pull)
-    gram = gram + swapped(gram)
-    quad_got = swapped(quad)
+    )(own, prod, prod_got, pull)
 
     def crossed(x, step):
         route = [
@@ -366,12 +397,12 @@
     block, ray, corr, norms = pl.pallas_call(
         functools.partial(last_kernel, bead_scale),
         out_shape=tuple(jax.ShapeDtypeStruct(shape, f32) for shape in shapes),
-        in_specs=[vmem] * 6,
+        in_specs=[vmem] * 4,
         out_specs=(hbm,) * 4,
         scratch_shapes=[pltpu.VMEM(shape, f32) for shape in shapes] + [pltpu.SemaphoreType.DMA((6,))],
         compiler_params=params,
         name="last",
-    )(own, prod, prod_got, quad, quad_got, gram)
+    )(own, prod, quad, gram)
     return block.reshape(comps, cols, width), ray, corr, norms.reshape(cols)
 
 

time: 25.8 us -> 25.2 us (0.977)
  Pallas kernels: 5.4 us -> 6.96 us
  starting transfers between devices: 9.57 us -> 8.27 us
  waiting for transfers between devices: 10 us -> 9.09 us
    ppermute x1, starting transfers between devices: 3.02 us -> 0.5 us  [per_device(): got = lax.ppermute(own, ('tile', 'col'), halo)]
    pallas_call x2 -> x3, Pallas kernels: 2.54 us -> 4.1 us  [the longest x1 1.78 us: per_device(): pl.pallas_call(second_kernel, out_shape=(block_shape, block_shape, jax.Sh...]
    ppermute x3 -> x1, waiting for transfers between devices: 2.31 us -> 0.97 us  [per_device(): prod_got = lax.ppermute(prod, 'col', [(c, c ^ 1) for c in range(n_col)])]
    ppermute x3 -> x1, starting transfers between devices: 0.4 us -> 1.32 us  [per_device(): prod_got = lax.ppermute(prod, 'col', [(c, c ^ 1) for c in range(n_col)])]
    ppermute x4, starting transfers between devices: 6.14 us -> 6.44 us  [crossed(): return lax.ppermute(x, ('tile', 'col'), route)]
    ppermute x1, waiting for transfers between devices: 3.3 us -> 3.59 us  [per_device(): got = lax.ppermute(own, ('tile', 'col'), halo)]
  transfers between devices with their start and end apart: 8 -> 6, of which waited for: 7 -> 6; matrix products, arithmetic and copies ran while one was open for 0% -> 0% of each run, Pallas kernels for 0% -> 3%
where the time goes in v4:
time: 25.2 us; the launch traced here: 25 us
  waiting for transfers between devices  9.09 us (36%)
  starting transfers between devices  8.27 us (33%)
  Pallas kernels  6.96 us (28%)
  between operations  0.66 us (3%)
    ppermute x4, starting transfers between devices, crossed(): return lax.ppermute(x, ('tile', 'col'), route)  6.44 us
    ppermute x4, waiting for transfers between devices, crossed(): return lax.ppermute(x, ('tile', 'col'), route)  4.53 us
    ppermute x1, waiting for transfers between devices, per_device(): got = lax.ppermute(own, ('tile', 'col'), halo)  3.59 us
    pallas_call x1, Pallas kernels, per_device(): pl.pallas_call(functools.partial(last_kernel, bead_scale), out_shape=tupl...  1.92 us
    pallas_call x1, Pallas kernels, per_device(): pl.pallas_call(second_kernel, out_shape=(block_shape, block_shape, jax.Sh...  1.78 us
    pallas_call x1, Pallas kernels, per_device(): pl.pallas_call(first_kernel, out_shape=(jax.ShapeDtypeStruct((rows + 8, w...  1.48 us
    ppermute x1, starting transfers between devices, per_device(): prod_got = lax.ppermute(prod, 'col', [(c, c ^ 1) for c in range(n_col)])  1.32 us
    ppermute x1, waiting for transfers between devices, per_device(): prod_got = lax.ppermute(prod, 'col', [(c, c ^ 1) for c in range(n_col)])  0.97 us
  transfers between devices with their start and end apart: 6, of which 6 were waited for; matrix products, arithmetic and copies ran while one was open for 0% of the time, Pallas kernels for 3%

profile of v4, /device:TPU:0, one launch (start us, length us, event | category | flops | bytes accessed | tf_op | source)
XLA Modules:
  0.0 25.0 jit_solution(276273158786170953)
XLA Ops:
  0.6 0.9 %pack.1.own_ref = f32[56,512]{1,0:T(8,128)S(1)} custom-call(f32[48,512]{1,0:T(8,128)} %bitcast.3, f32[3,512]{1,0:T(4,128)} %pos_ref.1, s32[2,1,4,8]{3,2,1,0:T(4,128)} %tiles_ref.1, s32[1,4]{1,0:T(1,128)} %count_ref.1), custom_call_target="tpu_custom_call" | custom-call | tf_op jit(solution)/shard_map/pack/pallas_call | solution.py:314
  1.6 0.5 %collective-permute-start = (f32[56,512]{1,0:T(8,128)S(1)}, f32[56,512]{1,0:T(8,128)S(1)}, u32[]{:S(2)}, u32[]{:S(2)}) collective-permute-start(f32[56,512]{1,0:T(8,128)S(1)} %pack.1.own_ref), channel_id=1, source_target_pairs={{5,0},{0,1},{7,2},{2,3},{1,4},{8,5},{3,6},{10,7},{13,8},{4,9},{15,... | collective-permute-start | bytes 344072 | tf_op jit(solution)/shard_map/ppermute | solution.py:339
  2.1 0.8 %own_pulls.1 = (bf16[8,640,384]{2,1,0:T(8,128)(2,1)S(1)}, f32[512,384]{1,0:T(8,128)S(1)}) custom-call(f32[56,512]{1,0:T(8,128)S(1)} %pack.1.own_ref), custom_call_target="tpu_custom_call" | custom-call | flops 100000000 | bytes 1000000 | tf_op jit(solution)/shard_map/own_pulls/pallas_call | solution.py:350
  2.9 3.6 %collective-permute-done.got_ref = f32[56,512]{1,0:T(8,128)S(1)} collective-permute-done((f32[56,512]{1,0:T(8,128)S(1)}, f32[56,512]{1,0:T(8,128)S(1)}, u32[]{:S(2)}, u32[]{:S(2)}) %collective-permute-start) | collective-permute-done | bytes 114720 | tf_op jit(solution)/shard_map/ppermute | solution.py:339
  6.5 1.5 %first.1 = (f32[56,512]{1,0:T(8,128)S(1)}, bf16[8,640,384]{2,1,0:T(8,128)(2,1)S(1)}) custom-call(f32[56,512]{1,0:T(8,128)S(1)} %pack.1.own_ref, f32[56,512]{1,0:T(8,128)S(1)} %collective-permute-done.got_ref, f32[512,384]{1,0:T(8,128)S(1)} %get-tuple-element.15.wide_own, ...), custom_call_target="tpu_custom_call", output_to_operand_aliasing={{1}: (3, {})} | custom-call | tf_op jit(solution)/shard_map/first/pallas_call | solution.py:359
  8.0 1.3 %collective-permute-start.1 = (f32[56,512]{1,0:T(8,128)S(1)}, f32[56,512]{1,0:T(8,128)S(1)}, u32[]{:S(2)}, u32[]{:S(2)}) collective-permute-start(f32[56,512]{1,0:T(8,128)S(1)} %get-tuple-element.17.prod_ref), channel_id=1, source_target_pairs={{0,1},{1,0},{2,3},{3,2},{4,5},{5,4},{6,7},{7,6},{8,9},{9,8},{10,11... | collective-permute-start | bytes 344072 | tf_op jit(solution)/shard_map/ppermute | solution.py:369
  9.3 1.0 %collective-permute-done.1.prod_got_ref = f32[56,512]{1,0:T(8,128)S(1)} collective-permute-done((f32[56,512]{1,0:T(8,128)S(1)}, f32[56,512]{1,0:T(8,128)S(1)}, u32[]{:S(2)}, u32[]{:S(2)}) %collective-permute-start.1) | collective-permute-done | bytes 114720 | tf_op jit(solution)/shard_map/ppermute | solution.py:369
  10.3 1.8 %second.1 = (f32[48,512]{1,0:T(8,128)S(1)}, f32[48,512]{1,0:T(8,128)S(1)}, f32[16,128]{1,0:T(8,128)S(1)}, bf16[8,640,384]{2,1,0:T(8,128)(2,1)S(1)}) custom-call(f32[56,512]{1,0:T(8,128)S(1)} %pack.1.own_ref, f32[56,512]{1,0:T(8,128)S(1)} %get-tuple-element.17.prod_ref, ...), custom_call_target="tpu_custom_call", output_to_operand_aliasing={{3}: (3, {})} | custom-call | tf_op jit(solution)/shard_map/second/pallas_call | solution.py:371
  12.1 3.5 %collective-permute-start.4 = (f32[16,128]{1,0:T(8,128)S(1)}, f32[16,128]{1,0:T(8,128)S(1)}, u32[]{:S(2)}, u32[]{:S(2)}) collective-permute-start(f32[16,128]{1,0:T(8,128)S(1)} %get-tuple-element.21), channel_id=1, source_target_pairs={{0,13},{1,12},{2,15},{3,14},{4,9},{5,8},{6,11},{7,10},{8,5},{9,4},... | collective-permute-start | bytes 24584 | tf_op jit(solution)/shard_map/ppermute | solution.py:386
  15.6 0.4 %collective-permute-start.3 = (f32[16,128]{1,0:T(8,128)S(1)}, f32[16,128]{1,0:T(8,128)S(1)}, u32[]{:S(2)}, u32[]{:S(2)}) collective-permute-start(f32[16,128]{1,0:T(8,128)S(1)} %get-tuple-element.21), channel_id=1, source_target_pairs={{0,9},{1,8},{2,11},{3,10},{4,13},{5,12},{6,15},{7,14},{8,1},{9,0},... | collective-permute-start | bytes 24584 | tf_op jit(solution)/shard_map/ppermute | solution.py:386
  16.0 0.2 collective-permute-start.2
  16.2 0.8 %collective-permute-done.4 = f32[16,128]{1,0:T(8,128)S(1)} collective-permute-done((f32[16,128]{1,0:T(8,128)S(1)}, f32[16,128]{1,0:T(8,128)S(1)}, u32[]{:S(2)}, u32[]{:S(2)}) %collective-permute-start.4) | collective-permute-done | bytes 8224 | tf_op jit(solution)/shard_map/ppermute | solution.py:386
  17.0 1.7 %collective-permute-done.3 = f32[16,128]{1,0:T(8,128)S(1)} collective-permute-done((f32[16,128]{1,0:T(8,128)S(1)}, f32[16,128]{1,0:T(8,128)S(1)}, u32[]{:S(2)}, u32[]{:S(2)}) %collective-permute-start.3) | collective-permute-done | bytes 8224 | tf_op jit(solution)/shard_map/ppermute | solution.py:386
  18.7 0.4 %collective-permute-done.2 = f32[16,128]{1,0:T(8,128)S(1)} collective-permute-done((f32[16,128]{1,0:T(8,128)S(1)}, f32[16,128]{1,0:T(8,128)S(1)}, u32[]{:S(2)}, u32[]{:S(2)}) %collective-permute-start.2) | collective-permute-done | bytes 8224 | tf_op jit(solution)/shard_map/ppermute | solution.py:386
  19.1 2.3 %collective-permute-start.5 = (f32[16,128]{1,0:T(8,128)S(1)}, f32[16,128]{1,0:T(8,128)S(1)}, u32[]{:S(2)}, u32[]{:S(2)}) collective-permute-start(f32[16,128]{1,0:T(8,128)S(1)} %add_add_fusion), channel_id=1, source_target_pairs={{0,17},{1,16},{2,19},{3,18},{4,21},{5,20},{6,23},{7,22},{8,25},{9,... | collective-permute-start | bytes 24584 | tf_op jit(solution)/shard_map/ppermute | solution.py:386
  21.4 1.6 %collective-permute-done.5 = f32[16,128]{1,0:T(8,128)S(1)} collective-permute-done((f32[16,128]{1,0:T(8,128)S(1)}, f32[16,128]{1,0:T(8,128)S(1)}, u32[]{:S(2)}, u32[]{:S(2)}) %collective-permute-start.5) | collective-permute-done | bytes 8224 | tf_op jit(solution)/shard_map/ppermute | solution.py:386
  23.1 1.9 %last.1 = (f32[48,512]{1,0:T(8,128)}, f32[16,16]{1,0:T(8,128)}, f32[16,16]{1,0:T(8,128)}, f32[1,16]{1,0:T(1,128)}) custom-call(f32[56,512]{1,0:T(8,128)S(1)} %pack.1.own_ref, f32[48,512]{1,0:T(8,128)S(1)} %get-tuple-element.19.prod_ref, f32[48,512]{1,0:T(8,128)S(1)} %get-tuple-element.20.quad_ref, f32[16,128]{1,0:T(8,128)S(1)} %add.15.gram_ref), custom_call_target="tpu_custom_call" | custom-call | tf_op jit(solution)/shard_map/last/pallas_call | solution.py:397
  (2 shorter events, 0.0 us)
Async XLA Ops:
  1.6 4.9 %collective-permute-start = (f32[56,512]{1,0:T(8,128)S(1)}, f32[56,512]{1,0:T(8,128)S(1)}, u32[]{:S(2)}, u32[]{:S(2)}) collective-permute-start(f32[56,512]{1,0:T(8,128)S(1)} %pack.1.own_ref), channel_id=1, source_target_pairs={{5,0},{0,1},{7,2},{2,3},{1,4},{8,5},{3,6},{10,7},{13,8},{4,9},{15,... | collective-permute-start | bytes 344072 | tf_op jit(solution)/shard_map/ppermute | solution.py:339
  8.0 2.3 %collective-permute-start.1 = (f32[56,512]{1,0:T(8,128)S(1)}, f32[56,512]{1,0:T(8,128)S(1)}, u32[]{:S(2)}, u32[]{:S(2)}) collective-permute-start(f32[56,512]{1,0:T(8,128)S(1)} %get-tuple-element.17.prod_ref), channel_id=1, source_target_pairs={{0,1},{1,0},{2,3},{3,2},{4,5},{5,4},{6,7},{7,6},{8,9},{9,8},{10,11... | collective-permute-start | bytes 344072 | tf_op jit(solution)/shard_map/ppermute | solution.py:369
  12.1 4.9 %collective-permute-start.4 = (f32[16,128]{1,0:T(8,128)S(1)}, f32[16,128]{1,0:T(8,128)S(1)}, u32[]{:S(2)}, u32[]{:S(2)}) collective-permute-start(f32[16,128]{1,0:T(8,128)S(1)} %get-tuple-element.21), channel_id=1, source_target_pairs={{0,13},{1,12},{2,15},{3,14},{4,9},{5,8},{6,11},{7,10},{8,5},{9,4},... | collective-permute-start | bytes 24584 | tf_op jit(solution)/shard_map/ppermute | solution.py:386
  15.6 3.1 %collective-permute-start.3 = (f32[16,128]{1,0:T(8,128)S(1)}, f32[16,128]{1,0:T(8,128)S(1)}, u32[]{:S(2)}, u32[]{:S(2)}) collective-permute-start(f32[16,128]{1,0:T(8,128)S(1)} %get-tuple-element.21), channel_id=1, source_target_pairs={{0,9},{1,8},{2,11},{3,10},{4,13},{5,12},{6,15},{7,14},{8,1},{9,0},... | collective-permute-start | bytes 24584 | tf_op jit(solution)/shard_map/ppermute | solution.py:386
  16.0 3.1 %collective-permute-start.2 = (f32[16,128]{1,0:T(8,128)S(1)}, f32[16,128]{1,0:T(8,128)S(1)}, u32[]{:S(2)}, u32[]{:S(2)}) collective-permute-start(f32[16,128]{1,0:T(8,128)S(1)} %get-tuple-element.21), channel_id=1, source_target_pairs={{0,5},{1,4},{2,7},{3,6},{4,1},{5,0},{6,3},{7,2},{8,13},{9,12},{10,... | collective-permute-start | bytes 24584 | tf_op jit(solution)/shard_map/ppermute | solution.py:386
  19.1 4.0 %collective-permute-start.5 = (f32[16,128]{1,0:T(8,128)S(1)}, f32[16,128]{1,0:T(8,128)S(1)}, u32[]{:S(2)}, u32[]{:S(2)}) collective-permute-start(f32[16,128]{1,0:T(8,128)S(1)} %add_add_fusion), channel_id=1, source_target_pairs={{0,17},{1,16},{2,19},{3,18},{4,21},{5,20},{6,23},{7,22},{8,25},{9,... | collective-permute-start | bytes 24584 | tf_op jit(solution)/shard_map/ppermute | solution.py:386

commit v5 on v4

--- a/solution.py
+++ b/solution.py
@@ -56,11 +56,6 @@
     return high, (x - high.astype(f32)).astype(bf16)
 
 
-def store_vectors(vec, high, low, x, place):
-    vec[:, place] = x
-    high[:, place], low[:, place] = split(x)
-
-
 def received_places(block):
     t = lax.axis_index("tile")
     missing = jnp.where(parity() == 0, t == 0, t == lax.axis_size("tile") - 1)
@@ -94,118 +89,182 @@
             pull[row, place, tile_slice(c)] = (weight * offset[c]).astype(bf16)
 
 
-def bound_of(pos, w, j):
-    reach = abs(w - j)
-    return pos[4 + reach : 5 + reach, tile_slice(min(w, j))]
-
-
 def by_parity(body):
     odd = parity()
     pl.when(odd == 0)(functools.partial(body, 0))
     pl.when(odd == 1)(functools.partial(body, 1))
 
 
-def apply_pulls(vec, high, low, pos, pull, w):
+class Tiles:
+    def __init__(self, place):
+        self.place = place
+
+    def __call__(self, which, near):
+        parts = []
+        for w in near:
+            refs, tile = self.place(w)
+            parts.append(refs[which][:, tile_slice(refs.get("pos_tile", tile) if which == "pos" else tile)])
+        return parts[0] if len(parts) == 1 else jnp.concatenate(parts, axis=1)
+
+    def bound(self, w, j):
+        reach = abs(w - j)
+        return self("pos", [min(w, j)])[4 + reach : 5 + reach]
+
+
+def sum_pulls(tiles, w, near, pull):
+    middle = jnp.mean(tiles("pos", [w]), axis=1, keepdims=True)
+    place = tiles("pos", near) - middle
+    vec = tiles("vec", near)
+    cols = vec.shape[0] // 3
+    row_of = lax.broadcasted_iota(jnp.int32, place.shape, 0)
+    extra = jnp.where(row_of < 3, place, jnp.where(row_of == 3, 1.0, 0.0))
+    along = sum(place[d : d + 1] * vec[d * cols : (d + 1) * cols] for d in range(3))
+    more_high, more_low = split(jnp.concatenate([along, extra, jnp.zeros_like(extra)], axis=0))
+    left = jnp.concatenate([tiles("high", near), more_high, tiles("low", near), more_low], axis=0)
+    n = left.shape[0] // 2
+    first = near[0] - w + REACH
+    part = slice(first * TILE_B, (first + len(near)) * TILE_B)
+    total = jnp.dot(left, pull[part, :], preferred_element_type=f32)
+    return total[0:n] + total[n:]
+
+
+def from_sums(tiles, w, total):
+    vec, pos = tiles("vec", [w]), tiles("pos", [w])
     rows = vec.shape[0]
     cols = rows // 3
-    near = slice((w - REACH) * TILE_B, (w + REACH + 1) * TILE_B)
-    here = tile_slice(w)
-    middle = jnp.mean(pos[:, here], axis=1, keepdims=True)
-    place = pos[:, near] - middle
-    row_of = lax.broadcasted_iota(jnp.int32, place.shape, 0)
-    extra = jnp.where(row_of < 3, place, jnp.where(row_of == 3, 1.0, 0.0))
-    along = sum(place[d : d + 1] * vec[d * cols : (d + 1) * cols, near] for d in range(3))
-    more_high, more_low = split(jnp.concatenate([along, extra, jnp.zeros_like(extra)], axis=0))
-    left_high = jnp.concatenate([high[:, near], more_high], axis=0)
-    left_low = jnp.concatenate([low[:, near], more_low], axis=0)
-    left = jnp.concatenate([left_high, left_low], axis=0)
-    n = left_high.shape[0]
-    total = jnp.dot(left, pull, preferred_element_type=f32)
-    total = total[0:n] + total[n:]
-    mine = [place[d : d + 1, REACH * TILE_B : (REACH + 1) * TILE_B] for d in range(3)]
+    mine = pos - jnp.mean(pos, axis=1, keepdims=True)
     out = []
     for c in range(3):
         part = total[:, tile_slice(c)]
         e = rows + cols
         term = -part[rows:e]
         for d in range(3):
-            diag = part[e + d : e + d + 1] - mine[d] * part[e + 3 : e + 4]
-            term += diag * vec[d * cols : (d + 1) * cols, here] + mine[d] * part[d * cols : (d + 1) * cols]
+            diag = part[e + d : e + d + 1] - mine[d : d + 1] * part[e + 3 : e + 4]
+            term += diag * vec[d * cols : (d + 1) * cols] + mine[d : d + 1] * part[d * cols : (d + 1) * cols]
         out.append(term * (spring_scale * step_size / cutoff_sq**2))
     return jnp.concatenate(out, axis=0)
 
 
-def own_kernel(own_ref, pull, wide):
-    rows = own_ref.shape[0] - 8
-    tiles = own_ref.shape[1] // TILE_B
-    pos = own_ref.at[rows : rows + 8]
-    wide[...] = spread_places(pos[...])
+def own_kernel(own_ref, pull, wide, high, low, part_ref):
+    rows, width = high.shape
+    tiles = width // TILE_B
+    half = tiles // 2
+    own = dict(vec=own_ref.at[0:rows], pos=own_ref.at[rows : rows + 8], high=high, low=low)
+    mine = Tiles(lambda u: (own, u))
+    wide[...] = spread_places(own["pos"][...])
+    high[...], low[...] = split(own["vec"][...])
+    near = [range(max(0, u - REACH), min(tiles, u + REACH + 1)) for u in range(tiles)]
     for u in range(tiles):
-        for j in range(max(0, u - REACH), min(tiles, u + REACH + 1)):
-            fill_pull(pos[:, tile_slice(u)], bound_of(pos, u, j), wide, j * TILE_B, pull, u + REACH, j - u + REACH)
-
-
-def first_kernel(own_ref, got_ref, wide_own, pull_in, out_ref, pull, vec, high, low, pos, wide_got):
-    rows = vec.shape[0]
-    width = own_ref.shape[1]
-    tiles = width // TILE_B
-    places = received_places(got_ref[rows : rows + 8, :])
-    out_ref[rows : rows + 8, :] = places
-    wide_got[...] = spread_places(places)
+        for j in near[u]:
+            fill_pull(mine("pos", [u]), mine.bound(u, j), wide, j * TILE_B, pull, u + REACH, j - u + REACH)
 
     def body(odd):
-        ours = slice((1 - odd) * width, (2 - odd) * width)
-        others = slice(odd * width, (1 + odd) * width)
-        store_vectors(vec, high, low, own_ref[0:rows, :], ours)
-        store_vectors(vec, high, low, got_ref[0:rows, :], others)
-        pos[:, ours] = own_ref[rows : rows + 8, :]
-        pos[:, others] = places
+        for k in range(half):
+            u = odd * half + k
+            part_ref[k] = sum_pulls(mine, u, near[u], pull.at[u + REACH])
+
+    by_parity(body)
+
+
+def first_kernel(
+    own_ref, got_ref, wide_own, high_own, low_own, part_ref, pull_in, out_ref, pull, places, wide_got, high_got, low_got
+):
+    rows, width = high_own.shape
+    tiles = width // TILE_B
+    places[...] = received_places(got_ref[rows : rows + 8, :])
+    out_ref[rows : rows + 8, :] = places[...]
+    wide_got[...] = spread_places(places[...])
+    high_got[...], low_got[...] = split(got_ref[0:rows, :])
+    own = dict(vec=own_ref.at[0:rows], pos=own_ref.at[rows : rows + 8], high=high_own, low=low_own, wide=wide_own)
+    got = dict(vec=got_ref.at[0:rows], pos=places, high=high_got, low=low_got, wide=wide_got)
+
+    def body(odd):
+        window = Tiles(lambda w: (got if w // tiles == odd else own, w % tiles))
         for r in range(tiles):
             w = r + REACH
             row = r + odd * tiles
-            for j in range(w - REACH, w + REACH + 1):
-                wide, base = (wide_got, odd) if j // tiles == odd else (wide_own, 1 - odd)
-                if wide is wide_got or w // tiles == odd:
-                    bound = bound_of(pos, w, j)
-                    fill_pull(pos[:, tile_slice(w)], bound, wide, (j - base * tiles) * TILE_B, pull, row, j - w + REACH)
-            out_ref[0:rows, tile_slice(r)] = apply_pulls(vec, high, low, pos, pull[row], w)
+            inner = w // tiles != odd
+            near = [j for j in range(w - REACH, w + REACH + 1) if not inner or j // tiles == odd]
+            for j in near:
+                refs, tile = window.place(j)
+                fill_pull(
+                    window("pos", [w]), window.bound(w, j), refs["wide"], tile * TILE_B, pull, row, j - w + REACH
+                )
+            total = sum_pulls(window, w, near, pull.at[row])
+            if inner:
+                total = total + part_ref[w % tiles - odd * (tiles // 2)]
+            out_ref[0:rows, tile_slice(r)] = from_sums(window, w, total)
 
     by_parity(body)
 
 
-def second_kernel(own_ref, prod_ref, prod_got_ref, pull_in, out_ref, mid_ref, gram_ref, pull, vec, high, low, pos, wide):
-    rows = vec.shape[0]
+def near_tiles(own_ref, ours, theirs, odd):
+    rows, width = ours["vec"].shape
+    tiles = width // TILE_B
+    sides = (ours, theirs) if odd == 0 else (theirs, ours)
+
+    def place(w):
+        side = sides[w // tiles]
+        if w < REACH:
+            pos, tile = sides[0]["got"], w + tiles - REACH
+        elif w < tiles + REACH:
+            pos, tile = own_ref.at[rows : rows + 8], w - REACH
+        else:
+            pos, tile = sides[1]["got"], w - tiles - REACH
+        return dict(side, pos=pos, pos_tile=tile), w % tiles
+
+    return Tiles(place)
+
+
+def middle_kernel(own_ref, prod_ref, pull, part_ref, high, low):
+    rows, width = high.shape
+    tiles = width // TILE_B
+    high[...], low[...] = split(prod_ref[0:rows, :])
+    ours = dict(vec=prod_ref.at[0:rows], got=prod_ref.at[rows : rows + 8], high=high, low=low)
+
+    def body(odd):
+        window = near_tiles(own_ref, ours, ours, odd)
+        for u in range(tiles):
+            w = u + REACH
+            near = [j for j in range(w - REACH, w + REACH + 1) if j // tiles == odd]
+            part_ref[u] = sum_pulls(window, w, near, pull.at[w])
+
+    by_parity(body)
+
+
+def second_kernel(own_ref, prod_ref, prod_got_ref, part_ref, pull_in, out_ref, mid_ref, gram_ref, pull, high, low, wide):
+    rows, width = high.shape
     cols = rows // 3
-    width = own_ref.shape[1]
     tiles = width // TILE_B
     edge = REACH * TILE_B
+    high[...], low[...] = split(prod_got_ref[0:rows, :])
+    ours = dict(vec=prod_ref.at[0:rows], got=prod_ref.at[rows : rows + 8])
+    theirs = dict(vec=prod_got_ref.at[0:rows], got=prod_got_ref.at[rows : rows + 8], high=high, low=low)
 
     def body(odd):
-        sides = prod_ref, prod_got_ref
-        pos[:, 0:edge] = sides[odd][rows : rows + 8, width - edge :]
-        pos[:, edge : edge + width] = own_ref[rows : rows + 8, :]
-        pos[:, edge + width :] = sides[1 - odd][rows : rows + 8, 0:edge]
-        store_vectors(vec, high, low, prod_ref[0:rows, :], slice(odd * width, (1 + odd) * width))
-        store_vectors(vec, high, low, prod_got_ref[0:rows, :], slice((1 - odd) * width, (2 - odd) * width))
+        window = near_tiles(own_ref, ours, theirs, odd)
         start = (1 - odd) * (tiles + REACH)
-        wide[...] = spread_places(pos[:, start * TILE_B : start * TILE_B + edge])
-        half = tiles // 2
-        for w in range(REACH + (1 - odd) * half, REACH + (2 - odd) * half):
-            for j in range(max(start, w - REACH), min(start + REACH, w + REACH + 1)):
-                bound = bound_of(pos, w, j)
-                fill_pull(pos[:, tile_slice(w)], bound, wide, (j - start) * TILE_B, pull, w, j - w + REACH)
+        wide[...] = spread_places(window("pos", range(start, start + REACH)))
+        for u in range(tiles):
+            w = u + REACH
+            near = [j for j in range(w - REACH, w + REACH + 1) if j // tiles != odd]
+            for j in near:
+                if start <= j < start + REACH:
+                    fill_pull(
+                        window("pos", [w]), window.bound(w, j), wide, (j - start) * TILE_B, pull, w, j - w + REACH
+                    )
+            total = part_ref[u] + sum_pulls(window, w, near, pull.at[w])
+            out_ref[:, tile_slice(u)] = from_sums(window, w, total)
+            mid_ref[:, tile_slice(u)] = window("vec", [w])
 
     by_parity(body)
-    for u in range(tiles):
-        out_ref[:, tile_slice(u)] = apply_pulls(vec, high, low, pos, pull[u + REACH], u + REACH)
-    mid_ref[...] = vec[:, edge : edge + width]
-    gram = jnp.zeros((rows, rows), f32)
-    for d in range(3):
-        band = slice(d * cols, (d + 1) * cols)
-        joint = jnp.concatenate(
-            [own_ref[band, :], mid_ref[band, :], out_ref[band, :]], axis=0
-        )
-        gram += lax.dot_general(joint, joint, (((1,), (1,)), ((), ())), precision=highest, preferred_element_type=f32)
+    bands = [slice(d * cols, (d + 1) * cols) for d in range(3)]
+    joint = jnp.concatenate(
+        [jnp.concatenate([own_ref[band, :], mid_ref[band, :], out_ref[band, :]], axis=0) for band in bands], axis=1
+    )
+    joint = jnp.concatenate(split(joint), axis=0)
+    gram = lax.dot_general(joint, joint, (((1,), (1,)), ((), ())), preferred_element_type=f32)
+    gram = gram[0:rows, 0:rows] + (gram[0:rows, rows:] + gram[rows:, 0:rows] + gram[rows:, rows:])
     gram_ref[...] = jnp.zeros(gram_ref.shape, f32)
     gram_ref[:, 0:rows] = gram[0:cols]
     gram_ref[:, rows : 2 * rows] = gram[cols : 2 * cols]
@@ -338,46 +397,62 @@
             halo.append((source * n_col + (c ^ 1), t * n_col + c))
     got = lax.ppermute(own, ("tile", "col"), halo)
 
-    def scratch(window):
-        return [
-            pltpu.VMEM((rows, window), f32),
-            pltpu.VMEM((rows, window), bf16),
-            pltpu.VMEM((rows, window), bf16),
-            pltpu.VMEM((8, window), f32),
-        ]
-
-    pulls = jax.ShapeDtypeStruct((2 * tiles, (2 * REACH + 1) * TILE_B, 3 * TILE_B), bf16)
-    pull, wide = pl.pallas_call(
+    def f32_array(*shape):
+        return jax.ShapeDtypeStruct(shape, f32)
+
+    def bf16_array(*shape):
+        return jax.ShapeDtypeStruct(shape, bf16)
+
+    parts = [pltpu.VMEM((rows, width), bf16)] * 2
+    sums = rows + cols + 16
+    pulls = bf16_array(2 * tiles, (2 * REACH + 1) * TILE_B, 3 * TILE_B)
+    hidden = pl.CostEstimate(flops=10**8, bytes_accessed=10**6, transcendentals=0)
+    pull, wide, high, low, part = pl.pallas_call(
         own_kernel,
-        out_shape=(pulls, jax.ShapeDtypeStruct((width, 3 * TILE_B), f32)),
+        out_shape=(
+            pulls,
+            f32_array(width, 3 * TILE_B),
+            bf16_array(rows, width),
+            bf16_array(rows, width),
+            f32_array(tiles // 2, sums, 3 * TILE_B),
+        ),
         in_specs=[vmem],
-        out_specs=(vmem,) * 2,
+        out_specs=(vmem,) * 5,
         compiler_params=params,
-        cost_estimate=pl.CostEstimate(flops=10**8, bytes_accessed=10**6, transcendentals=0),
+        cost_estimate=hidden,
         name="own_pulls",
     )(own)
     prod, pull = pl.pallas_call(
         first_kernel,
-        out_shape=(jax.ShapeDtypeStruct((rows + 8, width), f32), pulls),
-        in_specs=[vmem] * 4,
+        out_shape=(f32_array(rows + 8, width), pulls),
+        in_specs=[vmem] * 7,
         out_specs=(vmem,) * 2,
-        input_output_aliases={3: 1},
-        scratch_shapes=scratch(2 * width) + [pltpu.VMEM((width, 3 * TILE_B), f32)],
+        input_output_aliases={6: 1},
+        scratch_shapes=[pltpu.VMEM((8, width), f32), pltpu.VMEM((width, 3 * TILE_B), f32)] + parts,
         compiler_params=params,
         name="first",
-    )(own, got, wide, pull)
+    )(own, got, wide, high, low, part, pull)
     prod_got = lax.ppermute(prod, "col", [(c, c ^ 1) for c in range(n_col)])
-    block_shape = jax.ShapeDtypeStruct((rows, width), f32)
+    part = pl.pallas_call(
+        middle_kernel,
+        out_shape=f32_array(tiles, sums, 3 * TILE_B),
+        in_specs=[vmem] * 3,
+        out_specs=vmem,
+        scratch_shapes=parts,
+        compiler_params=params,
+        cost_estimate=hidden,
+        name="middle",
+    )(own, prod, pull)
     quad, prod, gram, pull = pl.pallas_call(
         second_kernel,
-        out_shape=(block_shape, block_shape, jax.ShapeDtypeStruct((cols, 128), f32), pulls),
-        in_specs=[vmem] * 4,
+        out_shape=(f32_array(rows, width), f32_array(rows, width), f32_array(cols, 128), pulls),
+        in_specs=[vmem] * 5,
         out_specs=(vmem,) * 4,
-        input_output_aliases={3: 3},
-        scratch_shapes=scratch(2 * width) + [pltpu.VMEM((REACH * TILE_B, 3 * TILE_B), f32)],
+        input_output_aliases={4: 3},
+        scratch_shapes=parts + [pltpu.VMEM((REACH * TILE_B, 3 * TILE_B), f32)],
         compiler_params=params,
         name="second",
-    )(own, prod, prod_got, pull)
+    )(own, prod, prod_got, part, pull)
 
     def crossed(x, step):
         route = [

time: 25.2 us -> 24.3 us (0.964)
  waiting for transfers between devices: 9.09 us -> 8.07 us
    ppermute x1, waiting for transfers between devices: 0.97 us -> 0.49 us  [per_device(): prod_got = lax.ppermute(prod, 'col', [(c, c ^ 1) for c in range(n_col)])]
    ppermute x1, waiting for transfers between devices: 3.59 us -> 3.19 us  [per_device(): got = lax.ppermute(own, ('tile', 'col'), halo)]
    pallas_call x3 -> x4, Pallas kernels: 4.1 us -> 4.32 us  [the longest x1 1.41 us: per_device(): pl.pallas_call(first_kernel, out_shape=(f32_array(rows + 8, width), pulls...]
  transfers between devices with their start and end apart: 6 -> 6, of which waited for: 6 -> 6; matrix products, arithmetic and copies ran while one was open for 0% -> 0% of each run, Pallas kernels for 3% -> 7%
where the time goes in v5:
time: 24.3 us; the launch traced here: 24.1 us
  starting transfers between devices  8.19 us (34%)
  waiting for transfers between devices  8.07 us (33%)
  Pallas kernels  7.18 us (30%)
  between operations  0.67 us (3%)
    ppermute x4, starting transfers between devices, crossed(): return lax.ppermute(x, ('tile', 'col'), route)  6.47 us
    ppermute x4, waiting for transfers between devices, crossed(): return lax.ppermute(x, ('tile', 'col'), route)  4.39 us
    ppermute x1, waiting for transfers between devices, per_device(): got = lax.ppermute(own, ('tile', 'col'), halo)  3.19 us
    pallas_call x1, Pallas kernels, per_device(): pl.pallas_call(functools.partial(last_kernel, bead_scale), out_shape=tupl...  1.92 us
    pallas_call x1, Pallas kernels, per_device(): pl.pallas_call(first_kernel, out_shape=(f32_array(rows + 8, width), pulls...  1.41 us
    pallas_call x1, Pallas kernels, per_device(): pl.pallas_call(own_kernel, out_shape=(pulls, f32_array(width, 3 * TILE_B)...  1.24 us
    ppermute x1, starting transfers between devices, per_device(): prod_got = lax.ppermute(prod, 'col', [(c, c ^ 1) for c in range(n_col)])  1.22 us
    pallas_call x1, Pallas kernels, per_device(): pl.pallas_call(second_kernel, out_shape=(f32_array(rows, width), f32_arra...  1.2 us
  transfers between devices with their start and end apart: 6, of which 6 were waited for; matrix products, arithmetic and copies ran while one was open for 0% of the time, Pallas kernels for 7%

profile of v5, /device:TPU:0, one launch (start us, length us, event | category | flops | bytes accessed | tf_op | source)
XLA Modules:
  0.0 24.1 jit_solution(6321266272229320262)
XLA Ops:
  0.6 0.9 %pack.1.own_ref = f32[56,512]{1,0:T(8,128)S(1)} custom-call(f32[48,512]{1,0:T(8,128)} %bitcast.3, f32[3,512]{1,0:T(4,128)} %pos_ref.1, s32[2,1,4,8]{3,2,1,0:T(4,128)} %tiles_ref.1, s32[1,4]{1,0:T(1,128)} %count_ref.1), custom_call_target="tpu_custom_call" | custom-call | tf_op jit(solution)/shard_map/pack/pallas_call | solution.py:373
  1.6 0.5 %collective-permute-start = (f32[56,512]{1,0:T(8,128)S(1)}, f32[56,512]{1,0:T(8,128)S(1)}, u32[]{:S(2)}, u32[]{:S(2)}) collective-permute-start(f32[56,512]{1,0:T(8,128)S(1)} %pack.1.own_ref), channel_id=1, source_target_pairs={{5,0},{0,1},{7,2},{2,3},{1,4},{8,5},{3,6},{10,7},{13,8},{4,9},{15,... | collective-permute-start | bytes 344072 | tf_op jit(solution)/shard_map/ppermute | solution.py:398
  2.1 1.2 %own_pulls.1 = (bf16[8,640,384]{2,1,0:T(8,128)(2,1)S(1)}, f32[512,384]{1,0:T(8,128)S(1)}, bf16[48,512]{1,0:T(8,128)(2,1)S(1)}, bf16[48,512]{1,0:T(8,128)(2,1)S(1)}, f32[2,80,384]{2,1,0:T(8,128)S(1)}) custom-call(f32[56,512]{1,0:T(8,128)S(1)} %pack.1.own_ref), custom_call_target="tpu_custom_call" | custom-call | flops 100000000 | bytes 1000000 | tf_op jit(solution)/shard_map/own_pulls/pallas_call | solution.py:410
  3.3 3.2 %collective-permute-done.got_ref = f32[56,512]{1,0:T(8,128)S(1)} collective-permute-done((f32[56,512]{1,0:T(8,128)S(1)}, f32[56,512]{1,0:T(8,128)S(1)}, u32[]{:S(2)}, u32[]{:S(2)}) %collective-permute-start) | collective-permute-done | bytes 114720 | tf_op jit(solution)/shard_map/ppermute | solution.py:398
  6.5 1.4 %first.1 = (f32[56,512]{1,0:T(8,128)S(1)}, bf16[8,640,384]{2,1,0:T(8,128)(2,1)S(1)}) custom-call(f32[56,512]{1,0:T(8,128)S(1)} %pack.1.own_ref, f32[56,512]{1,0:T(8,128)S(1)} %collective-permute-done.got_ref, f32[512,384]{1,0:T(8,128)S(1)} %get-tuple-element.18.wide_own, ...), custom_call_target="tpu_custom_call", output_to_operand_aliasing={{1}: (6, {})} | custom-call | tf_op jit(solution)/shard_map/first/pallas_call | solution.py:425
  7.9 1.2 %collective-permute-start.1 = (f32[56,512]{1,0:T(8,128)S(1)}, f32[56,512]{1,0:T(8,128)S(1)}, u32[]{:S(2)}, u32[]{:S(2)}) collective-permute-start(f32[56,512]{1,0:T(8,128)S(1)} %get-tuple-element.23.prod_ref), channel_id=1, source_target_pairs={{0,1},{1,0},{2,3},{3,2},{4,5},{5,4},{6,7},{7,6},{8,9},{9,8},{10,11... | collective-permute-start | bytes 344072 | tf_op jit(solution)/shard_map/ppermute | solution.py:435
  9.2 0.5 %middle.1.part_ref = f32[4,80,384]{2,1,0:T(8,128)S(1)} custom-call(f32[56,512]{1,0:T(8,128)S(1)} %pack.1.own_ref, f32[56,512]{1,0:T(8,128)S(1)} %get-tuple-element.23.prod_ref, bf16[8,640,384]{2,1,0:T(8,128)(2,1)S(1)} %get-tuple-element.24.pull.pull_in), custom_call_target="tpu_custom_call" | custom-call | flops 100000000 | bytes 1000000 | tf_op jit(solution)/shard_map/middle/pallas_call | solution.py:436
  9.6 0.5 %collective-permute-done.1.prod_got_ref = f32[56,512]{1,0:T(8,128)S(1)} collective-permute-done((f32[56,512]{1,0:T(8,128)S(1)}, f32[56,512]{1,0:T(8,128)S(1)}, u32[]{:S(2)}, u32[]{:S(2)}) %collective-permute-start.1) | collective-permute-done | bytes 114720 | tf_op jit(solution)/shard_map/ppermute | solution.py:435
  10.1 1.2 %second.1 = (f32[48,512]{1,0:T(8,128)S(1)}, f32[48,512]{1,0:T(8,128)S(1)}, f32[16,128]{1,0:T(8,128)S(1)}, bf16[8,640,384]{2,1,0:T(8,128)(2,1)S(1)}) custom-call(f32[56,512]{1,0:T(8,128)S(1)} %pack.1.own_ref, f32[56,512]{1,0:T(8,128)S(1)} %get-tuple-element.23.prod_ref, ...), custom_call_target="tpu_custom_call", output_to_operand_aliasing={{3}: (4, {})} | custom-call | tf_op jit(solution)/shard_map/second/pallas_call | solution.py:446
  11.3 3.5 %collective-permute-start.4 = (f32[16,128]{1,0:T(8,128)S(1)}, f32[16,128]{1,0:T(8,128)S(1)}, u32[]{:S(2)}, u32[]{:S(2)}) collective-permute-start(f32[16,128]{1,0:T(8,128)S(1)} %get-tuple-element.27), channel_id=1, source_target_pairs={{0,13},{1,12},{2,15},{3,14},{4,9},{5,8},{6,11},{7,10},{8,5},{9,4},... | collective-permute-start | bytes 24584 | tf_op jit(solution)/shard_map/ppermute | solution.py:461
  14.8 0.3 %collective-permute-start.3 = (f32[16,128]{1,0:T(8,128)S(1)}, f32[16,128]{1,0:T(8,128)S(1)}, u32[]{:S(2)}, u32[]{:S(2)}) collective-permute-start(f32[16,128]{1,0:T(8,128)S(1)} %get-tuple-element.27), channel_id=1, source_target_pairs={{0,9},{1,8},{2,11},{3,10},{4,13},{5,12},{6,15},{7,14},{8,1},{9,0},... | collective-permute-start | bytes 24584 | tf_op jit(solution)/shard_map/ppermute | solution.py:461
  15.1 0.2 collective-permute-start.2
  15.3 0.9 %collective-permute-done.4 = f32[16,128]{1,0:T(8,128)S(1)} collective-permute-done((f32[16,128]{1,0:T(8,128)S(1)}, f32[16,128]{1,0:T(8,128)S(1)}, u32[]{:S(2)}, u32[]{:S(2)}) %collective-permute-start.4) | collective-permute-done | bytes 8224 | tf_op jit(solution)/shard_map/ppermute | solution.py:461
  16.2 1.7 %collective-permute-done.3 = f32[16,128]{1,0:T(8,128)S(1)} collective-permute-done((f32[16,128]{1,0:T(8,128)S(1)}, f32[16,128]{1,0:T(8,128)S(1)}, u32[]{:S(2)}, u32[]{:S(2)}) %collective-permute-start.3) | collective-permute-done | bytes 8224 | tf_op jit(solution)/shard_map/ppermute | solution.py:461
  17.9 0.3 %collective-permute-done.2 = f32[16,128]{1,0:T(8,128)S(1)} collective-permute-done((f32[16,128]{1,0:T(8,128)S(1)}, f32[16,128]{1,0:T(8,128)S(1)}, u32[]{:S(2)}, u32[]{:S(2)}) %collective-permute-start.2) | collective-permute-done | bytes 8224 | tf_op jit(solution)/shard_map/ppermute | solution.py:461
  18.2 2.5 %collective-permute-start.5 = (f32[16,128]{1,0:T(8,128)S(1)}, f32[16,128]{1,0:T(8,128)S(1)}, u32[]{:S(2)}, u32[]{:S(2)}) collective-permute-start(f32[16,128]{1,0:T(8,128)S(1)} %add_add_fusion), channel_id=1, source_target_pairs={{0,17},{1,16},{2,19},{3,18},{4,21},{5,20},{6,23},{7,22},{8,25},{9,... | collective-permute-start | bytes 24584 | tf_op jit(solution)/shard_map/ppermute | solution.py:461
  20.7 1.5 %collective-permute-done.5 = f32[16,128]{1,0:T(8,128)S(1)} collective-permute-done((f32[16,128]{1,0:T(8,128)S(1)}, f32[16,128]{1,0:T(8,128)S(1)}, u32[]{:S(2)}, u32[]{:S(2)}) %collective-permute-start.5) | collective-permute-done | bytes 8224 | tf_op jit(solution)/shard_map/ppermute | solution.py:461
  22.2 1.9 %last.1 = (f32[48,512]{1,0:T(8,128)}, f32[16,16]{1,0:T(8,128)}, f32[16,16]{1,0:T(8,128)}, f32[1,16]{1,0:T(1,128)}) custom-call(f32[56,512]{1,0:T(8,128)S(1)} %pack.1.own_ref, f32[48,512]{1,0:T(8,128)S(1)} %get-tuple-element.25.prod_ref, f32[48,512]{1,0:T(8,128)S(1)} %get-tuple-element.26.quad_ref, f32[16,128]{1,0:T(8,128)S(1)} %add.15.gram_ref), custom_call_target="tpu_custom_call" | custom-call | tf_op jit(solution)/shard_map/last/pallas_call | solution.py:472
  (2 shorter events, 0.0 us)
Async XLA Ops:
  1.6 4.9 %collective-permute-start = (f32[56,512]{1,0:T(8,128)S(1)}, f32[56,512]{1,0:T(8,128)S(1)}, u32[]{:S(2)}, u32[]{:S(2)}) collective-permute-start(f32[56,512]{1,0:T(8,128)S(1)} %pack.1.own_ref), channel_id=1, source_target_pairs={{5,0},{0,1},{7,2},{2,3},{1,4},{8,5},{3,6},{10,7},{13,8},{4,9},{15,... | collective-permute-start | bytes 344072 | tf_op jit(solution)/shard_map/ppermute | solution.py:398
  7.9 2.2 %collective-permute-start.1 = (f32[56,512]{1,0:T(8,128)S(1)}, f32[56,512]{1,0:T(8,128)S(1)}, u32[]{:S(2)}, u32[]{:S(2)}) collective-permute-start(f32[56,512]{1,0:T(8,128)S(1)} %get-tuple-element.23.prod_ref), channel_id=1, source_target_pairs={{0,1},{1,0},{2,3},{3,2},{4,5},{5,4},{6,7},{7,6},{8,9},{9,8},{10,11... | collective-permute-start | bytes 344072 | tf_op jit(solution)/shard_map/ppermute | solution.py:435
  11.3 4.9 %collective-permute-start.4 = (f32[16,128]{1,0:T(8,128)S(1)}, f32[16,128]{1,0:T(8,128)S(1)}, u32[]{:S(2)}, u32[]{:S(2)}) collective-permute-start(f32[16,128]{1,0:T(8,128)S(1)} %get-tuple-element.27), channel_id=1, source_target_pairs={{0,13},{1,12},{2,15},{3,14},{4,9},{5,8},{6,11},{7,10},{8,5},{9,4},... | collective-permute-start | bytes 24584 | tf_op jit(solution)/shard_map/ppermute | solution.py:461
  14.8 3.1 %collective-permute-start.3 = (f32[16,128]{1,0:T(8,128)S(1)}, f32[16,128]{1,0:T(8,128)S(1)}, u32[]{:S(2)}, u32[]{:S(2)}) collective-permute-start(f32[16,128]{1,0:T(8,128)S(1)} %get-tuple-element.27), channel_id=1, source_target_pairs={{0,9},{1,8},{2,11},{3,10},{4,13},{5,12},{6,15},{7,14},{8,1},{9,0},... | collective-permute-start | bytes 24584 | tf_op jit(solution)/shard_map/ppermute | solution.py:461
  15.1 3.1 %collective-permute-start.2 = (f32[16,128]{1,0:T(8,128)S(1)}, f32[16,128]{1,0:T(8,128)S(1)}, u32[]{:S(2)}, u32[]{:S(2)}) collective-permute-start(f32[16,128]{1,0:T(8,128)S(1)} %get-tuple-element.27), channel_id=1, source_target_pairs={{0,5},{1,4},{2,7},{3,6},{4,1},{5,0},{6,3},{7,2},{8,13},{9,12},{10,... | collective-permute-start | bytes 24584 | tf_op jit(solution)/shard_map/ppermute | solution.py:461
  18.2 4.0 %collective-permute-start.5 = (f32[16,128]{1,0:T(8,128)S(1)}, f32[16,128]{1,0:T(8,128)S(1)}, u32[]{:S(2)}, u32[]{:S(2)}) collective-permute-start(f32[16,128]{1,0:T(8,128)S(1)} %add_add_fusion), channel_id=1, source_target_pairs={{0,17},{1,16},{2,19},{3,18},{4,21},{5,20},{6,23},{7,22},{8,25},{9,... | collective-permute-start | bytes 24584 | tf_op jit(solution)/shard_map/ppermute | solution.py:461

commit v6 on v5

--- a/solution.py
+++ b/solution.py
@@ -23,13 +23,17 @@
     return lax.rem(lax.axis_index("col") + lax.axis_index("tile") + 1, 2)
 
 
-def pack_kernel(vec_ref, pos_ref, tiles_ref, count_ref, out_ref, tiles, count, pos, sems):
+def pack_kernel(vec_ref, pos_ref, tiles_ref, count_ref, near_ref, far_ref, tiles, count, pos, sems):
     rows, width = vec_ref.shape
+    half = width // 2
+    near = pl.ds(pl.multiple_of((1 - parity()) * half, TILE_B), half)
+    far = pl.ds(pl.multiple_of(parity() * half, TILE_B), half)
     copies = [
         pltpu.make_async_copy(tiles_ref, tiles, sems.at[0]),
         pltpu.make_async_copy(count_ref, count, sems.at[1]),
         pltpu.make_async_copy(pos_ref, pos, sems.at[2]),
-        pltpu.make_async_copy(vec_ref, out_ref.at[0:rows], sems.at[3]),
+        pltpu.make_async_copy(vec_ref.at[:, near], near_ref.at[0:rows], sems.at[3]),
+        pltpu.make_async_copy(vec_ref.at[:, far], far_ref, sems.at[4]),
     ]
     for copy in copies:
         copy.start()
@@ -45,10 +49,19 @@
             reach = tiles[1, 0, c, s] - first_tile - row
             row = jnp.where(s < count[0, c], row, -1)
             live += jnp.where((tile_of == row) & (reach_of == reach), cutoff_sq, 0.0)
-    out_ref[rows : rows + 8, :] = live
     copies[2].wait()
-    out_ref[rows : rows + 3, :] = pos[...]
+    for n in range(2):
+        place = slice(rows + 8 * n, rows + 8 * n + 8)
+        part = slice(n * half, (n + 1) * half)
+        near_ref[place, :] = live[:, part]
+        near_ref[rows + 8 * n : rows + 8 * n + 3, :] = pos[:, part]
     copies[3].wait()
+    copies[4].wait()
+
+
+def joined_places(near):
+    rows = near.shape[0] - 16
+    return jnp.concatenate([near[rows : rows + 8, :], near[rows + 8 :, :]], axis=1)
 
 
 def split(x):
@@ -145,18 +158,22 @@
     return jnp.concatenate(out, axis=0)
 
 
-def own_kernel(own_ref, pull, wide, high, low, part_ref):
+def own_kernel(vec_ref, sent_ref, own_ref, pull, wide, high, low, part_ref, sem):
     rows, width = high.shape
+    copy = pltpu.make_async_copy(vec_ref, own_ref.at[0:rows], sem)
+    copy.start()
+    own_ref[rows : rows + 8, :] = joined_places(sent_ref)
     tiles = width // TILE_B
     half = tiles // 2
     own = dict(vec=own_ref.at[0:rows], pos=own_ref.at[rows : rows + 8], high=high, low=low)
     mine = Tiles(lambda u: (own, u))
     wide[...] = spread_places(own["pos"][...])
-    high[...], low[...] = split(own["vec"][...])
     near = [range(max(0, u - REACH), min(tiles, u + REACH + 1)) for u in range(tiles)]
     for u in range(tiles):
         for j in near[u]:
             fill_pull(mine("pos", [u]), mine.bound(u, j), wide, j * TILE_B, pull, u + REACH, j - u + REACH)
+    copy.wait()
+    high[...], low[...] = split(own["vec"][...])
 
     def body(odd):
         for k in range(half):
@@ -166,31 +183,52 @@
     by_parity(body)
 
 
-def first_kernel(
-    own_ref, got_ref, wide_own, high_own, low_own, part_ref, pull_in, out_ref, pull, places, wide_got, high_got, low_got
-):
-    rows, width = high_own.shape
-    tiles = width // TILE_B
-    places[...] = received_places(got_ref[rows : rows + 8, :])
-    out_ref[rows : rows + 8, :] = places[...]
+def outer_kernel(own_ref, got_ref, wide_own, pull_in, pull, places, wide_got):
+    width = wide_own.shape[0]
+    rows = own_ref.shape[0] - 8
+    tiles = width // TILE_B
+    places[...] = received_places(joined_places(got_ref))
     wide_got[...] = spread_places(places[...])
-    high_got[...], low_got[...] = split(got_ref[0:rows, :])
-    own = dict(vec=own_ref.at[0:rows], pos=own_ref.at[rows : rows + 8], high=high_own, low=low_own, wide=wide_own)
-    got = dict(vec=got_ref.at[0:rows], pos=places, high=high_got, low=low_got, wide=wide_got)
+    own = dict(pos=own_ref.at[rows : rows + 8], wide=wide_own)
+    got = dict(pos=places, wide=wide_got)
 
     def body(odd):
         window = Tiles(lambda w: (got if w // tiles == odd else own, w % tiles))
         for r in range(tiles):
             w = r + REACH
-            row = r + odd * tiles
+            for j in range(w - REACH, w + REACH + 1):
+                if w // tiles == odd or j // tiles == odd:
+                    refs, tile = window.place(j)
+                    across, bound = window("pos", [w]), window.bound(w, j)
+                    fill_pull(across, bound, refs["wide"], tile * TILE_B, pull, r + odd * tiles, j - w + REACH)
+
+    by_parity(body)
+
+
+def first_kernel(own_ref, near_ref, far_ref, places, high_own, low_own, part_ref, pull, out_ref, *parts):
+    rows, width = high_own.shape
+    tiles = width // TILE_B
+    half = tiles // 2
+    out_ref[rows : rows + 8, :] = places[...]
+    own = dict(vec=own_ref.at[0:rows], pos=own_ref.at[rows : rows + 8], high=high_own, low=low_own)
+    got = []
+    for vec, high, low in zip((near_ref.at[0:rows], far_ref), parts[0::2], parts[1::2]):
+        high[...], low[...] = split(vec[...])
+        got.append(dict(vec=vec, pos=places, high=high, low=low))
+
+    def body(odd):
+        def place(w):
+            if w // tiles != odd:
+                return own, w % tiles
+            tile = w % tiles
+            return dict(got[0 if tile // half != odd else 1], pos_tile=tile), tile % half
+
+        window = Tiles(place)
+        for r in range(tiles):
+            w = r + REACH
             inner = w // tiles != odd
             near = [j for j in range(w - REACH, w + REACH + 1) if not inner or j // tiles == odd]
-            for j in near:
-                refs, tile = window.place(j)
-                fill_pull(
-                    window("pos", [w]), window.bound(w, j), refs["wide"], tile * TILE_B, pull, row, j - w + REACH
-                )
-            total = sum_pulls(window, w, near, pull.at[row])
+            total = sum_pulls(window, w, near, pull.at[r + odd * tiles])
             if inner:
                 total = total + part_ref[w % tiles - odd * (tiles // 2)]
             out_ref[0:rows, tile_slice(r)] = from_sums(window, w, total)
@@ -232,7 +270,7 @@
     by_parity(body)
 
 
-def second_kernel(own_ref, prod_ref, prod_got_ref, part_ref, pull_in, out_ref, mid_ref, gram_ref, pull, high, low, wide):
+def second_kernel(own_ref, prod_ref, prod_got_ref, part_ref, pull_in, out_ref, mid_ref, gram_ref, pull, high, low, wide, sums):
     rows, width = high.shape
     cols = rows // 3
     tiles = width // TILE_B
@@ -253,11 +291,14 @@
                     fill_pull(
                         window("pos", [w]), window.bound(w, j), wide, (j - start) * TILE_B, pull, w, j - w + REACH
                     )
-            total = part_ref[u] + sum_pulls(window, w, near, pull.at[w])
-            out_ref[:, tile_slice(u)] = from_sums(window, w, total)
+            sums[u] = part_ref[u] + sum_pulls(window, w, near, pull.at[w])
             mid_ref[:, tile_slice(u)] = window("vec", [w])
 
     by_parity(body)
+    own = dict(vec=mid_ref, pos=own_ref.at[rows : rows + 8])
+    mine = Tiles(lambda u: (own, u))
+    for u in range(tiles):
+        out_ref[:, tile_slice(u)] = from_sums(mine, u, sums[u])
     bands = [slice(d * cols, (d + 1) * cols) for d in range(3)]
     joint = jnp.concatenate(
         [jnp.concatenate([own_ref[band, :], mid_ref[band, :], out_ref[band, :]], axis=0) for band in bands], axis=1
@@ -288,8 +329,7 @@
     return jnp.dot(a, b, precision=highest, preferred_element_type=f32)
 
 
-def turned(high, both, vec):
-    vec_high, vec_low = split(vec)
+def turned(high, both, vec_high, vec_low):
     n = high.shape[1]
     first = lax.dot_general(both, vec_high, (((0,), (0,)), ((), ())), preferred_element_type=f32)
     return first[0:n] + (first[n:] + lax.dot_general(high, vec_low, (((0,), (0,)), ((), ())), preferred_element_type=f32))
@@ -325,14 +365,11 @@
     cross = joint[cols:, 2 * cols :]
     corr = xx + rest
     side = xp - 2.0 * rest + cross
-    both = eliminate(jnp.concatenate([corr, side + xp], axis=1), cols)[:, cols:]
-    second = both - shift
     gram = side - mul(rest, shift)
     turn = eye + shift
-    squares = turn * (mul(pp, turn) - 2.0 * pq) + eye * qq - gram * second
+    squares = turn * (mul(pp, turn) - 2.0 * pq) + eye * qq
     ray[...] = gram * (bead_scale / step_size)
     small[...] = corr * bead_scale
-    norm[...] = jnp.sum(squares, axis=0, keepdims=True) * (bead_scale / step_size**2)
     copies = [
         pltpu.make_async_copy(ray, ray_ref, sems.at[0]),
         pltpu.make_async_copy(small, corr_ref, sems.at[1]),
@@ -340,14 +377,20 @@
     ]
     shift_high, shift_low = split(shift)
     shift_both = jnp.concatenate([shift_high, shift_low], axis=1)
+    bands = [slice(d * cols, (d + 1) * cols) for d in range(3)]
+    right = []
+    for band in bands:
+        vec, prod = own_ref[band, :], prod_ref[band, :]
+        moved = turned(shift_high, shift_both, *split(vec))
+        out[band, :] = vec - 2.0 * prod + quad_ref[band, :]
+        right.append(split(jnp.concatenate([vec - prod, moved], axis=0)))
+    both = eliminate(jnp.concatenate([corr, side + xp], axis=1), cols)[:, cols:]
+    second = both - shift
+    norm[...] = jnp.sum(squares - gram * second, axis=0, keepdims=True) * (bead_scale / step_size**2)
     factor_high, factor_low = split(jnp.concatenate([both, second], axis=0))
     factor_both = jnp.concatenate([factor_high, factor_low], axis=1)
-    for d in range(3):
-        band = slice(d * cols, (d + 1) * cols)
-        vec, prod = own_ref[band, :], prod_ref[band, :]
-        moved = turned(shift_high, shift_both, vec)
-        base = vec - 2.0 * prod + quad_ref[band, :]
-        out[band, :] = base + turned(factor_high, factor_both, jnp.concatenate([vec - prod, moved], axis=0))
+    for d, band in enumerate(bands):
+        out[band, :] += turned(factor_high, factor_both, *right[d])
         copies.append(pltpu.make_async_copy(out.at[band], out_ref.at[band], sems.at[3 + d]))
         if d == 0:
             for copy in copies:
@@ -369,24 +412,31 @@
     smem = pl.BlockSpec(memory_space=pltpu.SMEM)
     params = pltpu.CompilerParams(vmem_limit_bytes=24 * 2**20)
 
+    def f32_array(*shape):
+        return jax.ShapeDtypeStruct(shape, f32)
+
+    def bf16_array(*shape):
+        return jax.ShapeDtypeStruct(shape, bf16)
+
     hbm = pl.BlockSpec(memory_space=pltpu.HBM)
-    own = pl.pallas_call(
+    vectors, *tables = [
+        pltpu.with_memory_space_constraint(x, pltpu.HBM)
+        for x in (trial_block.reshape(rows, width), positions, pair_tiles, pair_count)
+    ]
+    near, far = pl.pallas_call(
         pack_kernel,
-        out_shape=jax.ShapeDtypeStruct((rows + 8, width), f32),
+        out_shape=(f32_array(rows + 16, width // 2), f32_array(rows, width // 2)),
         in_specs=[hbm] * 4,
-        out_specs=vmem,
+        out_specs=(vmem,) * 2,
         scratch_shapes=[
             pltpu.SMEM(pair_tiles.shape, jnp.int32),
             pltpu.SMEM(pair_count.shape, jnp.int32),
             pltpu.VMEM(positions.shape, f32),
-            pltpu.SemaphoreType.DMA((4,)),
+            pltpu.SemaphoreType.DMA((5,)),
         ],
         compiler_params=pltpu.CompilerParams(vmem_limit_bytes=4 * 2**20),
         name="pack",
-    )(*[
-        pltpu.with_memory_space_constraint(x, pltpu.HBM)
-        for x in (trial_block.reshape(rows, width), positions, pair_tiles, pair_count)
-    ])
+    )(vectors, *tables)
 
     halo = []
     for t in range(n_tile):
@@ -395,47 +445,54 @@
             if not 0 <= source < n_tile:
                 source = t
             halo.append((source * n_col + (c ^ 1), t * n_col + c))
-    got = lax.ppermute(own, ("tile", "col"), halo)
-
-    def f32_array(*shape):
-        return jax.ShapeDtypeStruct(shape, f32)
-
-    def bf16_array(*shape):
-        return jax.ShapeDtypeStruct(shape, bf16)
+    got_near = lax.ppermute(near, ("tile", "col"), halo)
+    got_far = lax.ppermute(far, ("tile", "col"), halo)
 
     parts = [pltpu.VMEM((rows, width), bf16)] * 2
-    sums = rows + cols + 16
+    sums = (rows + cols + 16, 3 * TILE_B)
     pulls = bf16_array(2 * tiles, (2 * REACH + 1) * TILE_B, 3 * TILE_B)
     hidden = pl.CostEstimate(flops=10**8, bytes_accessed=10**6, transcendentals=0)
-    pull, wide, high, low, part = pl.pallas_call(
+    own, pull, wide, high, low, part = pl.pallas_call(
         own_kernel,
         out_shape=(
+            f32_array(rows + 8, width),
             pulls,
             f32_array(width, 3 * TILE_B),
             bf16_array(rows, width),
             bf16_array(rows, width),
-            f32_array(tiles // 2, sums, 3 * TILE_B),
+            f32_array(tiles // 2, *sums),
         ),
-        in_specs=[vmem],
-        out_specs=(vmem,) * 5,
+        in_specs=[hbm, vmem],
+        out_specs=(vmem,) * 6,
+        scratch_shapes=[pltpu.SemaphoreType.DMA(())],
         compiler_params=params,
         cost_estimate=hidden,
         name="own_pulls",
-    )(own)
-    prod, pull = pl.pallas_call(
+    )(vectors, near)
+    pull, places = pl.pallas_call(
+        outer_kernel,
+        out_shape=(pulls, f32_array(8, width)),
+        in_specs=[vmem] * 4,
+        out_specs=(vmem,) * 2,
+        input_output_aliases={3: 0},
+        scratch_shapes=[pltpu.VMEM((width, 3 * TILE_B), f32)],
+        compiler_params=params,
+        cost_estimate=hidden,
+        name="outer_pulls",
+    )(own, got_near, wide, pull)
+    prod = pl.pallas_call(
         first_kernel,
-        out_shape=(f32_array(rows + 8, width), pulls),
-        in_specs=[vmem] * 7,
-        out_specs=(vmem,) * 2,
-        input_output_aliases={6: 1},
-        scratch_shapes=[pltpu.VMEM((8, width), f32), pltpu.VMEM((width, 3 * TILE_B), f32)] + parts,
+        out_shape=f32_array(rows + 8, width),
+        in_specs=[vmem] * 8,
+        out_specs=vmem,
+        scratch_shapes=[pltpu.VMEM((rows, width // 2), bf16)] * 4,
         compiler_params=params,
         name="first",
-    )(own, got, wide, high, low, part, pull)
+    )(own, got_near, got_far, places, high, low, part, pull)
     prod_got = lax.ppermute(prod, "col", [(c, c ^ 1) for c in range(n_col)])
     part = pl.pallas_call(
         middle_kernel,
-        out_shape=f32_array(tiles, sums, 3 * TILE_B),
+        out_shape=f32_array(tiles, *sums),
         in_specs=[vmem] * 3,
         out_specs=vmem,
         scratch_shapes=parts,
@@ -449,7 +506,7 @@
         in_specs=[vmem] * 5,
         out_specs=(vmem,) * 4,
         input_output_aliases={4: 3},
-        scratch_shapes=parts + [pltpu.VMEM((REACH * TILE_B, 3 * TILE_B), f32)],
+        scratch_shapes=parts + [pltpu.VMEM((REACH * TILE_B, 3 * TILE_B), f32), pltpu.VMEM((tiles, *sums), f32)],
         compiler_params=params,
         name="second",
     )(own, prod, prod_got, part, pull)

time: 24.3 us -> 23.4 us (0.963)
  waiting for transfers between devices: 8.07 us -> 4.8 us
  starting transfers between devices: 8.19 us -> 10.7 us
    ppermute x1 -> x2, waiting for transfers between devices: 3.19 us -> 0.01 us  [the longest x1 0.01 us: per_device(): got_near = lax.ppermute(near, ('tile', 'col'), halo)]
    ppermute x1 -> x2, starting transfers between devices: 0.5 us -> 3.13 us  [the longest x1 2.63 us: per_device(): got_far = lax.ppermute(far, ('tile', 'col'), halo)]
    pallas_call x1, Pallas kernels: 1.92 us -> 1.65 us  [per_device(): pl.pallas_call(functools.partial(last_kernel, bead_scale), out_shape=tupl...]
    pallas_call x4 -> x5, Pallas kernels: 4.06 us -> 4.09 us  [the longest x1 1.3 us: per_device(): pl.pallas_call(own_kernel, out_shape=(f32_array(rows + 8, width), pulls,...]
  transfers between devices with their start and end apart: 6 -> 7, of which waited for: 6 -> 5; matrix products, arithmetic and copies ran while one was open for 0% -> 0% of each run, Pallas kernels for 7% -> 11%
where the time goes in v6:
time: 23.4 us; the launch traced here: 23.2 us
  starting transfers between devices  10.7 us (46%)
  Pallas kernels  7.03 us (30%)
  waiting for transfers between devices  4.8 us (21%)
  between operations  0.69 us (3%)
    ppermute x4, starting transfers between devices, crossed(): return lax.ppermute(x, ('tile', 'col'), route)  6.52 us
    ppermute x4, waiting for transfers between devices, crossed(): return lax.ppermute(x, ('tile', 'col'), route)  4.3 us
    ppermute x1, starting transfers between devices, per_device(): got_far = lax.ppermute(far, ('tile', 'col'), halo)  2.63 us
    pallas_call x1, Pallas kernels, per_device(): pl.pallas_call(functools.partial(last_kernel, bead_scale), out_shape=tupl...  1.65 us
    pallas_call x1, Pallas kernels, per_device(): pl.pallas_call(own_kernel, out_shape=(f32_array(rows + 8, width), pulls,...  1.3 us
    pallas_call x1, Pallas kernels, per_device(): pl.pallas_call(second_kernel, out_shape=(f32_array(rows, width), f32_arra...  1.28 us
    ppermute x1, starting transfers between devices, per_device(): prod_got = lax.ppermute(prod, 'col', [(c, c ^ 1) for c in range(n_col)])  1.04 us
    pallas_call x1, Pallas kernels, per_device(): pl.pallas_call(pack_kernel, out_shape=(f32_array(rows + 16, width // 2),...  0.89 us
  transfers between devices with their start and end apart: 7, of which 5 were waited for; matrix products, arithmetic and copies ran while one was open for 0% of the time, Pallas kernels for 11%

profile of v6, /device:TPU:0, one launch (start us, length us, event | category | flops | bytes accessed | tf_op | source)
XLA Modules:
  0.0 23.2 jit_solution(17333162446338783775)
XLA Ops:
  0.6 0.9 %pack.1 = (f32[64,256]{1,0:T(8,128)S(1)}, f32[48,256]{1,0:T(8,128)S(1)}) custom-call(f32[48,512]{1,0:T(8,128)} %bitcast.3, f32[3,512]{1,0:T(4,128)} %pos_ref.1, s32[2,1,4,8]{3,2,1,0:T(4,128)} %tiles_ref.1, s32[1,4]{1,0:T(1,128)} %count_ref.1), custom_call_target="tpu_custom_call" | custom-call | tf_op jit(solution)/shard_map/pack/pallas_call | solution.py:426
  1.5 0.5 %collective-permute-start = (f32[64,256]{1,0:T(8,128)S(1)}, f32[64,256]{1,0:T(8,128)S(1)}, u32[]{:S(2)}, u32[]{:S(2)}) collective-permute-start(f32[64,256]{1,0:T(8,128)S(1)} %get-tuple-element.21.sent_ref), channel_id=1, source_target_pairs={{5,0},{0,1},{7,2},{2,3},{1,4},{8,5},{3,6},{10,7},{13,8},{4,9},{15,... | collective-permute-start | bytes 196616 | tf_op jit(solution)/shard_map/ppermute | solution.py:448
  2.0 2.6 %collective-permute-start.1 = (f32[48,256]{1,0:T(8,128)S(1)}, f32[48,256]{1,0:T(8,128)S(1)}, u32[]{:S(2)}, u32[]{:S(2)}) collective-permute-start(f32[48,256]{1,0:T(8,128)S(1)} %get-tuple-element.23), channel_id=1, source_target_pairs={{5,0},{0,1},{7,2},{2,3},{1,4},{8,5},{3,6},{10,7},{13,8},{4,9},{15,... | collective-permute-start | bytes 147464 | tf_op jit(solution)/shard_map/ppermute | solution.py:449
  4.7 1.3 %own_pulls.1 = (f32[56,512]{1,0:T(8,128)S(1)}, bf16[8,640,384]{2,1,0:T(8,128)(2,1)S(1)}, f32[512,384]{1,0:T(8,128)S(1)}, bf16[48,512]{1,0:T(8,128)(2,1)S(1)}, bf...) custom-call(f32[48,512]{1,0:T(8,128)} %bitcast.4, f32[64,256]{1,0:T(8,128)S(1)} %get-tuple-element.21.sent_ref), custom_call_target="tpu_custom_call" | custom-call | flops 100000000 | bytes 1000000 | tf_op jit(solution)/shard_map/own_pulls/pallas_call | solution.py:455
  6.0 0.0 collective-permute-done.got_ref.near_ref
  6.0 0.9 %outer_pulls.1 = (bf16[8,640,384]{2,1,0:T(8,128)(2,1)S(1)}, f32[8,512]{1,0:T(8,128)S(1)}) custom-call(f32[56,512]{1,0:T(8,128)S(1)} %get-tuple-element.22.own_ref, f32[64,256]{1,0:T(8,128)S(1)} %collective-permute-done.got_ref.near_ref, f32[512,384]{1,0:T(8,128)S(1)} %get-tuple-element.24.wide_own, ...), custom_call_target="tpu_custom_call", output_to_operand_aliasing={{0}: (3, {})} | custom-call | flops 100000000 | bytes 1000000 | tf_op jit(solution)/shard_map/outer_pulls/pallas_call | solution.py:472
  6.9 0.0 collective-permute-done.1.far_ref
  6.9 0.6 %first.1.prod_ref = f32[56,512]{1,0:T(8,128)S(1)} custom-call(f32[56,512]{1,0:T(8,128)S(1)} %get-tuple-element.22.own_ref, f32[64,256]{1,0:T(8,128)S(1)} %collective-permute-done.got_ref.near_ref, f32[48,256]{1,0:T(8,128)S(1)} %collective-permute-done.1.far_ref, f32[8,512]{1,0:T(8,128)S(1)} %get-tuple-element.26.places, ...), custom_call_target="tpu_custom_call" | custom-call | tf_op jit(solution)/shard_map/first/pallas_call | solution.py:483
  7.4 1.0 %collective-permute-start.2 = (f32[56,512]{1,0:T(8,128)S(1)}, f32[56,512]{1,0:T(8,128)S(1)}, u32[]{:S(2)}, u32[]{:S(2)}) collective-permute-start(f32[56,512]{1,0:T(8,128)S(1)} %first.1.prod_ref), channel_id=1, source_target_pairs={{0,1},{1,0},{2,3},{3,2},{4,5},{5,4},{6,7},{7,6},{8,9},{9,8},{10,11... | collective-permute-start | bytes 344072 | tf_op jit(solution)/shard_map/ppermute | solution.py:492
  8.5 0.5 %middle.1.part_ref = f32[4,80,384]{2,1,0:T(8,128)S(1)} custom-call(f32[56,512]{1,0:T(8,128)S(1)} %get-tuple-element.22.own_ref, f32[56,512]{1,0:T(8,128)S(1)} %first.1.prod_ref, bf16[8,640,384]{2,1,0:T(8,128)(2,1)S(1)} %get-tuple-element.30.pull.pull_in), custom_call_target="tpu_custom_call" | custom-call | flops 100000000 | bytes 1000000 | tf_op jit(solution)/shard_map/middle/pallas_call | solution.py:493
  9.0 0.5 %collective-permute-done.2.prod_got_ref = f32[56,512]{1,0:T(8,128)S(1)} collective-permute-done((f32[56,512]{1,0:T(8,128)S(1)}, f32[56,512]{1,0:T(8,128)S(1)}, u32[]{:S(2)}, u32[]{:S(2)}) %collective-permute-start.2) | collective-permute-done | bytes 114720 | tf_op jit(solution)/shard_map/ppermute | solution.py:492
  9.4 1.3 %second.1 = (f32[48,512]{1,0:T(8,128)S(1)}, f32[48,512]{1,0:T(8,128)S(1)}, f32[16,128]{1,0:T(8,128)S(1)}, bf16[8,640,384]{2,1,0:T(8,128)(2,1)S(1)}) custom-call(f32[56,512]{1,0:T(8,128)S(1)} %get-tuple-element.22.own_ref, f32[56,512]{1,0:T(8,128)S(1)} %first.1.prod_ref, ...), custom_call_target="tpu_custom_call", output_to_operand_aliasing={{3}: (4, {})} | custom-call | tf_op jit(solution)/shard_map/second/pallas_call | solution.py:503
  10.7 3.5 %collective-permute-start.5 = (f32[16,128]{1,0:T(8,128)S(1)}, f32[16,128]{1,0:T(8,128)S(1)}, u32[]{:S(2)}, u32[]{:S(2)}) collective-permute-start(f32[16,128]{1,0:T(8,128)S(1)} %get-tuple-element.33), channel_id=1, source_target_pairs={{0,13},{1,12},{2,15},{3,14},{4,9},{5,8},{6,11},{7,10},{8,5},{9,4},... | collective-permute-start | bytes 24584 | tf_op jit(solution)/shard_map/ppermute | solution.py:518
  14.2 0.3 %collective-permute-start.4 = (f32[16,128]{1,0:T(8,128)S(1)}, f32[16,128]{1,0:T(8,128)S(1)}, u32[]{:S(2)}, u32[]{:S(2)}) collective-permute-start(f32[16,128]{1,0:T(8,128)S(1)} %get-tuple-element.33), channel_id=1, source_target_pairs={{0,9},{1,8},{2,11},{3,10},{4,13},{5,12},{6,15},{7,14},{8,1},{9,0},... | collective-permute-start | bytes 24584 | tf_op jit(solution)/shard_map/ppermute | solution.py:518
  14.5 0.3 %collective-permute-start.3 = (f32[16,128]{1,0:T(8,128)S(1)}, f32[16,128]{1,0:T(8,128)S(1)}, u32[]{:S(2)}, u32[]{:S(2)}) collective-permute-start(f32[16,128]{1,0:T(8,128)S(1)} %get-tuple-element.33), channel_id=1, source_target_pairs={{0,5},{1,4},{2,7},{3,6},{4,1},{5,0},{6,3},{7,2},{8,13},{9,12},{10,... | collective-permute-start | bytes 24584 | tf_op jit(solution)/shard_map/ppermute | solution.py:518
  14.7 0.9 %collective-permute-done.5 = f32[16,128]{1,0:T(8,128)S(1)} collective-permute-done((f32[16,128]{1,0:T(8,128)S(1)}, f32[16,128]{1,0:T(8,128)S(1)}, u32[]{:S(2)}, u32[]{:S(2)}) %collective-permute-start.5) | collective-permute-done | bytes 8224 | tf_op jit(solution)/shard_map/ppermute | solution.py:518
  15.6 1.7 %collective-permute-done.4 = f32[16,128]{1,0:T(8,128)S(1)} collective-permute-done((f32[16,128]{1,0:T(8,128)S(1)}, f32[16,128]{1,0:T(8,128)S(1)}, u32[]{:S(2)}, u32[]{:S(2)}) %collective-permute-start.4) | collective-permute-done | bytes 8224 | tf_op jit(solution)/shard_map/ppermute | solution.py:518
  17.3 0.3 %collective-permute-done.3 = f32[16,128]{1,0:T(8,128)S(1)} collective-permute-done((f32[16,128]{1,0:T(8,128)S(1)}, f32[16,128]{1,0:T(8,128)S(1)}, u32[]{:S(2)}, u32[]{:S(2)}) %collective-permute-start.3) | collective-permute-done | bytes 8224 | tf_op jit(solution)/shard_map/ppermute | solution.py:518
  17.6 2.5 %collective-permute-start.6 = (f32[16,128]{1,0:T(8,128)S(1)}, f32[16,128]{1,0:T(8,128)S(1)}, u32[]{:S(2)}, u32[]{:S(2)}) collective-permute-start(f32[16,128]{1,0:T(8,128)S(1)} %add_add_fusion), channel_id=1, source_target_pairs={{0,17},{1,16},{2,19},{3,18},{4,21},{5,20},{6,23},{7,22},{8,25},{9,... | collective-permute-start | bytes 24584 | tf_op jit(solution)/shard_map/ppermute | solution.py:518
  20.1 1.5 %collective-permute-done.6 = f32[16,128]{1,0:T(8,128)S(1)} collective-permute-done((f32[16,128]{1,0:T(8,128)S(1)}, f32[16,128]{1,0:T(8,128)S(1)}, u32[]{:S(2)}, u32[]{:S(2)}) %collective-permute-start.6) | collective-permute-done | bytes 8224 | tf_op jit(solution)/shard_map/ppermute | solution.py:518
  21.6 1.7 %last.1 = (f32[48,512]{1,0:T(8,128)}, f32[16,16]{1,0:T(8,128)}, f32[16,16]{1,0:T(8,128)}, f32[1,16]{1,0:T(1,128)}) custom-call(f32[56,512]{1,0:T(8,128)S(1)} %get-tuple-element.22.own_ref, f32[48,512]{1,0:T(8,128)S(1)} %get-tuple-element.31.prod_ref, f32[48,512]{1,0:T(8,128)S(1)} %get-tuple-element.32.quad_ref, f32[16,128]{1,0:T(8,128)S(1)} %add.15.gram_ref), custom_call_target="tpu_custom_call" | custom-call | tf_op jit(solution)/shard_map/last/pallas_call | solution.py:529
  (2 shorter events, 0.0 us)
Async XLA Ops:
  1.5 4.4 %collective-permute-start = (f32[64,256]{1,0:T(8,128)S(1)}, f32[64,256]{1,0:T(8,128)S(1)}, u32[]{:S(2)}, u32[]{:S(2)}) collective-permute-start(f32[64,256]{1,0:T(8,128)S(1)} %get-tuple-element.21.sent_ref), channel_id=1, source_target_pairs={{5,0},{0,1},{7,2},{2,3},{1,4},{8,5},{3,6},{10,7},{13,8},{4,9},{15,... | collective-permute-start | bytes 196616 | tf_op jit(solution)/shard_map/ppermute | solution.py:448
  2.0 4.8 %collective-permute-start.1 = (f32[48,256]{1,0:T(8,128)S(1)}, f32[48,256]{1,0:T(8,128)S(1)}, u32[]{:S(2)}, u32[]{:S(2)}) collective-permute-start(f32[48,256]{1,0:T(8,128)S(1)} %get-tuple-element.23), channel_id=1, source_target_pairs={{5,0},{0,1},{7,2},{2,3},{1,4},{8,5},{3,6},{10,7},{13,8},{4,9},{15,... | collective-permute-start | bytes 147464 | tf_op jit(solution)/shard_map/ppermute | solution.py:449
  7.4 2.0 %collective-permute-start.2 = (f32[56,512]{1,0:T(8,128)S(1)}, f32[56,512]{1,0:T(8,128)S(1)}, u32[]{:S(2)}, u32[]{:S(2)}) collective-permute-start(f32[56,512]{1,0:T(8,128)S(1)} %first.1.prod_ref), channel_id=1, source_target_pairs={{0,1},{1,0},{2,3},{3,2},{4,5},{5,4},{6,7},{7,6},{8,9},{9,8},{10,11... | collective-permute-start | bytes 344072 | tf_op jit(solution)/shard_map/ppermute | solution.py:492
  10.7 4.9 %collective-permute-start.5 = (f32[16,128]{1,0:T(8,128)S(1)}, f32[16,128]{1,0:T(8,128)S(1)}, u32[]{:S(2)}, u32[]{:S(2)}) collective-permute-start(f32[16,128]{1,0:T(8,128)S(1)} %get-tuple-element.33), channel_id=1, source_target_pairs={{0,13},{1,12},{2,15},{3,14},{4,9},{5,8},{6,11},{7,10},{8,5},{9,4},... | collective-permute-start | bytes 24584 | tf_op jit(solution)/shard_map/ppermute | solution.py:518
  14.2 3.1 %collective-permute-start.4 = (f32[16,128]{1,0:T(8,128)S(1)}, f32[16,128]{1,0:T(8,128)S(1)}, u32[]{:S(2)}, u32[]{:S(2)}) collective-permute-start(f32[16,128]{1,0:T(8,128)S(1)} %get-tuple-element.33), channel_id=1, source_target_pairs={{0,9},{1,8},{2,11},{3,10},{4,13},{5,12},{6,15},{7,14},{8,1},{9,0},... | collective-permute-start | bytes 24584 | tf_op jit(solution)/shard_map/ppermute | solution.py:518
  14.5 3.1 %collective-permute-start.3 = (f32[16,128]{1,0:T(8,128)S(1)}, f32[16,128]{1,0:T(8,128)S(1)}, u32[]{:S(2)}, u32[]{:S(2)}) collective-permute-start(f32[16,128]{1,0:T(8,128)S(1)} %get-tuple-element.33), channel_id=1, source_target_pairs={{0,5},{1,4},{2,7},{3,6},{4,1},{5,0},{6,3},{7,2},{8,13},{9,12},{10,... | collective-permute-start | bytes 24584 | tf_op jit(solution)/shard_map/ppermute | solution.py:518
  17.6 4.0 %collective-permute-start.6 = (f32[16,128]{1,0:T(8,128)S(1)}, f32[16,128]{1,0:T(8,128)S(1)}, u32[]{:S(2)}, u32[]{:S(2)}) collective-permute-start(f32[16,128]{1,0:T(8,128)S(1)} %add_add_fusion), channel_id=1, source_target_pairs={{0,17},{1,16},{2,19},{3,18},{4,21},{5,20},{6,23},{7,22},{8,25},{9,... | collective-permute-start | bytes 24584 | tf_op jit(solution)/shard_map/ppermute | solution.py:518

commit v7 on v6

--- a/solution.py
+++ b/solution.py
@@ -205,97 +205,165 @@
     by_parity(body)
 
 
-def first_kernel(own_ref, near_ref, far_ref, places, high_own, low_own, part_ref, pull, out_ref, *parts):
+def halo_tiles(own, near, far, odd):
+    rows, width = own["vec"].shape
+    tiles = width // TILE_B
+    half = tiles // 2
+
+    def place(w):
+        tile = w % tiles
+        if w // tiles != odd:
+            return own, tile
+        return dict(far if tile // half == odd else near, pos_tile=tile), tile % half
+
+    return Tiles(place)
+
+
+def is_far(w, tiles, odd):
+    return w // tiles == odd and w % tiles // (tiles // 2) == odd
+
+
+def inner_kernel(own_ref, near_ref, places, high_own, low_own, part_ref, pull, out_ref, outer_ref, high, low):
     rows, width = high_own.shape
     tiles = width // TILE_B
     half = tiles // 2
-    out_ref[rows : rows + 8, :] = places[...]
+    edge = half * TILE_B
+    out_ref[rows : rows + 8, :] = places[:, 0:edge]
+    out_ref[rows + 8 :, :] = places[:, edge:]
+    high[...], low[...] = split(near_ref[0:rows, :])
     own = dict(vec=own_ref.at[0:rows], pos=own_ref.at[rows : rows + 8], high=high_own, low=low_own)
-    got = []
-    for vec, high, low in zip((near_ref.at[0:rows], far_ref), parts[0::2], parts[1::2]):
-        high[...], low[...] = split(vec[...])
-        got.append(dict(vec=vec, pos=places, high=high, low=low))
+    got = dict(vec=near_ref.at[0:rows], pos=places, high=high, low=low)
 
     def body(odd):
-        def place(w):
-            if w // tiles != odd:
-                return own, w % tiles
-            tile = w % tiles
-            return dict(got[0 if tile // half != odd else 1], pos_tile=tile), tile % half
-
-        window = Tiles(place)
+        window = halo_tiles(own, got, None, odd)
         for r in range(tiles):
             w = r + REACH
-            inner = w // tiles != odd
-            near = [j for j in range(w - REACH, w + REACH + 1) if not inner or j // tiles == odd]
-            total = sum_pulls(window, w, near, pull.at[r + odd * tiles])
-            if inner:
-                total = total + part_ref[w % tiles - odd * (tiles // 2)]
-            out_ref[0:rows, tile_slice(r)] = from_sums(window, w, total)
+            near = [j for j in range(w - REACH, w + REACH + 1) if not is_far(j, tiles, odd)]
+            if w // tiles == odd:
+                outer_ref[r % half] = sum_pulls(window, w, near, pull.at[r + odd * tiles])
+            else:
+                near = [j for j in near if j // tiles == odd]
+                total = part_ref[r % half] + sum_pulls(window, w, near, pull.at[r + odd * tiles])
+                out_ref[0:rows, tile_slice(r % half)] = from_sums(window, w, total)
 
     by_parity(body)
 
 
-def near_tiles(own_ref, ours, theirs, odd):
-    rows, width = ours["vec"].shape
-    tiles = width // TILE_B
-    sides = (ours, theirs) if odd == 0 else (theirs, ours)
+def outer_rows_kernel(own_ref, near_ref, far_ref, places, outer_ref, pull, out_ref, high, low):
+    rows, width = own_ref.shape[0] - 8, own_ref.shape[1]
+    tiles = width // TILE_B
+    half = tiles // 2
+    high[...], low[...] = split(far_ref[...])
+    own = dict(vec=own_ref.at[0:rows])
+    near_refs = dict(vec=near_ref.at[0:rows], pos=places)
+    far_refs = dict(vec=far_ref, pos=places, high=high, low=low)
+
+    def body(odd):
+        window = halo_tiles(own, near_refs, far_refs, odd)
+        for r in range(odd * half, (1 + odd) * half):
+            w = r + REACH
+            far = [j for j in range(w - REACH, w + REACH + 1) if is_far(j, tiles, odd)]
+            total = outer_ref[r % half] + sum_pulls(window, w, far, pull.at[r + odd * tiles])
+            out_ref[:, tile_slice(r % half)] = from_sums(window, w, total)
+
+    by_parity(body)
+
+
+def beside_tiles(own_pos, places, vectors, side):
+    tiles = own_pos.shape[1] // TILE_B
+    beside = dict(vectors, pos=places[1 - side])
 
     def place(w):
-        side = sides[w // tiles]
-        if w < REACH:
-            pos, tile = sides[0]["got"], w + tiles - REACH
-        elif w < tiles + REACH:
-            pos, tile = own_ref.at[rows : rows + 8], w - REACH
-        else:
-            pos, tile = sides[1]["got"], w - tiles - REACH
-        return dict(side, pos=pos, pos_tile=tile), w % tiles
+        if REACH <= w < tiles + REACH:
+            return dict(pos=own_pos), w - REACH
+        return beside, w if side == 0 else w - tiles - REACH
 
     return Tiles(place)
 
 
-def middle_kernel(own_ref, prod_ref, pull, part_ref, high, low):
-    rows, width = high.shape
-    tiles = width // TILE_B
+def beside_rows(tiles, side):
+    half = tiles // 2
+    there = range(REACH) if side == 0 else range(tiles + REACH, tiles + 2 * REACH)
+    for u in range(side * half, (1 + side) * half):
+        yield u, [j for j in there if abs(j - u - REACH) <= REACH]
+
+
+def places_of(ref):
+    rows = ref.shape[0] - 16
+    return ref.at[rows : rows + 8], ref.at[rows + 8 :]
+
+
+def own_sums_kernel(own_ref, prod_ref, outer_ref, pull, part_ref, edge_ref, high, low, high_outer, low_outer):
+    rows, width = own_ref.shape[0] - 8, own_ref.shape[1]
+    tiles = width // TILE_B
+    half = tiles // 2
+    own_pos = own_ref.at[rows : rows + 8]
     high[...], low[...] = split(prod_ref[0:rows, :])
-    ours = dict(vec=prod_ref.at[0:rows], got=prod_ref.at[rows : rows + 8], high=high, low=low)
+    high_outer[...], low_outer[...] = split(outer_ref[...])
 
     def body(odd):
-        window = near_tiles(own_ref, ours, ours, odd)
+        inner = dict(vec=prod_ref.at[0:rows], high=high, low=low)
+        inner_sums(own_pos, inner, odd, pull, part_ref)
+        ours = dict(vec=outer_ref, high=high_outer, low=low_outer)
+        window = beside_tiles(own_pos, places_of(prod_ref), ours, odd)
+        for u, near in beside_rows(tiles, odd):
+            edge_ref[u % half] = sum_pulls(window, u + REACH, near, pull.at[u + REACH])
+
+    by_parity(body)
+
+
+def inner_sums(own_pos, inner, side, pull, part_ref):
+    tiles = own_pos.shape[1] // TILE_B
+    half = tiles // 2
+    window = Tiles(lambda u: (dict(inner, pos=own_pos, pos_tile=u), u % half))
+    for u in range(tiles):
+        near = [j for j in range(side * half, (1 + side) * half) if abs(j - u) <= REACH]
+        part_ref[u] = sum_pulls(window, u, near, pull.at[u + REACH])
+
+
+def middle_kernel(own_ref, prod_ref, got_ref, ours_ref, edge_ref, pull_in, mid_ref, part_ref, pull, high, low, wide):
+    rows, width = mid_ref.shape
+    tiles = width // TILE_B
+    half = tiles // 2
+    edge = width // 2
+    own_pos = own_ref.at[rows : rows + 8]
+    high[...], low[...] = split(got_ref[0:rows, :])
+
+    def body(odd):
+        side = 1 - odd
+        mid_ref[:, odd * edge : (1 + odd) * edge] = prod_ref[0:rows, :]
+        mid_ref[:, side * edge : (1 + side) * edge] = got_ref[0:rows, :]
+        window = beside_tiles(own_pos, places_of(got_ref), {}, side)
+        first = side * (tiles + REACH)
+        wide[...] = spread_places(window("pos", range(first, first + REACH)))
+        for u, near in beside_rows(tiles, side):
+            w = u + REACH
+            for j in near:
+                fill_pull(window("pos", [w]), window.bound(w, j), wide, (j - first) * TILE_B, pull, w, j - w + REACH)
+        inner = dict(vec=got_ref.at[0:rows], high=high, low=low)
+        inner_sums(own_pos, inner, side, pull, part_ref)
         for u in range(tiles):
-            w = u + REACH
-            near = [j for j in range(w - REACH, w + REACH + 1) if j // tiles == odd]
-            part_ref[u] = sum_pulls(window, w, near, pull.at[w])
+            total = ours_ref[u] + part_ref[u]
+            part_ref[u] = total + edge_ref[u % half] if u // half == odd else total
 
     by_parity(body)
 
 
-def second_kernel(own_ref, prod_ref, prod_got_ref, part_ref, pull_in, out_ref, mid_ref, gram_ref, pull, high, low, wide, sums):
-    rows, width = high.shape
+def second_kernel(own_ref, mid_ref, got_ref, outer_ref, pull, sums_in, out_ref, gram_ref, sums, high, low):
+    rows, width = mid_ref.shape
     cols = rows // 3
     tiles = width // TILE_B
-    edge = REACH * TILE_B
-    high[...], low[...] = split(prod_got_ref[0:rows, :])
-    ours = dict(vec=prod_ref.at[0:rows], got=prod_ref.at[rows : rows + 8])
-    theirs = dict(vec=prod_got_ref.at[0:rows], got=prod_got_ref.at[rows : rows + 8], high=high, low=low)
+    own_pos = own_ref.at[rows : rows + 8]
+    high[...], low[...] = split(outer_ref[...])
 
     def body(odd):
-        window = near_tiles(own_ref, ours, theirs, odd)
-        start = (1 - odd) * (tiles + REACH)
-        wide[...] = spread_places(window("pos", range(start, start + REACH)))
-        for u in range(tiles):
-            w = u + REACH
-            near = [j for j in range(w - REACH, w + REACH + 1) if j // tiles != odd]
-            for j in near:
-                if start <= j < start + REACH:
-                    fill_pull(
-                        window("pos", [w]), window.bound(w, j), wide, (j - start) * TILE_B, pull, w, j - w + REACH
-                    )
-            sums[u] = part_ref[u] + sum_pulls(window, w, near, pull.at[w])
-            mid_ref[:, tile_slice(u)] = window("vec", [w])
+        theirs = dict(vec=outer_ref, high=high, low=low)
+        window = beside_tiles(own_pos, places_of(got_ref), theirs, 1 - odd)
+        for u, near in beside_rows(tiles, 1 - odd):
+            sums[u] = sums[u] + sum_pulls(window, u + REACH, near, pull.at[u + REACH])
 
     by_parity(body)
-    own = dict(vec=mid_ref, pos=own_ref.at[rows : rows + 8])
+    own = dict(vec=mid_ref, pos=own_pos)
     mine = Tiles(lambda u: (own, u))
     for u in range(tiles):
         out_ref[:, tile_slice(u)] = from_sums(mine, u, sums[u])
@@ -412,6 +480,9 @@
     smem = pl.BlockSpec(memory_space=pltpu.SMEM)
     params = pltpu.CompilerParams(vmem_limit_bytes=24 * 2**20)
 
+    def swapped(x):
+        return lax.ppermute(x, "col", [(c, c ^ 1) for c in range(n_col)])
+
     def f32_array(*shape):
         return jax.ShapeDtypeStruct(shape, f32)
 
@@ -480,36 +551,59 @@
         cost_estimate=hidden,
         name="outer_pulls",
     )(own, got_near, wide, pull)
-    prod = pl.pallas_call(
-        first_kernel,
-        out_shape=f32_array(rows + 8, width),
-        in_specs=[vmem] * 8,
+    half_parts = [pltpu.VMEM((rows, width // 2), bf16)] * 2
+    prod, outer = pl.pallas_call(
+        inner_kernel,
+        out_shape=(f32_array(rows + 16, width // 2), f32_array(tiles // 2, *sums)),
+        in_specs=[vmem] * 7,
+        out_specs=(vmem,) * 2,
+        scratch_shapes=half_parts,
+        compiler_params=params,
+        cost_estimate=hidden,
+        name="inner",
+    )(own, got_near, places, high, low, part, pull)
+    prod_got = swapped(prod)
+    outer = pl.pallas_call(
+        outer_rows_kernel,
+        out_shape=f32_array(rows, width // 2),
+        in_specs=[vmem] * 6,
         out_specs=vmem,
-        scratch_shapes=[pltpu.VMEM((rows, width // 2), bf16)] * 4,
-        compiler_params=params,
-        name="first",
-    )(own, got_near, got_far, places, high, low, part, pull)
-    prod_got = lax.ppermute(prod, "col", [(c, c ^ 1) for c in range(n_col)])
-    part = pl.pallas_call(
+        scratch_shapes=half_parts,
+        compiler_params=params,
+        name="outer_rows",
+    )(own, got_near, got_far, places, outer, pull)
+    outer_got = swapped(outer)
+    part, edge = pl.pallas_call(
+        own_sums_kernel,
+        out_shape=(f32_array(tiles, *sums), f32_array(tiles // 2, *sums)),
+        in_specs=[vmem] * 4,
+        out_specs=(vmem,) * 2,
+        scratch_shapes=half_parts * 2,
+        compiler_params=params,
+        cost_estimate=hidden,
+        name="own_sums",
+    )(own, prod, outer, pull)
+    mid, part, pull = pl.pallas_call(
         middle_kernel,
-        out_shape=f32_array(tiles, *sums),
-        in_specs=[vmem] * 3,
-        out_specs=vmem,
-        scratch_shapes=parts,
+        out_shape=(f32_array(rows, width), f32_array(tiles, *sums), pulls),
+        in_specs=[vmem] * 6,
+        out_specs=(vmem,) * 3,
+        input_output_aliases={5: 2},
+        scratch_shapes=half_parts + [pltpu.VMEM((REACH * TILE_B, 3 * TILE_B), f32)],
         compiler_params=params,
         cost_estimate=hidden,
         name="middle",
-    )(own, prod, pull)
-    quad, prod, gram, pull = pl.pallas_call(
+    )(own, prod, prod_got, part, edge, pull)
+    quad, gram, _ = pl.pallas_call(
         second_kernel,
-        out_shape=(f32_array(rows, width), f32_array(rows, width), f32_array(cols, 128), pulls),
-        in_specs=[vmem] * 5,
-        out_specs=(vmem,) * 4,
-        input_output_aliases={4: 3},
-        scratch_shapes=parts + [pltpu.VMEM((REACH * TILE_B, 3 * TILE_B), f32), pltpu.VMEM((tiles, *sums), f32)],
+        out_shape=(f32_array(rows, width), f32_array(cols, 128), f32_array(tiles, *sums)),
+        in_specs=[vmem] * 6,
+        out_specs=(vmem,) * 3,
+        input_output_aliases={5: 2},
+        scratch_shapes=half_parts,
         compiler_params=params,
         name="second",
-    )(own, prod, prod_got, part, pull)
+    )(own, mid, prod_got, outer_got, pull, part)
 
     def crossed(x, step):
         route = [
@@ -534,7 +628,7 @@
         scratch_shapes=[pltpu.VMEM(shape, f32) for shape in shapes] + [pltpu.SemaphoreType.DMA((6,))],
         compiler_params=params,
         name="last",
-    )(own, prod, quad, gram)
+    )(own, mid, quad, gram)
     return block.reshape(comps, cols, width), ray, corr, norms.reshape(cols)
 
 

time: 23.4 us -> 23 us (0.983)
  starting transfers between devices: 10.7 us -> 10.2 us
  Pallas kernels: 7.03 us -> 7.3 us
    pallas_call x2 -> x4, Pallas kernels: 1.03 us -> 1.76 us  [the longest x1 0.53 us: per_device(): pl.pallas_call(middle_kernel, out_shape=(f32_array(rows, width), f32_arra...]
    ppermute x4, starting transfers between devices: 6.52 us -> 5.98 us  [crossed(): return lax.ppermute(x, ('tile', 'col'), route)]
    pallas_call x1, Pallas kernels: 1.28 us -> 0.82 us  [per_device(): pl.pallas_call(second_kernel, out_shape=(f32_array(rows, width), f32_arra...]
    ppermute x1 -> x2, waiting for transfers between devices: 0.49 us -> 0.19 us  [swapped(): return lax.ppermute(x, 'col', [(c, c ^ 1) for c in range(n_col)])]
    ppermute x1 -> x2, starting transfers between devices: 1.04 us -> 1.11 us  [swapped(): return lax.ppermute(x, 'col', [(c, c ^ 1) for c in range(n_col)])]
  transfers between devices with their start and end apart: 7 -> 8, of which waited for: 5 -> 5; matrix products, arithmetic and copies ran while one was open for 0% -> 0% of each run, Pallas kernels for 11% -> 17%
where the time goes in v7:
time: 23 us; the launch traced here: 22.8 us
  starting transfers between devices  10.2 us (44%)
  Pallas kernels  7.3 us (32%)
  waiting for transfers between devices  4.58 us (20%)
  between operations  0.7 us (3%)
    ppermute x4, starting transfers between devices, crossed(): return lax.ppermute(x, ('tile', 'col'), route)  5.98 us
    ppermute x4, waiting for transfers between devices, crossed(): return lax.ppermute(x, ('tile', 'col'), route)  4.38 us
    ppermute x1, starting transfers between devices, per_device(): got_far = lax.ppermute(far, ('tile', 'col'), halo)  2.63 us
    pallas_call x1, Pallas kernels, per_device(): pl.pallas_call(functools.partial(last_kernel, bead_scale), out_shape=tupl...  1.65 us
    pallas_call x1, Pallas kernels, per_device(): pl.pallas_call(own_kernel, out_shape=(f32_array(rows + 8, width), pulls,...  1.3 us
    ppermute x2, starting transfers between devices, swapped(): return lax.ppermute(x, 'col', [(c, c ^ 1) for c in range(n_col)])  1.11 us
    pallas_call x1, Pallas kernels, per_device(): pl.pallas_call(pack_kernel, out_shape=(f32_array(rows + 16, width // 2),...  0.89 us
    pallas_call x1, Pallas kernels, per_device(): pl.pallas_call(outer_kernel, out_shape=(pulls, f32_array(8, width)), in_s...  0.88 us
  transfers between devices with their start and end apart: 8, of which 5 were waited for; matrix products, arithmetic and copies ran while one was open for 0% of the time, Pallas kernels for 17%

profile of v7, /device:TPU:0, one launch (start us, length us, event | category | flops | bytes accessed | tf_op | source)
XLA Modules:
  0.0 22.8 jit_solution(6711058839744965553)
XLA Ops:
  0.6 0.9 %pack.1 = (f32[64,256]{1,0:T(8,128)S(1)}, f32[48,256]{1,0:T(8,128)S(1)}) custom-call(f32[48,512]{1,0:T(8,128)} %bitcast.3, f32[3,512]{1,0:T(4,128)} %pos_ref.1, s32[2,1,4,8]{3,2,1,0:T(4,128)} %tiles_ref.1, s32[1,4]{1,0:T(1,128)} %count_ref.1), custom_call_target="tpu_custom_call" | custom-call | tf_op jit(solution)/shard_map/pack/pallas_call | solution.py:497
  1.5 0.5 %collective-permute-start = (f32[64,256]{1,0:T(8,128)S(1)}, f32[64,256]{1,0:T(8,128)S(1)}, u32[]{:S(2)}, u32[]{:S(2)}) collective-permute-start(f32[64,256]{1,0:T(8,128)S(1)} %get-tuple-element.27.sent_ref), channel_id=1, source_target_pairs={{5,0},{0,1},{7,2},{2,3},{1,4},{8,5},{3,6},{10,7},{13,8},{4,9},{15,... | collective-permute-start | bytes 196616 | tf_op jit(solution)/shard_map/ppermute | solution.py:519
  2.0 2.6 %collective-permute-start.2 = (f32[48,256]{1,0:T(8,128)S(1)}, f32[48,256]{1,0:T(8,128)S(1)}, u32[]{:S(2)}, u32[]{:S(2)}) collective-permute-start(f32[48,256]{1,0:T(8,128)S(1)} %get-tuple-element.37), channel_id=1, source_target_pairs={{5,0},{0,1},{7,2},{2,3},{1,4},{8,5},{3,6},{10,7},{13,8},{4,9},{15,... | collective-permute-start | bytes 147464 | tf_op jit(solution)/shard_map/ppermute | solution.py:520
  4.7 1.3 %own_pulls.1 = (f32[56,512]{1,0:T(8,128)S(1)}, bf16[8,640,384]{2,1,0:T(8,128)(2,1)S(1)}, f32[512,384]{1,0:T(8,128)S(1)}, bf16[48,512]{1,0:T(8,128)(2,1)S(1)}, bf...) custom-call(f32[48,512]{1,0:T(8,128)} %bitcast.4, f32[64,256]{1,0:T(8,128)S(1)} %get-tuple-element.27.sent_ref), custom_call_target="tpu_custom_call" | custom-call | flops 100000000 | bytes 1000000 | tf_op jit(solution)/shard_map/own_pulls/pallas_call | solution.py:526
  6.0 0.0 collective-permute-done.got_ref.near_ref
  6.0 0.9 %outer_pulls.1 = (bf16[8,640,384]{2,1,0:T(8,128)(2,1)S(1)}, f32[8,512]{1,0:T(8,128)S(1)}) custom-call(f32[56,512]{1,0:T(8,128)S(1)} %get-tuple-element.28.own_ref, f32[64,256]{1,0:T(8,128)S(1)} %collective-permute-done.got_ref.near_ref, f32[512,384]{1,0:T(8,128)S(1)} %get-tuple-element.29.wide_own, ...), custom_call_target="tpu_custom_call", output_to_operand_aliasing={{0}: (3, {})} | custom-call | flops 100000000 | bytes 1000000 | tf_op jit(solution)/shard_map/outer_pulls/pallas_call | solution.py:543
  6.9 0.5 %inner.1 = (f32[64,256]{1,0:T(8,128)S(1)}, f32[2,80,384]{2,1,0:T(8,128)S(1)}) custom-call(f32[56,512]{1,0:T(8,128)S(1)} %get-tuple-element.28.own_ref, f32[64,256]{1,0:T(8,128)S(1)} %collective-permute-done.got_ref.near_ref, f32[8,512]{1,0:T(8,128)S(1)} %get-tuple-element.31.places, bf16[48,512]{1,0:T(8,128)(2,1)S(1)} %get-tuple-element.32.high_own, ...), custom_call_target="tpu_custom_call" | custom-call | flops 100000000 | bytes 1000000 | tf_op jit(solution)/shard_map/inner/pallas_call | solution.py:555
  7.3 1.0 %collective-permute-start.1 = (f32[64,256]{1,0:T(8,128)S(1)}, f32[64,256]{1,0:T(8,128)S(1)}, u32[]{:S(2)}, u32[]{:S(2)}) collective-permute-start(f32[64,256]{1,0:T(8,128)S(1)} %get-tuple-element.36.prod_ref), channel_id=1, source_target_pairs={{0,1},{1,0},{2,3},{3,2},{4,5},{5,4},{6,7},{7,6},{8,9},{9,8},{10,11... | collective-permute-start | bytes 196616 | tf_op jit(solution)/shard_map/ppermute | solution.py:484
  8.4 0.3 %outer_rows.1.outer_ref = f32[48,256]{1,0:T(8,128)S(1)} custom-call(f32[56,512]{1,0:T(8,128)S(1)} %get-tuple-element.28.own_ref, f32[64,256]{1,0:T(8,128)S(1)} %collective-permute-done.got_ref.near_ref, f32[48,256]{1,0:T(8,128)S(1)} %collective-permute-done.2.far_ref, f32[8,512]{1,0:T(8,128)S(1)} %get-tuple-element.31.places, ...), custom_call_target="tpu_custom_call" | custom-call | tf_op jit(solution)/shard_map/outer_rows/pallas_call | solution.py:566
  8.7 0.1 collective-permute-start.3
  8.8 0.5 %own_sums.1 = (f32[4,80,384]{2,1,0:T(8,128)S(1)}, f32[2,80,384]{2,1,0:T(8,128)S(1)}) custom-call(f32[56,512]{1,0:T(8,128)S(1)} %get-tuple-element.28.own_ref, f32[64,256]{1,0:T(8,128)S(1)} %get-tuple-element.36.prod_ref, f32[48,256]{1,0:T(8,128)S(1)} %outer_rows.1.outer_ref, bf16[8,640,384]{2,1,0:T(8,128)(2,1)S(1)} %get-tuple-element.35.pull.pull_in), custom_call_target="tpu_custom_call" | custom-call | flops 100000000 | bytes 1000000 | tf_op jit(solution)/shard_map/own_sums/pallas_call | solution.py:576
  9.2 0.0 collective-permute-done.1.got_ref
  9.3 0.5 %middle.1 = (f32[48,512]{1,0:T(8,128)S(1)}, f32[4,80,384]{2,1,0:T(8,128)S(1)}, bf16[8,640,384]{2,1,0:T(8,128)(2,1)S(1)}) custom-call(f32[56,512]{1,0:T(8,128)S(1)} %get-tuple-element.28.own_ref, f32[64,256]{1,0:T(8,128)S(1)} %get-tuple-element.36.prod_ref, f32[64,256]{1,0:T(8,128)S(1)} %collective-permute-done.1.got_ref, ...), custom_call_target="tpu_custom_call", output_to_operand_aliasing={{2}: (5, {})} | custom-call | flops 100000000 | bytes 1000000 | tf_op jit(solution)/shard_map/middle/pallas_call | solution.py:586
  9.8 0.2 collective-permute-done.3.outer_ref
  10.0 0.8 %second.1 = (f32[48,512]{1,0:T(8,128)S(1)}, f32[16,128]{1,0:T(8,128)S(1)}, f32[4,80,384]{2,1,0:T(8,128)S(1)}) custom-call(f32[56,512]{1,0:T(8,128)S(1)} %get-tuple-element.28.own_ref, f32[48,512]{1,0:T(8,128)S(1)} %get-tuple-element.41.mid_ref.prod_ref, f32[64,256]{1,0:T(8,128)S(1)} %collective-permute-done.1.got_ref, ...), custom_call_target="tpu_custom_call", output_to_operand_aliasing={{2}: (5, {})} | custom-call | tf_op jit(solution)/shard_map/second/pallas_call | solution.py:597
  10.8 3.0 %collective-permute-start.6 = (f32[16,128]{1,0:T(8,128)S(1)}, f32[16,128]{1,0:T(8,128)S(1)}, u32[]{:S(2)}, u32[]{:S(2)}) collective-permute-start(f32[16,128]{1,0:T(8,128)S(1)} %get-tuple-element.45), channel_id=1, source_target_pairs={{0,13},{1,12},{2,15},{3,14},{4,9},{5,8},{6,11},{7,10},{8,5},{9,4},... | collective-permute-start | bytes 24584 | tf_op jit(solution)/shard_map/ppermute | solution.py:612
  13.8 0.3 %collective-permute-start.5 = (f32[16,128]{1,0:T(8,128)S(1)}, f32[16,128]{1,0:T(8,128)S(1)}, u32[]{:S(2)}, u32[]{:S(2)}) collective-permute-start(f32[16,128]{1,0:T(8,128)S(1)} %get-tuple-element.45), channel_id=1, source_target_pairs={{0,9},{1,8},{2,11},{3,10},{4,13},{5,12},{6,15},{7,14},{8,1},{9,0},... | collective-permute-start | bytes 24584 | tf_op jit(solution)/shard_map/ppermute | solution.py:612
  14.1 0.2 collective-permute-start.4
  14.3 0.9 %collective-permute-done.6 = f32[16,128]{1,0:T(8,128)S(1)} collective-permute-done((f32[16,128]{1,0:T(8,128)S(1)}, f32[16,128]{1,0:T(8,128)S(1)}, u32[]{:S(2)}, u32[]{:S(2)}) %collective-permute-start.6) | collective-permute-done | bytes 8224 | tf_op jit(solution)/shard_map/ppermute | solution.py:612
  15.2 1.7 %collective-permute-done.5 = f32[16,128]{1,0:T(8,128)S(1)} collective-permute-done((f32[16,128]{1,0:T(8,128)S(1)}, f32[16,128]{1,0:T(8,128)S(1)}, u32[]{:S(2)}, u32[]{:S(2)}) %collective-permute-start.5) | collective-permute-done | bytes 8224 | tf_op jit(solution)/shard_map/ppermute | solution.py:612
  16.9 0.3 %collective-permute-done.4 = f32[16,128]{1,0:T(8,128)S(1)} collective-permute-done((f32[16,128]{1,0:T(8,128)S(1)}, f32[16,128]{1,0:T(8,128)S(1)}, u32[]{:S(2)}, u32[]{:S(2)}) %collective-permute-start.4) | collective-permute-done | bytes 8224 | tf_op jit(solution)/shard_map/ppermute | solution.py:612
  17.2 2.5 %collective-permute-start.7 = (f32[16,128]{1,0:T(8,128)S(1)}, f32[16,128]{1,0:T(8,128)S(1)}, u32[]{:S(2)}, u32[]{:S(2)}) collective-permute-start(f32[16,128]{1,0:T(8,128)S(1)} %add_add_fusion), channel_id=1, source_target_pairs={{0,17},{1,16},{2,19},{3,18},{4,21},{5,20},{6,23},{7,22},{8,25},{9,... | collective-permute-start | bytes 24584 | tf_op jit(solution)/shard_map/ppermute | solution.py:612
  19.7 1.5 %collective-permute-done.7 = f32[16,128]{1,0:T(8,128)S(1)} collective-permute-done((f32[16,128]{1,0:T(8,128)S(1)}, f32[16,128]{1,0:T(8,128)S(1)}, u32[]{:S(2)}, u32[]{:S(2)}) %collective-permute-start.7) | collective-permute-done | bytes 8224 | tf_op jit(solution)/shard_map/ppermute | solution.py:612
  21.2 1.7 %last.1 = (f32[48,512]{1,0:T(8,128)}, f32[16,16]{1,0:T(8,128)}, f32[16,16]{1,0:T(8,128)}, f32[1,16]{1,0:T(1,128)}) custom-call(f32[56,512]{1,0:T(8,128)S(1)} %get-tuple-element.28.own_ref, f32[48,512]{1,0:T(8,128)S(1)} %get-tuple-element.41.mid_ref.prod_ref, f32[48,512]{1,0:T(8,128)S(1)} %get-tuple-element.44.quad_ref, f32[16,128]{1,0:T(8,128)S(1)} %add.15.gram_ref), custom_call_target="tpu_custom_call" | custom-call | tf_op jit(solution)/shard_map/last/pallas_call | solution.py:623
  (3 shorter events, 0.0 us)
Async XLA Ops:
  1.5 4.4 %collective-permute-start = (f32[64,256]{1,0:T(8,128)S(1)}, f32[64,256]{1,0:T(8,128)S(1)}, u32[]{:S(2)}, u32[]{:S(2)}) collective-permute-start(f32[64,256]{1,0:T(8,128)S(1)} %get-tuple-element.27.sent_ref), channel_id=1, source_target_pairs={{5,0},{0,1},{7,2},{2,3},{1,4},{8,5},{3,6},{10,7},{13,8},{4,9},{15,... | collective-permute-start | bytes 196616 | tf_op jit(solution)/shard_map/ppermute | solution.py:519
  2.0 6.3 %collective-permute-start.2 = (f32[48,256]{1,0:T(8,128)S(1)}, f32[48,256]{1,0:T(8,128)S(1)}, u32[]{:S(2)}, u32[]{:S(2)}) collective-permute-start(f32[48,256]{1,0:T(8,128)S(1)} %get-tuple-element.37), channel_id=1, source_target_pairs={{5,0},{0,1},{7,2},{2,3},{1,4},{8,5},{3,6},{10,7},{13,8},{4,9},{15,... | collective-permute-start | bytes 147464 | tf_op jit(solution)/shard_map/ppermute | solution.py:520
  7.3 1.9 %collective-permute-start.1 = (f32[64,256]{1,0:T(8,128)S(1)}, f32[64,256]{1,0:T(8,128)S(1)}, u32[]{:S(2)}, u32[]{:S(2)}) collective-permute-start(f32[64,256]{1,0:T(8,128)S(1)} %get-tuple-element.36.prod_ref), channel_id=1, source_target_pairs={{0,1},{1,0},{2,3},{3,2},{4,5},{5,4},{6,7},{7,6},{8,9},{9,8},{10,11... | collective-permute-start | bytes 196616 | tf_op jit(solution)/shard_map/ppermute | solution.py:484
  8.7 1.3 %collective-permute-start.3 = (f32[48,256]{1,0:T(8,128)S(1)}, f32[48,256]{1,0:T(8,128)S(1)}, u32[]{:S(2)}, u32[]{:S(2)}) collective-permute-start(f32[48,256]{1,0:T(8,128)S(1)} %outer_rows.1.outer_ref), channel_id=1, source_target_pairs={{0,1},{1,0},{2,3},{3,2},{4,5},{5,4},{6,7},{7,6},{8,9},{9,8},{10,11... | collective-permute-start | bytes 147464 | tf_op jit(solution)/shard_map/ppermute | solution.py:484
  10.8 4.4 %collective-permute-start.6 = (f32[16,128]{1,0:T(8,128)S(1)}, f32[16,128]{1,0:T(8,128)S(1)}, u32[]{:S(2)}, u32[]{:S(2)}) collective-permute-start(f32[16,128]{1,0:T(8,128)S(1)} %get-tuple-element.45), channel_id=1, source_target_pairs={{0,13},{1,12},{2,15},{3,14},{4,9},{5,8},{6,11},{7,10},{8,5},{9,4},... | collective-permute-start | bytes 24584 | tf_op jit(solution)/shard_map/ppermute | solution.py:612
  13.8 3.1 %collective-permute-start.5 = (f32[16,128]{1,0:T(8,128)S(1)}, f32[16,128]{1,0:T(8,128)S(1)}, u32[]{:S(2)}, u32[]{:S(2)}) collective-permute-start(f32[16,128]{1,0:T(8,128)S(1)} %get-tuple-element.45), channel_id=1, source_target_pairs={{0,9},{1,8},{2,11},{3,10},{4,13},{5,12},{6,15},{7,14},{8,1},{9,0},... | collective-permute-start | bytes 24584 | tf_op jit(solution)/shard_map/ppermute | solution.py:612
  14.1 3.1 %collective-permute-start.4 = (f32[16,128]{1,0:T(8,128)S(1)}, f32[16,128]{1,0:T(8,128)S(1)}, u32[]{:S(2)}, u32[]{:S(2)}) collective-permute-start(f32[16,128]{1,0:T(8,128)S(1)} %get-tuple-element.45), channel_id=1, source_target_pairs={{0,5},{1,4},{2,7},{3,6},{4,1},{5,0},{6,3},{7,2},{8,13},{9,12},{10,... | collective-permute-start | bytes 24584 | tf_op jit(solution)/shard_map/ppermute | solution.py:612
  17.2 4.0 %collective-permute-start.7 = (f32[16,128]{1,0:T(8,128)S(1)}, f32[16,128]{1,0:T(8,128)S(1)}, u32[]{:S(2)}, u32[]{:S(2)}) collective-permute-start(f32[16,128]{1,0:T(8,128)S(1)} %add_add_fusion), channel_id=1, source_target_pairs={{0,17},{1,16},{2,19},{3,18},{4,21},{5,20},{6,23},{7,22},{8,25},{9,... | collective-permute-start | bytes 24584 | tf_op jit(solution)/shard_map/ppermute | solution.py:612

commit v8 on v7

--- a/solution.py
+++ b/solution.py
@@ -303,7 +303,8 @@
 
     def body(odd):
         inner = dict(vec=prod_ref.at[0:rows], high=high, low=low)
-        inner_sums(own_pos, inner, odd, pull, part_ref)
+        for u, total in inner_sums(own_pos, inner, odd, pull):
+            part_ref[u] = total
         ours = dict(vec=outer_ref, high=high_outer, low=low_outer)
         window = beside_tiles(own_pos, places_of(prod_ref), ours, odd)
         for u, near in beside_rows(tiles, odd):
@@ -312,13 +313,13 @@
     by_parity(body)
 
 
-def inner_sums(own_pos, inner, side, pull, part_ref):
+def inner_sums(own_pos, inner, side, pull):
     tiles = own_pos.shape[1] // TILE_B
     half = tiles // 2
     window = Tiles(lambda u: (dict(inner, pos=own_pos, pos_tile=u), u % half))
     for u in range(tiles):
         near = [j for j in range(side * half, (1 + side) * half) if abs(j - u) <= REACH]
-        part_ref[u] = sum_pulls(window, u, near, pull.at[u + REACH])
+        yield u, sum_pulls(window, u, near, pull.at[u + REACH])
 
 
 def middle_kernel(own_ref, prod_ref, got_ref, ours_ref, edge_ref, pull_in, mid_ref, part_ref, pull, high, low, wide):
@@ -341,9 +342,8 @@
             for j in near:
                 fill_pull(window("pos", [w]), window.bound(w, j), wide, (j - first) * TILE_B, pull, w, j - w + REACH)
         inner = dict(vec=got_ref.at[0:rows], high=high, low=low)
-        inner_sums(own_pos, inner, side, pull, part_ref)
-        for u in range(tiles):
-            total = ours_ref[u] + part_ref[u]
+        for u, total in inner_sums(own_pos, inner, side, pull):
+            total = ours_ref[u] + total
             part_ref[u] = total + edge_ref[u % half] if u // half == odd else total
 
     by_parity(body)
@@ -371,9 +371,12 @@
     joint = jnp.concatenate(
         [jnp.concatenate([own_ref[band, :], mid_ref[band, :], out_ref[band, :]], axis=0) for band in bands], axis=1
     )
-    joint = jnp.concatenate(split(joint), axis=0)
-    gram = lax.dot_general(joint, joint, (((1,), (1,)), ((), ())), preferred_element_type=f32)
-    gram = gram[0:rows, 0:rows] + (gram[0:rows, rows:] + gram[rows:, 0:rows] + gram[rows:, rows:])
+    parts = split(joint)
+    both = jnp.concatenate(parts, axis=0)
+    by_high, by_low = [
+        lax.dot_general(both, part, (((1,), (1,)), ((), ())), preferred_element_type=f32) for part in parts
+    ]
+    gram = by_high[0:rows] + (by_high[rows:] + by_low[0:rows] + by_low[rows:])
     gram_ref[...] = jnp.zeros(gram_ref.shape, f32)
     gram_ref[:, 0:rows] = gram[0:cols]
     gram_ref[:, rows : 2 * rows] = gram[cols : 2 * cols]

time: 23 us -> 22.9 us (level)
  no operation moved by 1% of the time
where the time goes in v8:
time: 22.9 us; the launch traced here: 22.7 us
  starting transfers between devices  10.2 us (45%)
  Pallas kernels  7.23 us (32%)
  waiting for transfers between devices  4.58 us (20%)
  between operations  0.7 us (3%)
    ppermute x4, starting transfers between devices, crossed(): return lax.ppermute(x, ('tile', 'col'), route)  5.97 us
    ppermute x4, waiting for transfers between devices, crossed(): return lax.ppermute(x, ('tile', 'col'), route)  4.38 us
    ppermute x1, starting transfers between devices, per_device(): got_far = lax.ppermute(far, ('tile', 'col'), halo)  2.63 us
    pallas_call x1, Pallas kernels, per_device(): pl.pallas_call(functools.partial(last_kernel, bead_scale), out_shape=tupl...  1.65 us
    pallas_call x1, Pallas kernels, per_device(): pl.pallas_call(own_kernel, out_shape=(f32_array(rows + 8, width), pulls,...  1.3 us
    ppermute x2, starting transfers between devices, swapped(): return lax.ppermute(x, 'col', [(c, c ^ 1) for c in range(n_col)])  1.11 us
    pallas_call x1, Pallas kernels, per_device(): pl.pallas_call(pack_kernel, out_shape=(f32_array(rows + 16, width // 2),...  0.89 us
    pallas_call x1, Pallas kernels, per_device(): pl.pallas_call(outer_kernel, out_shape=(pulls, f32_array(8, width)), in_s...  0.88 us
  transfers between devices with their start and end apart: 8, of which 5 were waited for; matrix products, arithmetic and copies ran while one was open for 0% of the time, Pallas kernels for 17%

profile of v8, /device:TPU:0, one launch (start us, length us, event | category | flops | bytes accessed | tf_op | source)
XLA Modules:
  0.0 22.7 jit_solution(16907408497589250992)
XLA Ops:
  0.6 0.9 %pack.1 = (f32[64,256]{1,0:T(8,128)S(1)}, f32[48,256]{1,0:T(8,128)S(1)}) custom-call(f32[48,512]{1,0:T(8,128)} %bitcast.3, f32[3,512]{1,0:T(4,128)} %pos_ref.1, s32[2,1,4,8]{3,2,1,0:T(4,128)} %tiles_ref.1, s32[1,4]{1,0:T(1,128)} %count_ref.1), custom_call_target="tpu_custom_call" | custom-call | tf_op jit(solution)/shard_map/pack/pallas_call | solution.py:500
  1.5 0.5 %collective-permute-start = (f32[64,256]{1,0:T(8,128)S(1)}, f32[64,256]{1,0:T(8,128)S(1)}, u32[]{:S(2)}, u32[]{:S(2)}) collective-permute-start(f32[64,256]{1,0:T(8,128)S(1)} %get-tuple-element.27.sent_ref), channel_id=1, source_target_pairs={{5,0},{0,1},{7,2},{2,3},{1,4},{8,5},{3,6},{10,7},{13,8},{4,9},{15,... | collective-permute-start | bytes 196616 | tf_op jit(solution)/shard_map/ppermute | solution.py:522
  2.0 2.6 %collective-permute-start.2 = (f32[48,256]{1,0:T(8,128)S(1)}, f32[48,256]{1,0:T(8,128)S(1)}, u32[]{:S(2)}, u32[]{:S(2)}) collective-permute-start(f32[48,256]{1,0:T(8,128)S(1)} %get-tuple-element.37), channel_id=1, source_target_pairs={{5,0},{0,1},{7,2},{2,3},{1,4},{8,5},{3,6},{10,7},{13,8},{4,9},{15,... | collective-permute-start | bytes 147464 | tf_op jit(solution)/shard_map/ppermute | solution.py:523
  4.7 1.3 %own_pulls.1 = (f32[56,512]{1,0:T(8,128)S(1)}, bf16[8,640,384]{2,1,0:T(8,128)(2,1)S(1)}, f32[512,384]{1,0:T(8,128)S(1)}, bf16[48,512]{1,0:T(8,128)(2,1)S(1)}, bf...) custom-call(f32[48,512]{1,0:T(8,128)} %bitcast.4, f32[64,256]{1,0:T(8,128)S(1)} %get-tuple-element.27.sent_ref), custom_call_target="tpu_custom_call" | custom-call | flops 100000000 | bytes 1000000 | tf_op jit(solution)/shard_map/own_pulls/pallas_call | solution.py:529
  6.0 0.9 %outer_pulls.1 = (bf16[8,640,384]{2,1,0:T(8,128)(2,1)S(1)}, f32[8,512]{1,0:T(8,128)S(1)}) custom-call(f32[56,512]{1,0:T(8,128)S(1)} %get-tuple-element.28.own_ref, f32[64,256]{1,0:T(8,128)S(1)} %collective-permute-done.got_ref.near_ref, f32[512,384]{1,0:T(8,128)S(1)} %get-tuple-element.29.wide_own, ...), custom_call_target="tpu_custom_call", output_to_operand_aliasing={{0}: (3, {})} | custom-call | flops 100000000 | bytes 1000000 | tf_op jit(solution)/shard_map/outer_pulls/pallas_call | solution.py:546
  6.9 0.5 %inner.1 = (f32[64,256]{1,0:T(8,128)S(1)}, f32[2,80,384]{2,1,0:T(8,128)S(1)}) custom-call(f32[56,512]{1,0:T(8,128)S(1)} %get-tuple-element.28.own_ref, f32[64,256]{1,0:T(8,128)S(1)} %collective-permute-done.got_ref.near_ref, f32[8,512]{1,0:T(8,128)S(1)} %get-tuple-element.31.places, bf16[48,512]{1,0:T(8,128)(2,1)S(1)} %get-tuple-element.32.high_own, ...), custom_call_target="tpu_custom_call" | custom-call | flops 100000000 | bytes 1000000 | tf_op jit(solution)/shard_map/inner/pallas_call | solution.py:558
  7.3 1.0 %collective-permute-start.1 = (f32[64,256]{1,0:T(8,128)S(1)}, f32[64,256]{1,0:T(8,128)S(1)}, u32[]{:S(2)}, u32[]{:S(2)}) collective-permute-start(f32[64,256]{1,0:T(8,128)S(1)} %get-tuple-element.36.prod_ref), channel_id=1, source_target_pairs={{0,1},{1,0},{2,3},{3,2},{4,5},{5,4},{6,7},{7,6},{8,9},{9,8},{10,11... | collective-permute-start | bytes 196616 | tf_op jit(solution)/shard_map/ppermute | solution.py:487
  8.4 0.0 collective-permute-done.2.far_ref
  8.4 0.3 %outer_rows.1.outer_ref = f32[48,256]{1,0:T(8,128)S(1)} custom-call(f32[56,512]{1,0:T(8,128)S(1)} %get-tuple-element.28.own_ref, f32[64,256]{1,0:T(8,128)S(1)} %collective-permute-done.got_ref.near_ref, f32[48,256]{1,0:T(8,128)S(1)} %collective-permute-done.2.far_ref, f32[8,512]{1,0:T(8,128)S(1)} %get-tuple-element.31.places, ...), custom_call_target="tpu_custom_call" | custom-call | tf_op jit(solution)/shard_map/outer_rows/pallas_call | solution.py:569
  8.7 0.1 collective-permute-start.3
  8.8 0.5 %own_sums.1 = (f32[4,80,384]{2,1,0:T(8,128)S(1)}, f32[2,80,384]{2,1,0:T(8,128)S(1)}) custom-call(f32[56,512]{1,0:T(8,128)S(1)} %get-tuple-element.28.own_ref, f32[64,256]{1,0:T(8,128)S(1)} %get-tuple-element.36.prod_ref, f32[48,256]{1,0:T(8,128)S(1)} %outer_rows.1.outer_ref, bf16[8,640,384]{2,1,0:T(8,128)(2,1)S(1)} %get-tuple-element.35.pull.pull_in), custom_call_target="tpu_custom_call" | custom-call | flops 100000000 | bytes 1000000 | tf_op jit(solution)/shard_map/own_sums/pallas_call | solution.py:579
  9.2 0.0 collective-permute-done.1.got_ref
  9.3 0.5 %middle.1 = (f32[48,512]{1,0:T(8,128)S(1)}, f32[4,80,384]{2,1,0:T(8,128)S(1)}, bf16[8,640,384]{2,1,0:T(8,128)(2,1)S(1)}) custom-call(f32[56,512]{1,0:T(8,128)S(1)} %get-tuple-element.28.own_ref, f32[64,256]{1,0:T(8,128)S(1)} %get-tuple-element.36.prod_ref, f32[64,256]{1,0:T(8,128)S(1)} %collective-permute-done.1.got_ref, ...), custom_call_target="tpu_custom_call", output_to_operand_aliasing={{2}: (5, {})} | custom-call | flops 100000000 | bytes 1000000 | tf_op jit(solution)/shard_map/middle/pallas_call | solution.py:589
  9.8 0.2 collective-permute-done.3.outer_ref
  10.0 0.7 %second.1 = (f32[48,512]{1,0:T(8,128)S(1)}, f32[16,128]{1,0:T(8,128)S(1)}, f32[4,80,384]{2,1,0:T(8,128)S(1)}) custom-call(f32[56,512]{1,0:T(8,128)S(1)} %get-tuple-element.28.own_ref, f32[48,512]{1,0:T(8,128)S(1)} %get-tuple-element.41.mid_ref.prod_ref, f32[64,256]{1,0:T(8,128)S(1)} %collective-permute-done.1.got_ref, ...), custom_call_target="tpu_custom_call", output_to_operand_aliasing={{2}: (5, {})} | custom-call | tf_op jit(solution)/shard_map/second/pallas_call | solution.py:600
  10.7 3.0 %collective-permute-start.6 = (f32[16,128]{1,0:T(8,128)S(1)}, f32[16,128]{1,0:T(8,128)S(1)}, u32[]{:S(2)}, u32[]{:S(2)}) collective-permute-start(f32[16,128]{1,0:T(8,128)S(1)} %get-tuple-element.45), channel_id=1, source_target_pairs={{0,13},{1,12},{2,15},{3,14},{4,9},{5,8},{6,11},{7,10},{8,5},{9,4},... | collective-permute-start | bytes 24584 | tf_op jit(solution)/shard_map/ppermute | solution.py:615
  13.8 0.3 %collective-permute-start.5 = (f32[16,128]{1,0:T(8,128)S(1)}, f32[16,128]{1,0:T(8,128)S(1)}, u32[]{:S(2)}, u32[]{:S(2)}) collective-permute-start(f32[16,128]{1,0:T(8,128)S(1)} %get-tuple-element.45), channel_id=1, source_target_pairs={{0,9},{1,8},{2,11},{3,10},{4,13},{5,12},{6,15},{7,14},{8,1},{9,0},... | collective-permute-start | bytes 24584 | tf_op jit(solution)/shard_map/ppermute | solution.py:615
  14.0 0.2 collective-permute-start.4
  14.2 0.9 %collective-permute-done.6 = f32[16,128]{1,0:T(8,128)S(1)} collective-permute-done((f32[16,128]{1,0:T(8,128)S(1)}, f32[16,128]{1,0:T(8,128)S(1)}, u32[]{:S(2)}, u32[]{:S(2)}) %collective-permute-start.6) | collective-permute-done | bytes 8224 | tf_op jit(solution)/shard_map/ppermute | solution.py:615
  15.1 1.7 %collective-permute-done.5 = f32[16,128]{1,0:T(8,128)S(1)} collective-permute-done((f32[16,128]{1,0:T(8,128)S(1)}, f32[16,128]{1,0:T(8,128)S(1)}, u32[]{:S(2)}, u32[]{:S(2)}) %collective-permute-start.5) | collective-permute-done | bytes 8224 | tf_op jit(solution)/shard_map/ppermute | solution.py:615
  16.8 0.3 %collective-permute-done.4 = f32[16,128]{1,0:T(8,128)S(1)} collective-permute-done((f32[16,128]{1,0:T(8,128)S(1)}, f32[16,128]{1,0:T(8,128)S(1)}, u32[]{:S(2)}, u32[]{:S(2)}) %collective-permute-start.4) | collective-permute-done | bytes 8224 | tf_op jit(solution)/shard_map/ppermute | solution.py:615
  17.1 2.5 %collective-permute-start.7 = (f32[16,128]{1,0:T(8,128)S(1)}, f32[16,128]{1,0:T(8,128)S(1)}, u32[]{:S(2)}, u32[]{:S(2)}) collective-permute-start(f32[16,128]{1,0:T(8,128)S(1)} %add_add_fusion), channel_id=1, source_target_pairs={{0,17},{1,16},{2,19},{3,18},{4,21},{5,20},{6,23},{7,22},{8,25},{9,... | collective-permute-start | bytes 24584 | tf_op jit(solution)/shard_map/ppermute | solution.py:615
  19.6 1.5 %collective-permute-done.7 = f32[16,128]{1,0:T(8,128)S(1)} collective-permute-done((f32[16,128]{1,0:T(8,128)S(1)}, f32[16,128]{1,0:T(8,128)S(1)}, u32[]{:S(2)}, u32[]{:S(2)}) %collective-permute-start.7) | collective-permute-done | bytes 8224 | tf_op jit(solution)/shard_map/ppermute | solution.py:615
  21.1 1.7 %last.1 = (f32[48,512]{1,0:T(8,128)}, f32[16,16]{1,0:T(8,128)}, f32[16,16]{1,0:T(8,128)}, f32[1,16]{1,0:T(1,128)}) custom-call(f32[56,512]{1,0:T(8,128)S(1)} %get-tuple-element.28.own_ref, f32[48,512]{1,0:T(8,128)S(1)} %get-tuple-element.41.mid_ref.prod_ref, f32[48,512]{1,0:T(8,128)S(1)} %get-tuple-element.44.quad_ref, f32[16,128]{1,0:T(8,128)S(1)} %add.15.gram_ref), custom_call_target="tpu_custom_call" | custom-call | tf_op jit(solution)/shard_map/last/pallas_call | solution.py:626
  (3 shorter events, 0.0 us)
Async XLA Ops:
  1.5 4.4 %collective-permute-start = (f32[64,256]{1,0:T(8,128)S(1)}, f32[64,256]{1,0:T(8,128)S(1)}, u32[]{:S(2)}, u32[]{:S(2)}) collective-permute-start(f32[64,256]{1,0:T(8,128)S(1)} %get-tuple-element.27.sent_ref), channel_id=1, source_target_pairs={{5,0},{0,1},{7,2},{2,3},{1,4},{8,5},{3,6},{10,7},{13,8},{4,9},{15,... | collective-permute-start | bytes 196616 | tf_op jit(solution)/shard_map/ppermute | solution.py:522
  2.0 6.3 %collective-permute-start.2 = (f32[48,256]{1,0:T(8,128)S(1)}, f32[48,256]{1,0:T(8,128)S(1)}, u32[]{:S(2)}, u32[]{:S(2)}) collective-permute-start(f32[48,256]{1,0:T(8,128)S(1)} %get-tuple-element.37), channel_id=1, source_target_pairs={{5,0},{0,1},{7,2},{2,3},{1,4},{8,5},{3,6},{10,7},{13,8},{4,9},{15,... | collective-permute-start | bytes 147464 | tf_op jit(solution)/shard_map/ppermute | solution.py:523
  7.3 1.9 %collective-permute-start.1 = (f32[64,256]{1,0:T(8,128)S(1)}, f32[64,256]{1,0:T(8,128)S(1)}, u32[]{:S(2)}, u32[]{:S(2)}) collective-permute-start(f32[64,256]{1,0:T(8,128)S(1)} %get-tuple-element.36.prod_ref), channel_id=1, source_target_pairs={{0,1},{1,0},{2,3},{3,2},{4,5},{5,4},{6,7},{7,6},{8,9},{9,8},{10,11... | collective-permute-start | bytes 196616 | tf_op jit(solution)/shard_map/ppermute | solution.py:487
  8.7 1.3 %collective-permute-start.3 = (f32[48,256]{1,0:T(8,128)S(1)}, f32[48,256]{1,0:T(8,128)S(1)}, u32[]{:S(2)}, u32[]{:S(2)}) collective-permute-start(f32[48,256]{1,0:T(8,128)S(1)} %outer_rows.1.outer_ref), channel_id=1, source_target_pairs={{0,1},{1,0},{2,3},{3,2},{4,5},{5,4},{6,7},{7,6},{8,9},{9,8},{10,11... | collective-permute-start | bytes 147464 | tf_op jit(solution)/shard_map/ppermute | solution.py:487
  10.7 4.4 %collective-permute-start.6 = (f32[16,128]{1,0:T(8,128)S(1)}, f32[16,128]{1,0:T(8,128)S(1)}, u32[]{:S(2)}, u32[]{:S(2)}) collective-permute-start(f32[16,128]{1,0:T(8,128)S(1)} %get-tuple-element.45), channel_id=1, source_target_pairs={{0,13},{1,12},{2,15},{3,14},{4,9},{5,8},{6,11},{7,10},{8,5},{9,4},... | collective-permute-start | bytes 24584 | tf_op jit(solution)/shard_map/ppermute | solution.py:615
  13.8 3.1 %collective-permute-start.5 = (f32[16,128]{1,0:T(8,128)S(1)}, f32[16,128]{1,0:T(8,128)S(1)}, u32[]{:S(2)}, u32[]{:S(2)}) collective-permute-start(f32[16,128]{1,0:T(8,128)S(1)} %get-tuple-element.45), channel_id=1, source_target_pairs={{0,9},{1,8},{2,11},{3,10},{4,13},{5,12},{6,15},{7,14},{8,1},{9,0},... | collective-permute-start | bytes 24584 | tf_op jit(solution)/shard_map/ppermute | solution.py:615
  14.0 3.1 %collective-permute-start.4 = (f32[16,128]{1,0:T(8,128)S(1)}, f32[16,128]{1,0:T(8,128)S(1)}, u32[]{:S(2)}, u32[]{:S(2)}) collective-permute-start(f32[16,128]{1,0:T(8,128)S(1)} %get-tuple-element.45), channel_id=1, source_target_pairs={{0,5},{1,4},{2,7},{3,6},{4,1},{5,0},{6,3},{7,2},{8,13},{9,12},{10,... | collective-permute-start | bytes 24584 | tf_op jit(solution)/shard_map/ppermute | solution.py:615
  17.1 4.0 %collective-permute-start.7 = (f32[16,128]{1,0:T(8,128)S(1)}, f32[16,128]{1,0:T(8,128)S(1)}, u32[]{:S(2)}, u32[]{:S(2)}) collective-permute-start(f32[16,128]{1,0:T(8,128)S(1)} %add_add_fusion), channel_id=1, source_target_pairs={{0,17},{1,16},{2,19},{3,18},{4,21},{5,20},{6,23},{7,22},{8,25},{9,... | collective-permute-start | bytes 24584 | tf_op jit(solution)/shard_map/ppermute | solution.py:615

commit v9 on v8

--- a/solution.py
+++ b/solution.py
@@ -9,7 +9,7 @@
 
 TILE_B = 128
 REACH = 2
-CHUNK = 32
+CHUNK = 16
 
 spring_scale = 1.0 / 64.0
 cutoff_sq = 225.0

time: 22.9 us -> 23 us (level)
  no operation moved by 1% of the time
where the time goes in v9:
time: 23 us; the launch traced here: 22.8 us
  starting transfers between devices  10.2 us (44%)
  Pallas kernels  7.23 us (31%)
  waiting for transfers between devices  4.62 us (20%)
  between operations  0.7 us (3%)
    ppermute x4, starting transfers between devices, crossed(): return lax.ppermute(x, ('tile', 'col'), route)  5.96 us
    ppermute x4, waiting for transfers between devices, crossed(): return lax.ppermute(x, ('tile', 'col'), route)  4.41 us
    ppermute x1, starting transfers between devices, per_device(): got_far = lax.ppermute(far, ('tile', 'col'), halo)  2.63 us
    pallas_call x1, Pallas kernels, per_device(): pl.pallas_call(functools.partial(last_kernel, bead_scale), out_shape=tupl...  1.65 us
    pallas_call x1, Pallas kernels, per_device(): pl.pallas_call(own_kernel, out_shape=(f32_array(rows + 8, width), pulls,...  1.3 us
    ppermute x2, starting transfers between devices, swapped(): return lax.ppermute(x, 'col', [(c, c ^ 1) for c in range(n_col)])  1.1 us
    pallas_call x1, Pallas kernels, per_device(): pl.pallas_call(pack_kernel, out_shape=(f32_array(rows + 16, width // 2),...  0.89 us
    pallas_call x1, Pallas kernels, per_device(): pl.pallas_call(outer_kernel, out_shape=(pulls, f32_array(8, width)), in_s...  0.88 us
  transfers between devices with their start and end apart: 8, of which 5 were waited for; matrix products, arithmetic and copies ran while one was open for 0% of the time, Pallas kernels for 17%

profile of v9, /device:TPU:0, one launch (start us, length us, event | category | flops | bytes accessed | tf_op | source)
XLA Modules:
  0.0 22.8 jit_solution(2589385175513598207)
XLA Ops:
  0.6 0.9 %pack.1 = (f32[64,256]{1,0:T(8,128)S(1)}, f32[48,256]{1,0:T(8,128)S(1)}) custom-call(f32[48,512]{1,0:T(8,128)} %bitcast.3, f32[3,512]{1,0:T(4,128)} %pos_ref.1, s32[2,1,4,8]{3,2,1,0:T(4,128)} %tiles_ref.1, s32[1,4]{1,0:T(1,128)} %count_ref.1), custom_call_target="tpu_custom_call" | custom-call | tf_op jit(solution)/shard_map/pack/pallas_call | solution.py:500
  1.5 0.5 %collective-permute-start = (f32[64,256]{1,0:T(8,128)S(1)}, f32[64,256]{1,0:T(8,128)S(1)}, u32[]{:S(2)}, u32[]{:S(2)}) collective-permute-start(f32[64,256]{1,0:T(8,128)S(1)} %get-tuple-element.27.sent_ref), channel_id=1, source_target_pairs={{5,0},{0,1},{7,2},{2,3},{1,4},{8,5},{3,6},{10,7},{13,8},{4,9},{15,... | collective-permute-start | bytes 196616 | tf_op jit(solution)/shard_map/ppermute | solution.py:522
  2.0 2.6 %collective-permute-start.2 = (f32[48,256]{1,0:T(8,128)S(1)}, f32[48,256]{1,0:T(8,128)S(1)}, u32[]{:S(2)}, u32[]{:S(2)}) collective-permute-start(f32[48,256]{1,0:T(8,128)S(1)} %get-tuple-element.37), channel_id=1, source_target_pairs={{5,0},{0,1},{7,2},{2,3},{1,4},{8,5},{3,6},{10,7},{13,8},{4,9},{15,... | collective-permute-start | bytes 147464 | tf_op jit(solution)/shard_map/ppermute | solution.py:523
  4.7 1.3 %own_pulls.1 = (f32[56,512]{1,0:T(8,128)S(1)}, bf16[8,640,384]{2,1,0:T(8,128)(2,1)S(1)}, f32[512,384]{1,0:T(8,128)S(1)}, bf16[48,512]{1,0:T(8,128)(2,1)S(1)}, bf...) custom-call(f32[48,512]{1,0:T(8,128)} %bitcast.4, f32[64,256]{1,0:T(8,128)S(1)} %get-tuple-element.27.sent_ref), custom_call_target="tpu_custom_call" | custom-call | flops 100000000 | bytes 1000000 | tf_op jit(solution)/shard_map/own_pulls/pallas_call | solution.py:529
  6.0 0.9 %outer_pulls.1 = (bf16[8,640,384]{2,1,0:T(8,128)(2,1)S(1)}, f32[8,512]{1,0:T(8,128)S(1)}) custom-call(f32[56,512]{1,0:T(8,128)S(1)} %get-tuple-element.28.own_ref, f32[64,256]{1,0:T(8,128)S(1)} %collective-permute-done.got_ref.near_ref, f32[512,384]{1,0:T(8,128)S(1)} %get-tuple-element.29.wide_own, ...), custom_call_target="tpu_custom_call", output_to_operand_aliasing={{0}: (3, {})} | custom-call | flops 100000000 | bytes 1000000 | tf_op jit(solution)/shard_map/outer_pulls/pallas_call | solution.py:546
  6.9 0.5 %inner.1 = (f32[64,256]{1,0:T(8,128)S(1)}, f32[2,80,384]{2,1,0:T(8,128)S(1)}) custom-call(f32[56,512]{1,0:T(8,128)S(1)} %get-tuple-element.28.own_ref, f32[64,256]{1,0:T(8,128)S(1)} %collective-permute-done.got_ref.near_ref, f32[8,512]{1,0:T(8,128)S(1)} %get-tuple-element.31.places, bf16[48,512]{1,0:T(8,128)(2,1)S(1)} %get-tuple-element.32.high_own, ...), custom_call_target="tpu_custom_call" | custom-call | flops 100000000 | bytes 1000000 | tf_op jit(solution)/shard_map/inner/pallas_call | solution.py:558
  7.4 1.0 %collective-permute-start.1 = (f32[64,256]{1,0:T(8,128)S(1)}, f32[64,256]{1,0:T(8,128)S(1)}, u32[]{:S(2)}, u32[]{:S(2)}) collective-permute-start(f32[64,256]{1,0:T(8,128)S(1)} %get-tuple-element.36.prod_ref), channel_id=1, source_target_pairs={{0,1},{1,0},{2,3},{3,2},{4,5},{5,4},{6,7},{7,6},{8,9},{9,8},{10,11... | collective-permute-start | bytes 196616 | tf_op jit(solution)/shard_map/ppermute | solution.py:487
  8.4 0.0 collective-permute-done.2.far_ref
  8.4 0.3 %outer_rows.1.outer_ref = f32[48,256]{1,0:T(8,128)S(1)} custom-call(f32[56,512]{1,0:T(8,128)S(1)} %get-tuple-element.28.own_ref, f32[64,256]{1,0:T(8,128)S(1)} %collective-permute-done.got_ref.near_ref, f32[48,256]{1,0:T(8,128)S(1)} %collective-permute-done.2.far_ref, f32[8,512]{1,0:T(8,128)S(1)} %get-tuple-element.31.places, ...), custom_call_target="tpu_custom_call" | custom-call | tf_op jit(solution)/shard_map/outer_rows/pallas_call | solution.py:569
  8.7 0.1 collective-permute-start.3
  8.8 0.5 %own_sums.1 = (f32[4,80,384]{2,1,0:T(8,128)S(1)}, f32[2,80,384]{2,1,0:T(8,128)S(1)}) custom-call(f32[56,512]{1,0:T(8,128)S(1)} %get-tuple-element.28.own_ref, f32[64,256]{1,0:T(8,128)S(1)} %get-tuple-element.36.prod_ref, f32[48,256]{1,0:T(8,128)S(1)} %outer_rows.1.outer_ref, bf16[8,640,384]{2,1,0:T(8,128)(2,1)S(1)} %get-tuple-element.35.pull.pull_in), custom_call_target="tpu_custom_call" | custom-call | flops 100000000 | bytes 1000000 | tf_op jit(solution)/shard_map/own_sums/pallas_call | solution.py:579
  9.2 0.0 collective-permute-done.1.got_ref
  9.3 0.5 %middle.1 = (f32[48,512]{1,0:T(8,128)S(1)}, f32[4,80,384]{2,1,0:T(8,128)S(1)}, bf16[8,640,384]{2,1,0:T(8,128)(2,1)S(1)}) custom-call(f32[56,512]{1,0:T(8,128)S(1)} %get-tuple-element.28.own_ref, f32[64,256]{1,0:T(8,128)S(1)} %get-tuple-element.36.prod_ref, f32[64,256]{1,0:T(8,128)S(1)} %collective-permute-done.1.got_ref, ...), custom_call_target="tpu_custom_call", output_to_operand_aliasing={{2}: (5, {})} | custom-call | flops 100000000 | bytes 1000000 | tf_op jit(solution)/shard_map/middle/pallas_call | solution.py:589
  9.8 0.2 collective-permute-done.3.outer_ref
  10.0 0.7 %second.1 = (f32[48,512]{1,0:T(8,128)S(1)}, f32[16,128]{1,0:T(8,128)S(1)}, f32[4,80,384]{2,1,0:T(8,128)S(1)}) custom-call(f32[56,512]{1,0:T(8,128)S(1)} %get-tuple-element.28.own_ref, f32[48,512]{1,0:T(8,128)S(1)} %get-tuple-element.41.mid_ref.prod_ref, f32[64,256]{1,0:T(8,128)S(1)} %collective-permute-done.1.got_ref, ...), custom_call_target="tpu_custom_call", output_to_operand_aliasing={{2}: (5, {})} | custom-call | tf_op jit(solution)/shard_map/second/pallas_call | solution.py:600
  10.7 3.0 %collective-permute-start.6 = (f32[16,128]{1,0:T(8,128)S(1)}, f32[16,128]{1,0:T(8,128)S(1)}, u32[]{:S(2)}, u32[]{:S(2)}) collective-permute-start(f32[16,128]{1,0:T(8,128)S(1)} %get-tuple-element.45), channel_id=1, source_target_pairs={{0,13},{1,12},{2,15},{3,14},{4,9},{5,8},{6,11},{7,10},{8,5},{9,4},... | collective-permute-start | bytes 24584 | tf_op jit(solution)/shard_map/ppermute | solution.py:615
  13.8 0.3 %collective-permute-start.5 = (f32[16,128]{1,0:T(8,128)S(1)}, f32[16,128]{1,0:T(8,128)S(1)}, u32[]{:S(2)}, u32[]{:S(2)}) collective-permute-start(f32[16,128]{1,0:T(8,128)S(1)} %get-tuple-element.45), channel_id=1, source_target_pairs={{0,9},{1,8},{2,11},{3,10},{4,13},{5,12},{6,15},{7,14},{8,1},{9,0},... | collective-permute-start | bytes 24584 | tf_op jit(solution)/shard_map/ppermute | solution.py:615
  14.0 0.2 collective-permute-start.4
  14.2 0.9 %collective-permute-done.6 = f32[16,128]{1,0:T(8,128)S(1)} collective-permute-done((f32[16,128]{1,0:T(8,128)S(1)}, f32[16,128]{1,0:T(8,128)S(1)}, u32[]{:S(2)}, u32[]{:S(2)}) %collective-permute-start.6) | collective-permute-done | bytes 8224 | tf_op jit(solution)/shard_map/ppermute | solution.py:615
  15.1 1.7 %collective-permute-done.5 = f32[16,128]{1,0:T(8,128)S(1)} collective-permute-done((f32[16,128]{1,0:T(8,128)S(1)}, f32[16,128]{1,0:T(8,128)S(1)}, u32[]{:S(2)}, u32[]{:S(2)}) %collective-permute-start.5) | collective-permute-done | bytes 8224 | tf_op jit(solution)/shard_map/ppermute | solution.py:615
  16.8 0.3 %collective-permute-done.4 = f32[16,128]{1,0:T(8,128)S(1)} collective-permute-done((f32[16,128]{1,0:T(8,128)S(1)}, f32[16,128]{1,0:T(8,128)S(1)}, u32[]{:S(2)}, u32[]{:S(2)}) %collective-permute-start.4) | collective-permute-done | bytes 8224 | tf_op jit(solution)/shard_map/ppermute | solution.py:615
  17.1 2.5 %collective-permute-start.7 = (f32[16,128]{1,0:T(8,128)S(1)}, f32[16,128]{1,0:T(8,128)S(1)}, u32[]{:S(2)}, u32[]{:S(2)}) collective-permute-start(f32[16,128]{1,0:T(8,128)S(1)} %add_add_fusion), channel_id=1, source_target_pairs={{0,17},{1,16},{2,19},{3,18},{4,21},{5,20},{6,23},{7,22},{8,25},{9,... | collective-permute-start | bytes 24584 | tf_op jit(solution)/shard_map/ppermute | solution.py:615
  19.6 1.5 %collective-permute-done.7 = f32[16,128]{1,0:T(8,128)S(1)} collective-permute-done((f32[16,128]{1,0:T(8,128)S(1)}, f32[16,128]{1,0:T(8,128)S(1)}, u32[]{:S(2)}, u32[]{:S(2)}) %collective-permute-start.7) | collective-permute-done | bytes 8224 | tf_op jit(solution)/shard_map/ppermute | solution.py:615
  21.1 1.7 %last.1 = (f32[48,512]{1,0:T(8,128)}, f32[16,16]{1,0:T(8,128)}, f32[16,16]{1,0:T(8,128)}, f32[1,16]{1,0:T(1,128)}) custom-call(f32[56,512]{1,0:T(8,128)S(1)} %get-tuple-element.28.own_ref, f32[48,512]{1,0:T(8,128)S(1)} %get-tuple-element.41.mid_ref.prod_ref, f32[48,512]{1,0:T(8,128)S(1)} %get-tuple-element.44.quad_ref, f32[16,128]{1,0:T(8,128)S(1)} %add.15.gram_ref), custom_call_target="tpu_custom_call" | custom-call | tf_op jit(solution)/shard_map/last/pallas_call | solution.py:626
  (3 shorter events, 0.0 us)
Async XLA Ops:
  1.5 4.4 %collective-permute-start = (f32[64,256]{1,0:T(8,128)S(1)}, f32[64,256]{1,0:T(8,128)S(1)}, u32[]{:S(2)}, u32[]{:S(2)}) collective-permute-start(f32[64,256]{1,0:T(8,128)S(1)} %get-tuple-element.27.sent_ref), channel_id=1, source_target_pairs={{5,0},{0,1},{7,2},{2,3},{1,4},{8,5},{3,6},{10,7},{13,8},{4,9},{15,... | collective-permute-start | bytes 196616 | tf_op jit(solution)/shard_map/ppermute | solution.py:522
  2.0 6.3 %collective-permute-start.2 = (f32[48,256]{1,0:T(8,128)S(1)}, f32[48,256]{1,0:T(8,128)S(1)}, u32[]{:S(2)}, u32[]{:S(2)}) collective-permute-start(f32[48,256]{1,0:T(8,128)S(1)} %get-tuple-element.37), channel_id=1, source_target_pairs={{5,0},{0,1},{7,2},{2,3},{1,4},{8,5},{3,6},{10,7},{13,8},{4,9},{15,... | collective-permute-start | bytes 147464 | tf_op jit(solution)/shard_map/ppermute | solution.py:523
  7.4 1.9 %collective-permute-start.1 = (f32[64,256]{1,0:T(8,128)S(1)}, f32[64,256]{1,0:T(8,128)S(1)}, u32[]{:S(2)}, u32[]{:S(2)}) collective-permute-start(f32[64,256]{1,0:T(8,128)S(1)} %get-tuple-element.36.prod_ref), channel_id=1, source_target_pairs={{0,1},{1,0},{2,3},{3,2},{4,5},{5,4},{6,7},{7,6},{8,9},{9,8},{10,11... | collective-permute-start | bytes 196616 | tf_op jit(solution)/shard_map/ppermute | solution.py:487
  8.7 1.3 %collective-permute-start.3 = (f32[48,256]{1,0:T(8,128)S(1)}, f32[48,256]{1,0:T(8,128)S(1)}, u32[]{:S(2)}, u32[]{:S(2)}) collective-permute-start(f32[48,256]{1,0:T(8,128)S(1)} %outer_rows.1.outer_ref), channel_id=1, source_target_pairs={{0,1},{1,0},{2,3},{3,2},{4,5},{5,4},{6,7},{7,6},{8,9},{9,8},{10,11... | collective-permute-start | bytes 147464 | tf_op jit(solution)/shard_map/ppermute | solution.py:487
  10.7 4.4 %collective-permute-start.6 = (f32[16,128]{1,0:T(8,128)S(1)}, f32[16,128]{1,0:T(8,128)S(1)}, u32[]{:S(2)}, u32[]{:S(2)}) collective-permute-start(f32[16,128]{1,0:T(8,128)S(1)} %get-tuple-element.45), channel_id=1, source_target_pairs={{0,13},{1,12},{2,15},{3,14},{4,9},{5,8},{6,11},{7,10},{8,5},{9,4},... | collective-permute-start | bytes 24584 | tf_op jit(solution)/shard_map/ppermute | solution.py:615
  13.8 3.1 %collective-permute-start.5 = (f32[16,128]{1,0:T(8,128)S(1)}, f32[16,128]{1,0:T(8,128)S(1)}, u32[]{:S(2)}, u32[]{:S(2)}) collective-permute-start(f32[16,128]{1,0:T(8,128)S(1)} %get-tuple-element.45), channel_id=1, source_target_pairs={{0,9},{1,8},{2,11},{3,10},{4,13},{5,12},{6,15},{7,14},{8,1},{9,0},... | collective-permute-start | bytes 24584 | tf_op jit(solution)/shard_map/ppermute | solution.py:615
  14.0 3.1 %collective-permute-start.4 = (f32[16,128]{1,0:T(8,128)S(1)}, f32[16,128]{1,0:T(8,128)S(1)}, u32[]{:S(2)}, u32[]{:S(2)}) collective-permute-start(f32[16,128]{1,0:T(8,128)S(1)} %get-tuple-element.45), channel_id=1, source_target_pairs={{0,5},{1,4},{2,7},{3,6},{4,1},{5,0},{6,3},{7,2},{8,13},{9,12},{10,... | collective-permute-start | bytes 24584 | tf_op jit(solution)/shard_map/ppermute | solution.py:615
  17.1 4.0 %collective-permute-start.7 = (f32[16,128]{1,0:T(8,128)S(1)}, f32[16,128]{1,0:T(8,128)S(1)}, u32[]{:S(2)}, u32[]{:S(2)}) collective-permute-start(f32[16,128]{1,0:T(8,128)S(1)} %add_add_fusion), channel_id=1, source_target_pairs={{0,17},{1,16},{2,19},{3,18},{4,21},{5,20},{6,23},{7,22},{8,25},{9,... | collective-permute-start | bytes 24584 | tf_op jit(solution)/shard_map/ppermute | solution.py:615
